TPU v7x, 512 devices: a whole 4x4x16 slice. The times are simulated.
512 devices in a mesh: dp: 2 (over core), ctx: 32 (over x_hi, z), ch: 8 (over x_lo, y).
Axes of the slice: x: 4 (x_hi: 2, x_lo: 2; x = x_hi * 2 + x_lo), y: 4, z: 16, core: 2. Of those that a mesh axis runs over, the one named last changes fastest.
Arguments:
- query_proj: bfloat16 [8192, 8192], P(('dp', 'ctx'), 'ch'), may hold values from -6 to 6
- key_proj: bfloat16 [8192, 8192], P(('dp', 'ctx'), 'ch'), may hold values from -6 to 6
- value_proj: bfloat16 [8192, 8192], P(('dp', 'ctx'), 'ch'), may hold values from -6 to 6
- cotangent: bfloat16 [8192, 8192], P(('dp', 'ctx'), 'ch'), may hold values from -6 to 6
- filter_taps: bfloat16 [256, 8192], P(None, ('ch', 'ctx')), may hold values from -0.375 to 0.375
- span_slot: int32 [2, 32], P('dp'), may hold values from 0 to 31, each once within a row
- doc_lengths: int32 [2, 24], P('dp'), may hold values from 1 to 2, 32 in all within a row
Outputs:
- grad_query: bfloat16 [8192, 8192], P(('dp', 'ctx'), 'ch')
- grad_key: bfloat16 [8192, 8192], P(('dp', 'ctx'), 'ch')
- grad_value: bfloat16 [8192, 8192], P(('dp', 'ctx'), 'ch')
- grad_filter: bfloat16 [256, 8192], P(None, ('ch', 'ctx'))
Inputs may be any that keep to these rules, and one draw needn't show every extreme that they name: Each row span_slot[w] is a permutation of the spans of window w. Each row doc_lengths[w] sums to 32 and holds 2 at least once.
All inputs are finite; a program needn't handle non-finite values.
Results may differ from a plain program's by a relative error of at most 0.012.
Values may be sent and summed in bfloat16 or wider, within the bound.
No kernel may reach another device: no remote copies, remote signals or barrier semaphores. Data moves between devices by JAX's collectives and lax.ppermute only.
A program may use at most 64 MiB of HBM per device.

v0:
```python
import jax
import jax.numpy as jnp
import numpy as np
from jax import lax
from jax.sharding import PartitionSpec as P

SPAN = 128


def doc_starts(lengths_row, spans):
    starts = jnp.cumsum(lengths_row) - lengths_row
    span_ids = jnp.arange(spans, dtype=jnp.int32)
    inside = starts[None, :] <= span_ids[:, None]
    return jnp.max(jnp.where(inside, starts[None, :], 0), axis=1)


def build_blocks(taps_t, block_len, blocks):
    length = taps_t.shape[1]
    extended = jnp.pad(taps_t, ((0, 0), (block_len, (blocks + 1) * block_len - length)))
    offsets = np.arange(block_len)[:, None] - np.arange(block_len)[None, :] + block_len
    result = []
    for lag_block in range(blocks):
        table = jnp.asarray(offsets + lag_block * block_len, dtype=jnp.int32)
        result.append(jnp.take(extended, table, axis=1))
    return result


def diagonal_sums(flipped):
    channels, block_len, _ = flipped.shape
    padded = jnp.pad(flipped, ((0, 0), (0, 0), (0, block_len))).reshape(
        channels, 2 * block_len * block_len
    )
    skewed = padded[:, : block_len * (2 * block_len - 1)].reshape(
        channels, block_len, 2 * block_len - 1
    )
    return jnp.sum(skewed, axis=1)


def shift_later(array, lag_block):
    if lag_block == 0:
        return array
    count = array.shape[1]
    return jnp.pad(array[:, : count - lag_block], ((0, 0), (lag_block, 0), (0, 0)))


def shift_earlier(array, lag_block):
    if lag_block == 0:
        return array
    return jnp.pad(array[:, lag_block:], ((0, 0), (0, lag_block), (0, 0)))


def conv_forward(series, toeplitz, masks):
    summed = jnp.zeros(series.shape, jnp.float32)
    for lag_block in range(len(toeplitz)):
        source = shift_later(series, lag_block) * masks[lag_block][None, :, None]
        summed = summed + jnp.einsum(
            "cts,cjs->cjt", toeplitz[lag_block], source, preferred_element_type=jnp.float32
        )
    return summed


def conv_backward(series, grad_out, toeplitz, masks, length):
    channels, count, block_len = series.shape
    blocks = len(toeplitz)
    total_len = (blocks + 2) * block_len
    reversed_series = series[:, :, ::-1]
    grad_in = jnp.zeros(series.shape, jnp.float32)
    grad_ext = jnp.zeros((channels, total_len), jnp.float32)
    for lag_block in range(blocks):
        masked = grad_out * masks[lag_block][None, :, None]
        grad_in = grad_in + jnp.einsum(
            "cts,cjt->cjs",
            toeplitz[lag_block],
            shift_earlier(masked, lag_block),
            preferred_element_type=jnp.float32,
        )
        outer = jnp.einsum(
            "cjt,cjs->cts",
            masked,
            shift_later(reversed_series, lag_block),
            preferred_element_type=jnp.float32,
        )
        sums = diagonal_sums(outer)
        grad_ext = grad_ext + jnp.pad(
            sums, ((0, 0), (lag_block * block_len + 1, (blocks - lag_block) * block_len))
        )
    return (grad_in, grad_ext[:, block_len : block_len + length])


def per_device(query_proj, key_proj, value_proj, cotangent, filter_taps, span_slot, doc_lengths):
    parts = lax.axis_size("ctx")
    tok_dev, width = query_proj.shape
    narrow = width // parts
    rows_all = tok_dev * parts
    spans = rows_all // SPAN
    length = filter_taps.shape[0]
    blocks = (length + SPAN - 2) // SPAN + 1
    slot_ids = span_slot[0]
    span_ids = jnp.arange(spans, dtype=jnp.int32)
    inverse = jnp.sum(
        jnp.where(slot_ids[None, :] == span_ids[:, None], span_ids[None, :], 0), axis=1
    )
    starts = doc_starts(doc_lengths[0], spans)
    masks = [(span_ids - lag_block >= starts).astype(jnp.bfloat16) for lag_block in range(blocks)]
    toeplitz = build_blocks(jnp.transpose(filter_taps), SPAN, blocks)
    scale = float(rows_all * lax.axis_size("dp")) ** (-0.5)

    def to_order(array):
        return jnp.take(array.reshape(narrow, spans, SPAN), inverse, axis=1)

    def to_slots(array):
        return jnp.take(array, slot_ids, axis=1).reshape(narrow, rows_all)

    mixer_local = (key_proj.astype(jnp.float32) * value_proj.astype(jnp.float32)).astype(
        jnp.bfloat16
    )
    mixer_cols = lax.all_to_all(
        jnp.transpose(mixer_local), "ctx", split_axis=0, concat_axis=1, tiled=True
    )
    mixer = to_order(mixer_cols)
    mixed = conv_forward(mixer, toeplitz, masks).astype(jnp.bfloat16)
    mixed_local = jnp.transpose(
        lax.all_to_all(to_slots(mixed), "ctx", split_axis=1, concat_axis=0, tiled=True)
    )
    grad_query = (cotangent.astype(jnp.float32) * mixed_local.astype(jnp.float32)).astype(
        jnp.bfloat16
    )
    grad_mix_local = (cotangent.astype(jnp.float32) * query_proj.astype(jnp.float32)).astype(
        jnp.bfloat16
    )
    grad_mix_cols = lax.all_to_all(
        jnp.transpose(grad_mix_local), "ctx", split_axis=0, concat_axis=1, tiled=True
    )
    grad_series, grad_kernel = conv_backward(
        mixer, to_order(grad_mix_cols), toeplitz, masks, length
    )
    series_local = jnp.transpose(
        lax.all_to_all(
            to_slots(grad_series.astype(jnp.bfloat16)),
            "ctx",
            split_axis=1,
            concat_axis=0,
            tiled=True,
        )
    )
    series_wide = series_local.astype(jnp.float32)
    grad_key = (series_wide * value_proj.astype(jnp.float32)).astype(jnp.bfloat16)
    grad_value = (series_wide * key_proj.astype(jnp.float32)).astype(jnp.bfloat16)
    summed = lax.psum((grad_kernel * scale).astype(jnp.bfloat16), "dp").astype(jnp.float32)
    grad_filter = jnp.transpose(summed).astype(jnp.bfloat16)
    return (grad_query, grad_key, grad_value, grad_filter)


def solution(mesh):
    return jax.shard_map(
        per_device,
        mesh=mesh,
        in_specs=(
            P(("dp", "ctx"), "ch"),
            P(("dp", "ctx"), "ch"),
            P(("dp", "ctx"), "ch"),
            P(("dp", "ctx"), "ch"),
            P(None, ("ch", "ctx")),
            P("dp", None),
            P("dp", None),
        ),
        out_specs=(
            P(("dp", "ctx"), "ch"),
            P(("dp", "ctx"), "ch"),
            P(("dp", "ctx"), "ch"),
            P(None, ("ch", "ctx")),
        ),
        check_vma=False,
    )
```

profile of v0, /device:TPU:1, one launch (start us, length us, event | category | flops | bytes accessed | tf_op | source)
XLA Modules:
  0.0 359.5 jit_solution(15578626207706104470)
XLA Ops:
  0.6 1.1 copy.33
  1.8 1.2 copy.42
  3.0 0.8 fusion.11
  3.8 18.6 %all-to-all-start.2 = ((bf16[32,32,128]{2,1,0:T(8,128)(2,1)}), bf16[32,32,128]{2,1,0:T(8,128)(2,1)}, u32[]{:S(2)}, u32[]{:S(2)}) async-start(bf16[32,32,128]{2,1,0:T(8,128)(2,1)} %bitcast.18), calls=%async_computation.2 | async-start | bytes 524288 | tf_op jit(solution)/shard_map/all_to_all | solution.py:131
  22.4 0.9 broadcast_clamp_fusion.2
  23.9 0.8 select_reduce_fusion
  24.7 0.9 broadcast_clamp_fusion.1
  25.5 0.9 broadcast_clamp_fusion
  26.4 0.8 copy.37
  27.3 57.4 %gather_fusion.1 = bf16[16384,32]{1,0:T(8,128)(2,1)} fusion(bf16[32,640]{0,1:T(8,128)(2,1)S(1)} %pad.48, s32[16384]{0:T(1024)S(1)} %broadcast_clamp_fusion.2), kind=kCustom, calls=%fused_computation.1.clone | custom fusion | bytes 2162688 | tf_op jit(solution)/shard_map/jit(_take)/gather | solution.py:24
  84.7 4.0 %copy.38 = bf16[128,128,32]{1,0,2:T(8,128)(2,1)S(1)} copy(bf16[128,128,32]{2,1,0:T(8,128)(2,1)} %bitcast.82) | data formatting | bytes 2097152 | tf_op jit(solution)/shard_map/jit(_take)/gather | solution.py:24
  88.7 57.4 %gather_fusion.2 = bf16[16384,32]{1,0:T(8,128)(2,1)} fusion(bf16[32,640]{0,1:T(8,128)(2,1)S(1)} %pad.48, s32[16384]{0:T(1024)S(1)} %broadcast_clamp_fusion.1), kind=kCustom, calls=%fused_computation.5.clone | custom fusion | bytes 2162688 | tf_op jit(solution)/shard_map/jit(_take)/gather | solution.py:24
  146.1 4.0 %copy.39 = bf16[128,128,32]{1,0,2:T(8,128)(2,1)S(1)} copy(bf16[128,128,32]{2,1,0:T(8,128)(2,1)} %bitcast.83) | data formatting | bytes 2097152 | tf_op jit(solution)/shard_map/jit(_take)/gather | solution.py:24
  150.1 57.4 %gather_fusion.3 = bf16[16384,32]{1,0:T(8,128)(2,1)} fusion(bf16[32,640]{0,1:T(8,128)(2,1)S(1)} %pad.48, s32[16384]{0:T(1024)S(1)} %broadcast_clamp_fusion), kind=kCustom, calls=%fused_computation.6.clone | custom fusion | bytes 2162688 | tf_op jit(solution)/shard_map/jit(_take)/gather | solution.py:24
  207.4 4.0 %copy.40 = bf16[128,128,32]{1,0,2:T(8,128)(2,1)S(1)} copy(bf16[128,128,32]{2,1,0:T(8,128)(2,1)} %bitcast.81) | data formatting | bytes 2097152 | tf_op jit(solution)/shard_map/jit(_take)/gather | solution.py:24
  211.8 1.6 gather_fusion.5
  213.6 0.7 copy-done.4
  215.7 0.8 copy.44
  216.5 2.2 gather_fusion.6
  218.7 1.8 select_bitcast_fusion
  220.5 14.0 %all-to-all-start.3 = ((bf16[32,32,128]{2,0,1:T(8,128)(2,1)}), bf16[32,32,128]{2,0,1:T(8,128)(2,1)S(1)}, u32[]{:S(2)}, u32[]{:S(2)}) async-start(bf16[32,32,128]{2,0,1:T(8,128)(2,1)} %select_bitcast_fusion), calls=%async_computation.3 | async-start | bytes 524288 | tf_op jit(solution)/shard_map/all_to_all | solution.py:138
  234.5 1.8 copy.34
  236.3 1.8 copy.35
  238.1 17.0 %all-to-all-done.3 = bf16[32,32,128]{2,0,1:T(8,128)(2,1)S(1)} async-done(((bf16[32,32,128]{2,0,1:T(8,128)(2,1)}), bf16[32,32,128]{2,0,1:T(8,128)(2,1)S(1)}, u32[]{:S(2)}, u32[]{:S(2)}) %all-to-all-start.3) | async-done | bytes 262176 | tf_op jit(solution)/shard_map/all_to_all | solution.py:138
  255.1 2.0 fusion.12
  257.1 25.5 %all_to_all.52 = bf16[32,32,128]{2,1,0:T(8,128)(2,1)S(1)} all-to-all(bf16[32,32,128]{2,1,0:T(8,128)(2,1)S(1)} %bitcast.85), channel_id=1, replica_groups=mesh['dp'=2,'ctx'=32,'ch'=8] {'ctx'}, dimensions={0} | all-to-all | bytes 524288 | tf_op jit(solution)/shard_map/all_to_all | solution.py:117
  282.6 1.3 gather_fusion
  283.8 1.0 fusion.15
  285.6 0.7 convolution_add_fusion.3
  286.3 0.7 fusion
  287.7 0.8 select_bitcast_fusion.1
  288.5 6.1 %all-to-all-start.1 = ((bf16[32,32,128]{2,0,1:T(8,128)(2,1)}), bf16[32,32,128]{2,0,1:T(8,128)(2,1)S(1)}, u32[]{:S(2)}, u32[]{:S(2)}) async-start(bf16[32,32,128]{2,0,1:T(8,128)(2,1)} %select_bitcast_fusion.1), calls=%async_computation.1 | async-start | bytes 524288 | tf_op jit(solution)/shard_map/all_to_all | solution.py:123
  294.6 1.8 copy.46
  296.4 1.8 copy.47
  299.8 2.4 copy.50
  302.2 2.2 slice.62
  304.5 9.4 %reshape.94 = f32[32,128,255]{2,1,0:T(8,128)} reshape(f32[32,32640]{1,0:T(8,128)} %slice.62) | data formatting | bytes 8355840 | tf_op jit(solution)/shard_map/reshape | solution.py:33
  313.9 2.6 reduce_sum.39
  317.5 2.4 copy.49
  319.9 2.2 slice.61
  322.2 9.4 %reshape.92 = f32[32,128,255]{2,1,0:T(8,128)} reshape(f32[32,32640]{1,0:T(8,128)} %slice.61) | data formatting | bytes 8355840 | tf_op jit(solution)/shard_map/reshape | solution.py:33
  331.6 2.6 reduce_sum.38
  335.3 2.4 copy.48
  337.7 2.2 slice.60
  340.0 9.4 %reshape.90 = f32[32,128,255]{2,1,0:T(8,128)} reshape(f32[32,32640]{1,0:T(8,128)} %slice.60) | data formatting | bytes 8355840 | tf_op jit(solution)/shard_map/reshape | solution.py:33
  349.3 2.6 reduce_sum.37
  352.1 6.4 %psum.7 = bf16[256,32]{0,1:T(8,128)(2,1)} all-reduce(bf16[256,32]{0,1:T(8,128)(2,1)S(1)} %fusion.35), channel_id=1, replica_groups=mesh['dp'=2,'ctx'=32,'ch'=8] {'dp'}, use_global_device_ids=true, to_apply=%region_6.9 | all-reduce | flops 8192 | bytes 32768 | tf_op jit(solution)/shard_map/psum | solution.py:149
  358.6 0.9 copy.45
  (51 shorter events, 7.7 us)
Async XLA Ops:
  1.8 25.5 %copy-start.2 = (bf16[128,1024]{0,1:T(8,128)(2,1)}, bf16[128,1024]{0,1:T(8,128)(2,1)S(1)}, u32[]{:S(2)}) copy-start(bf16[128,1024]{0,1:T(8,128)(2,1)S(1)} %copy.33) | copy-start | bytes 786436
  3.8 208.1 %all-to-all-start.2 = ((bf16[32,32,128]{2,1,0:T(8,128)(2,1)}), bf16[32,32,128]{2,1,0:T(8,128)(2,1)}, u32[]{:S(2)}, u32[]{:S(2)}) async-start(bf16[32,32,128]{2,1,0:T(8,128)(2,1)} %bitcast.18), calls=%async_computation.2 | async-start | bytes 524288 | tf_op jit(solution)/shard_map/all_to_all | solution.py:131
  207.4 4.0 %copy-start.8 = (s32[1,24]{1,0:T(1,128)S(1)}, s32[1,24]{1,0:T(1,128)}, u32[]{:S(2)}) copy-start(s32[1,24]{1,0:T(1,128)} %param.20) | copy-start | bytes 292
  207.4 4.4 %copy-start.9 = (s32[1,32]{1,0:T(1,128)S(1)}, s32[1,32]{1,0:T(1,128)}, u32[]{:S(2)}) copy-start(s32[1,32]{1,0:T(1,128)} %param.19) | copy-start | bytes 388
  213.4 3.1 copy-start
  213.5 0.7 copy-start.4
  213.5 0.8 copy-start.6
  220.5 34.6 %all-to-all-start.3 = ((bf16[32,32,128]{2,0,1:T(8,128)(2,1)}), bf16[32,32,128]{2,0,1:T(8,128)(2,1)S(1)}, u32[]{:S(2)}, u32[]{:S(2)}) async-start(bf16[32,32,128]{2,0,1:T(8,128)(2,1)} %select_bitcast_fusion), calls=%async_computation.3 | async-start | bytes 524288 | tf_op jit(solution)/shard_map/all_to_all | solution.py:138
  285.6 13.2 %copy-start.7 = (bf16[32,32,128]{2,1,0:T(8,128)(2,1)S(1)}, bf16[32,32,128]{2,1,0:T(8,128)(2,1)}, u32[]{:S(2)}) copy-start(bf16[32,32,128]{2,1,0:T(8,128)(2,1)} %copy-done.6) | copy-start | bytes 786436
  288.5 70.0 %all-to-all-start.1 = ((bf16[32,32,128]{2,0,1:T(8,128)(2,1)}), bf16[32,32,128]{2,0,1:T(8,128)(2,1)S(1)}, u32[]{:S(2)}, u32[]{:S(2)}) async-start(bf16[32,32,128]{2,0,1:T(8,128)(2,1)} %select_bitcast_fusion.1), calls=%async_computation.1 | async-start | bytes 524288 | tf_op jit(solution)/shard_map/all_to_all | solution.py:123
  313.9 2.6 copy-start.5
  331.6 2.6 copy-start.1
  349.3 9.2 %copy-start.3 = (bf16[128,1024]{0,1:T(8,128)(2,1)S(1)}, bf16[128,1024]{0,1:T(8,128)(2,1)}, u32[]{:S(2)}) copy-start(bf16[128,1024]{0,1:T(8,128)(2,1)} %copy-done.2) | copy-start | bytes 786436
where the time goes:
time: 361 us; the launch traced here: 359 us
  local copies, waits for them, and re-layouts  247 us (68%)
  starting transfers between devices  38.7 us (11%)
  blocking collectives  31.9 us (9%)
  other arithmetic  18.9 us (5%)
  waiting for transfers between devices  17 us (5%)
  matrix products  4.87 us (1%)
    gather x6, local copies, waits for them, and re-layouts, build_blocks(): result.append(jnp.take(extended, table, axis=1))  184 us
    reshape x3, local copies, waits for them, and re-layouts, diagonal_sums(): padded[:, :block_len * (2 * block_len - 1)]  28.1 us
    all_to_all x1, blocking collectives, per_device(): lax.all_to_all(jnp.transpose(mixer_local), 'ctx', split_axis=0, concat_ax...  25.5 us
    unnamed x31, local copies, waits for them, and re-layouts  19.2 us
    all_to_all x1, starting transfers between devices, per_device(): lax.all_to_all(jnp.transpose(grad_mix_local), 'ctx', split_axis=0, concat...  18.6 us
    all_to_all x1, waiting for transfers between devices, per_device(): lax.all_to_all(to_slots(grad_series.astype(jnp.bfloat16)), 'ctx', split_a...  17 us
    all_to_all x1, starting transfers between devices, per_device(): lax.all_to_all(to_slots(grad_series.astype(jnp.bfloat16)), 'ctx', split_a...  14 us
    reduce_sum x3, other arithmetic, diagonal_sums(): return jnp.sum(skewed, axis=1)  7.91 us
  transfers between devices with their start and end apart: 3, of which 1 were waited for; matrix products, arithmetic and copies ran while one was open for 70% of the time, Pallas kernels for 0%

commit v1 on v0

v1 whole, which is shorter than its diff:
```python
import functools

import jax
import jax.numpy as jnp
import numpy as np
from jax import lax
from jax.experimental import pallas as pl
from jax.experimental.pallas import tpu as pltpu
from jax.sharding import PartitionSpec as P

SPAN = 128
PTS = 2 * SPAN
HALF = SPAN // 2
F32, BF16 = jnp.float32, jnp.bfloat16


def split_bf16(matrix):
    high = matrix.astype(BF16)
    low = (matrix - high.astype(np.float64)).astype(BF16)
    return high, low


def transforms():
    freq = np.arange(SPAN)[:, None]
    point = np.arange(PTS)[None, :]
    angle = 2 * np.pi * ((freq * point) % PTS) / PTS
    real, imag = np.cos(angle), -np.sin(angle)
    imag[0] = np.where(np.arange(PTS) % 2 == 0, 1.0, -1.0)
    forward = np.concatenate([real, imag], 0)
    weight = np.full((PTS, 1), 2.0 / PTS)
    weight[0], weight[SPAN] = 1.0 / PTS, 1.0 / PTS
    inverse = (forward * weight).T
    return forward, inverse


def dot(a, b, dims=((1,), (0,))):
    return lax.dot_general(a, b, (dims, ((), ())), preferred_element_type=F32)


def halves(x):
    high = x.astype(BF16)
    return high, (x - high.astype(F32)).astype(BF16)


def spectrum_left(high, low, x):
    return dot(high, x) + dot(low, x)


def spectrum_right(x, high, low):
    return dot(x, high) + dot(x, low)


def invert_left(high, low, spec):
    s_high, s_low = halves(spec)
    return dot(high, s_high) + (dot(high, s_low) + dot(low, s_high))


def invert_right(spec, high, low):
    s_high, s_low = halves(spec)
    return dot(s_high, high) + (dot(s_low, high) + dot(s_high, low))


def multiply(ar, ai, br, bi, zero, sign):
    b_im = sign * jnp.where(zero, 0.0, bi)
    b_second = jnp.where(zero, bi, br)
    return ar * br - ai * b_im, ai * b_second + ar * b_im


def pack_halves(lo, hi):
    axis = lo.ndim - 1
    left = lax.broadcasted_iota(jnp.int32, lo.shape, axis) < HALF
    first = jnp.where(left, lo, pltpu.roll(hi, HALF, axis))
    second = jnp.where(left, pltpu.roll(lo, HALF, axis), hi)
    return first, second


def own_kind(slot_ref, len_ref):
    span = slot_ref[0, lax.axis_index("ctx")]

    def step(d, carry):
        pos, kind = carry
        length = len_ref[0, d]
        two = length == 2
        kind = jnp.where(two & (span == pos), 1, kind)
        kind = jnp.where(two & (span == pos + 1), 2, kind)
        return pos + length, kind

    zero = jnp.int32(0)
    return lax.fori_loop(0, len_ref.shape[1], step, (zero, zero))[1]


def send_kernel(slot_ref, len_ref, taps_ref, q_ref, k_ref, v_ref, c_ref, out_ref):
    kind = own_kind(slot_ref, len_ref)
    count = out_ref.shape[0]

    def put(a_ref, b_ref):
        product = a_ref[...].astype(F32) * b_ref[...].astype(F32)
        out_ref[:, 0:32, :] = jnp.transpose(product).astype(BF16).reshape(count, 32, SPAN)

    @pl.when(kind == 1)
    def _():
        put(k_ref, v_ref)

    @pl.when(kind != 1)
    def _():
        put(c_ref, q_ref)

    taps = jnp.transpose(taps_ref[0:SPAN, :].astype(F32))
    first, second = pack_halves(taps[0:16], taps[16:32])
    mine = jnp.where(lax.axis_index("dp") == 0, first, second).astype(BF16)
    out_ref[:, 32:48, :] = jnp.broadcast_to(mine[None], (count, 16, SPAN))


def partial_kernel(
    slot_ref, len_ref, q_ref, k_ref, v_ref, c_ref, fwd_hi, fwd_lo, inv_hi, inv_lo,
    keep_ref, send_ref, table_ref, inverse_ref,
):
    @pl.when(pl.program_id(0) == 0)
    def _():
        slots = slot_ref.shape[1]

        def fill(r, carry):
            inverse_ref[slot_ref[0, r]] = r
            return carry

        lax.fori_loop(0, slots, fill, 0)

        def step(d, pos):
            length = len_ref[0, d]
            two = length == 2
            a = inverse_ref[pos]
            b = inverse_ref[jnp.minimum(pos + 1, slots - 1)]
            table_ref[0, a] = jnp.where(two, 1, 0)
            table_ref[1, a] = jnp.where(two, b, a)

            @pl.when(two)
            def _():
                table_ref[0, b] = -1
                table_ref[1, b] = a

            return pos + length

        lax.fori_loop(0, len_ref.shape[1], step, jnp.int32(0))

    x = (k_ref[...].astype(F32) * v_ref[...].astype(F32)).astype(BF16)
    g = (c_ref[...].astype(F32) * q_ref[...].astype(F32)).astype(BF16)
    xs = spectrum_left(fwd_hi[...], fwd_lo[...], x)
    gs = spectrum_left(fwd_hi[...], fwd_lo[...], g)
    shape = (SPAN, x.shape[1])
    zero = lax.broadcasted_iota(jnp.int32, shape, 0) == 0
    pr, pi = multiply(gs[:SPAN], gs[SPAN:], xs[:SPAN], xs[SPAN:], zero, -1.0)
    taps = invert_left(inv_hi[...], inv_lo[...], jnp.concatenate([pr, pi], 0))
    count = keep_ref.shape[0]
    rows = jnp.transpose(taps).reshape(count, 32, SPAN)
    first, second = pack_halves(rows[:, 0:16], rows[:, 16:32])
    is_first = lax.axis_index("dp") == 0
    keep_ref[...] = jnp.where(is_first, first, second)
    send_ref[...] = jnp.where(is_first, second, first).astype(BF16)


def pair_kernel(
    table_ref, got_ref, taps_ref, keep_ref, other_ref, fwd_hi, fwd_lo, inv_hi, inv_lo,
    tap_hi, tap_lo, out_ref, spec_ref,
):
    slots = got_ref.shape[0]
    taps = jnp.transpose(taps_ref[...].astype(F32)).astype(BF16)
    hs = spectrum_right(taps, tap_hi[...], tap_lo[...])
    hr, hi = hs[:, :SPAN], hs[:, SPAN:]
    zero = lax.broadcasted_iota(jnp.int32, hr.shape, 1) == 0
    h_im = jnp.where(zero, 0.0, hi)
    h_second = jnp.where(zero, hi, hr)
    series = got_ref[:, 0:32, :].reshape(slots * 32, SPAN)
    spec = spectrum_right(series, fwd_hi[...], fwd_lo[...])
    spec = spec.reshape(slots, 32, PTS)
    for p in range(slots):
        sign = table_ref[0, p].astype(F32)
        to = table_ref[1, p]
        on = jnp.abs(sign)
        sr, si = spec[p, :, :SPAN], spec[p, :, SPAN:]
        spec_ref[to, :, :SPAN] = on * (sr * hr) - sign * (si * h_im)
        spec_ref[to, :, SPAN:] = on * (si * h_second) + sign * (sr * h_im)
    result = invert_right(spec_ref[...].reshape(slots * 32, PTS), inv_hi[...], inv_lo[...])
    out_ref[:, 0:32, :] = result.astype(BF16).reshape(slots, 32, SPAN)
    out_ref[:, 32:48, :] = (keep_ref[...] + other_ref[...].astype(F32)).astype(BF16)


def pair_taps_kernel(table_ref, got_ref, fwd_hi, fwd_lo, lag_hi, lag_lo, out_ref, spec_ref):
    slots = got_ref.shape[0]
    series = got_ref[:, 0:32, :].reshape(slots * 32, SPAN)
    spec_ref[...] = spectrum_right(series, fwd_hi[...], fwd_lo[...]).reshape(slots, 32, PTS)
    zero = lax.broadcasted_iota(jnp.int32, (32, SPAN), 1) == 0

    def step(p, carry):
        tr, ti = carry
        to = table_ref[1, p]
        on = jnp.where(table_ref[0, p] == 1, 1.0, 0.0)
        xs, gs = spec_ref[p], spec_ref[to]
        pr, pi = multiply(gs[:, :SPAN], gs[:, SPAN:], xs[:, :SPAN], xs[:, SPAN:], zero, -1.0)
        return tr + on * pr, ti + on * pi

    none = jnp.zeros((32, SPAN), F32)
    tr, ti = lax.fori_loop(0, slots, step, (none, none))
    out_ref[...] = invert_right(jnp.concatenate([tr, ti], 1), lag_hi[...], lag_lo[...])


def local_kernel(
    own_ref, other_ref, q_ref, k_ref, v_ref, c_ref, fwd_hi, fwd_lo, inv_hi, inv_lo,
    first_hi, first_lo, second_hi, second_lo, mixed_ref, series_ref,
):
    x = (k_ref[...].astype(F32) * v_ref[...].astype(F32)).astype(BF16)
    g = (c_ref[...].astype(F32) * q_ref[...].astype(F32)).astype(BF16)
    xs = spectrum_left(fwd_hi[...], fwd_lo[...], x)
    gs = spectrum_left(fwd_hi[...], fwd_lo[...], g)
    own, other = own_ref[...], other_ref[...]
    is_first = lax.axis_index("dp") == 0
    left = lax.broadcasted_iota(jnp.int32, own.shape, 2) < HALF

    def rows(packed):
        packed = packed.astype(F32)
        both = jnp.concatenate([jnp.where(left, packed, 0.0), jnp.where(left, 0.0, packed)], 1)
        return both.astype(BF16).reshape(own.shape[0] * 32, SPAN)

    first = rows(jnp.where(is_first, own.astype(F32), other.astype(F32)))
    second = rows(jnp.where(is_first, other.astype(F32), own.astype(F32)))
    nt = ((1,), (1,))
    hs = dot(first_hi[...], first, nt) + dot(first_lo[...], first, nt)
    hs = hs + (dot(second_hi[...], second, nt) + dot(second_lo[...], second, nt))
    zero = lax.broadcasted_iota(jnp.int32, (SPAN, x.shape[1]), 0) == 0
    hr, hi = hs[:SPAN], hs[SPAN:]
    mr, mi = multiply(xs[:SPAN], xs[SPAN:], hr, hi, zero, 1.0)
    mixed_ref[...] = invert_left(inv_hi[...], inv_lo[...], jnp.concatenate([mr, mi], 0))
    sr, si = multiply(gs[:SPAN], gs[SPAN:], hr, hi, zero, -1.0)
    series_ref[...] = invert_left(inv_hi[...], inv_lo[...], jnp.concatenate([sr, si], 0))


def tap_sum_kernel(got_ref, out_ref):
    out_ref[...] = jnp.sum(got_ref[...].astype(F32), axis=0)


def finish_kernel(
    slot_ref, len_ref, got_ref, mixed_ref, series_ref, k_ref, v_ref, c_ref,
    gq_ref, gk_ref, gv_ref,
):
    kind = own_kind(slot_ref, len_ref)
    rows = got_ref[:, 0:32, :].astype(F32).reshape(got_ref.shape[0] * 32, SPAN)
    pair = jnp.transpose(rows)
    mixed = mixed_ref[...] + jnp.where(kind == 2, pair, 0.0)
    series = series_ref[...] + jnp.where(kind == 1, pair, 0.0)
    mixed = mixed.astype(BF16).astype(F32)
    series = series.astype(BF16).astype(F32)
    gq_ref[...] = (c_ref[...].astype(F32) * mixed).astype(BF16)
    gk_ref[...] = (series * v_ref[...].astype(F32)).astype(BF16)
    gv_ref[...] = (series * k_ref[...].astype(F32)).astype(BF16)


def taps_out_kernel(scale, own_ref, other_ref, pair_ref, pair_other_ref, out_ref):
    is_first = lax.axis_index("dp") == 0
    own, other = own_ref[...], other_ref[...]
    first = jnp.where(is_first, own, other)
    second = jnp.where(is_first, other, own)
    lo, hi = pack_halves(first, second)
    near = jnp.concatenate([lo, hi], 0)
    total = pair_ref[...] + pair_other_ref[...]
    total = jnp.concatenate([total[:, :SPAN] + near, total[:, SPAN:]], 1)
    out_ref[...] = (jnp.transpose(total) * scale).astype(BF16)


SMEM = pl.BlockSpec(memory_space=pltpu.SMEM)
VMEM = pl.BlockSpec(memory_space=pltpu.VMEM)


def params():
    return pltpu.CompilerParams(vmem_limit_bytes=48 * 1024 * 1024)


def cost(flops, moved):
    return pl.CostEstimate(flops=int(flops), bytes_accessed=int(moved), transcendentals=0)


def per_device(query, key, value, cotangent, filter_taps, span_slot, doc_lengths):
    parts = lax.axis_size("ctx")
    tokens, width = query.shape
    scale = float(tokens * parts * lax.axis_size("dp")) ** (-0.5)
    forward, inverse = transforms()
    fwd = [jnp.asarray(m) for m in split_bf16(forward[:, :SPAN])]
    fwd_t = [jnp.asarray(m) for m in split_bf16(forward[:, :SPAN].T)]
    inv = [jnp.asarray(m) for m in split_bf16(inverse[:SPAN])]
    inv_t = [jnp.asarray(m) for m in split_bf16(inverse[:SPAN].T)]
    tap_t = [jnp.asarray(m) for m in split_bf16(np.roll(forward, -SPAN, 1).T)]
    lag_t = [jnp.asarray(m) for m in split_bf16(np.roll(inverse, SPAN, 0).T)]
    early, late = forward[:, :HALF], forward[:, HALF:SPAN]
    first = [jnp.asarray(m) for m in split_bf16(np.concatenate([early, early], 1))]
    second = [jnp.asarray(m) for m in split_bf16(np.concatenate([late, late], 1))]
    swap = [(0, 1), (1, 0)]
    block = 256
    steps = width // block
    wide = pl.BlockSpec((tokens, block), lambda i: (0, i))
    group = block // 32
    packed = pl.BlockSpec((group, 16, SPAN), lambda i: (i, 0, 0))

    def whole(array):
        return pl.BlockSpec(array.shape, lambda i: (0,) * array.ndim)

    out = pl.pallas_call(
        send_kernel,
        out_shape=jax.ShapeDtypeStruct((parts, 48, SPAN), BF16),
        in_specs=[SMEM, SMEM] + [VMEM] * 5,
        out_specs=VMEM,
        compiler_params=params(),
        cost_estimate=cost(2 * tokens * width, 10 * tokens * width),
        name="send",
    )(span_slot, doc_lengths, filter_taps, query, key, value, cotangent)
    got = lax.all_to_all(out, "ctx", split_axis=0, concat_axis=0, tiled=True)

    keep, give, table = pl.pallas_call(
        partial_kernel,
        grid=(steps,),
        out_shape=(
            jax.ShapeDtypeStruct((parts, 16, SPAN), F32),
            jax.ShapeDtypeStruct((parts, 16, SPAN), BF16),
            jax.ShapeDtypeStruct((2, parts), jnp.int32),
        ),
        in_specs=[SMEM, SMEM] + [wide] * 4 + [whole(m) for m in fwd + inv],
        out_specs=(packed, packed, SMEM),
        scratch_shapes=[pltpu.SMEM((parts,), jnp.int32)],
        compiler_params=params(),
        cost_estimate=cost(2e9, 10 * tokens * width),
        name="partial_taps",
    )(span_slot, doc_lengths, query, key, value, cotangent, *fwd, *inv)
    taken = lax.ppermute(give, "dp", swap)

    back = pl.pallas_call(
        pair_kernel,
        out_shape=jax.ShapeDtypeStruct((parts, 48, SPAN), BF16),
        in_specs=[SMEM] + [VMEM] * 10,
        out_specs=VMEM,
        scratch_shapes=[pltpu.VMEM((parts, 32, PTS), F32)],
        compiler_params=params(),
        cost_estimate=cost(1e9, 10 * tokens * width),
        name="pair",
    )(table, got, filter_taps, keep, taken, *fwd_t, *inv_t, *tap_t)
    landed = lax.all_to_all(back, "ctx", split_axis=0, concat_axis=0, tiled=True)

    pair_taps = pl.pallas_call(
        pair_taps_kernel,
        out_shape=jax.ShapeDtypeStruct((32, PTS), F32),
        in_specs=[SMEM] + [VMEM] * 5,
        out_specs=VMEM,
        scratch_shapes=[pltpu.VMEM((parts, 32, PTS), F32)],
        compiler_params=params(),
        cost_estimate=cost(1e9, 6 * tokens * width),
        name="pair_taps",
    )(table, got, *fwd_t, *lag_t)
    pair_taps_other = lax.ppermute(pair_taps, "dp", swap)

    taps_own = got[:, 32:48, :]
    taps_other = lax.ppermute(taps_own, "dp", swap)
    mixed, series = pl.pallas_call(
        local_kernel,
        grid=(steps,),
        out_shape=(jax.ShapeDtypeStruct((tokens, width), F32),) * 2,
        in_specs=[packed, packed] + [wide] * 4 + [whole(m) for m in fwd + inv + first + second],
        out_specs=(wide, wide),
        compiler_params=params(),
        cost_estimate=cost(3e9, 20 * tokens * width),
        name="local",
    )(taps_own, taps_other, query, key, value, cotangent, *fwd, *inv, *first, *second)

    near = pl.pallas_call(
        tap_sum_kernel,
        grid=(1,),
        out_shape=jax.ShapeDtypeStruct((16, SPAN), F32),
        in_specs=[pl.BlockSpec((parts, 16, SPAN), lambda i: (0, 2, 0))],
        out_specs=pl.BlockSpec((16, SPAN), lambda i: (0, 0)),
        compiler_params=params(),
        cost_estimate=cost(parts * 16 * SPAN, parts * 32 * SPAN),
        name="tap_sum",
    )(landed)
    near_other = lax.ppermute(near, "dp", swap)

    grads = pl.pallas_call(
        finish_kernel,
        grid=(steps,),
        out_shape=(jax.ShapeDtypeStruct((tokens, width), BF16),) * 3,
        in_specs=[SMEM, SMEM, pl.BlockSpec((group, 48, SPAN), lambda i: (i, 0, 0))] + [wide] * 5,
        out_specs=(wide,) * 3,
        compiler_params=params(),
        cost_estimate=cost(10 * tokens * width, 24 * tokens * width),
        name="finish",
    )(span_slot, doc_lengths, landed, mixed, series, key, value, cotangent)

    grad_filter = pl.pallas_call(
        functools.partial(taps_out_kernel, scale),
        out_shape=jax.ShapeDtypeStruct((PTS, 32), BF16),
        in_specs=[VMEM] * 4,
        out_specs=VMEM,
        compiler_params=params(),
        name="taps_out",
    )(near, near_other, pair_taps, pair_taps_other)
    return (*grads, grad_filter)


def solution(mesh):
    return jax.shard_map(
        per_device,
        mesh=mesh,
        in_specs=(
            P(("dp", "ctx"), "ch"),
            P(("dp", "ctx"), "ch"),
            P(("dp", "ctx"), "ch"),
            P(("dp", "ctx"), "ch"),
            P(None, ("ch", "ctx")),
            P("dp", None),
            P("dp", None),
        ),
        out_specs=(
            P(("dp", "ctx"), "ch"),
            P(("dp", "ctx"), "ch"),
            P(("dp", "ctx"), "ch"),
            P(None, ("ch", "ctx")),
        ),
        check_vma=False,
    )
```

time: 361 us -> 101 us (0.28)
  local copies, waits for them, and re-layouts: 247 us -> 5.47 us
  blocking collectives: 31.9 us -> 0 us
  waiting for transfers between devices: 17 us -> 38.5 us
  other arithmetic: 18.9 us -> 0 us
  Pallas kernels: 0 us -> 17.9 us
  matrix products: 4.87 us -> 0 us
    gather x10 -> x0, local copies, waits for them, and re-layouts: 190 us -> none  [the longest x6 184 us: build_blocks(): result.append(jnp.take(extended, table, axis=1))]
    reshape x3 -> x0, local copies, waits for them, and re-layouts: 28.1 us -> none  [diagonal_sums(): padded[:, :block_len * (2 * block_len - 1)]]
    all_to_all x1 -> x0, blocking collectives: 25.5 us -> none  [per_device(): lax.all_to_all(jnp.transpose(mixer_local), 'ctx', split_axis=0, concat_ax...]
    all_to_all x3 -> x2, waiting for transfers between devices: 17 us -> 37.6 us  [the longest x1 19.4 us: per_device(): lax.all_to_all(back, 'ctx', split_axis=0, concat_axis=0, tiled=True)]
    pallas_call x0 -> x8, Pallas kernels: none -> 17.9 us  [the longest x1 4.39 us: per_device(): pl.pallas_call(partial_kernel, grid=(steps,), out_shape=(jax.ShapeDtypeSt...]
    all_to_all x3 -> x2, starting transfers between devices: 38.7 us -> 24.4 us  [the longest x1 18.6 us: per_device(): got = lax.all_to_all(out, 'ctx', split_axis=0, concat_axis=0, tiled=True)]
    unnamed x31 -> x54, local copies, waits for them, and re-layouts: 19.2 us -> 5.46 us
    ppermute x0 -> x4, starting transfers between devices: none -> 13 us  [the longest x1 4.89 us: per_device(): near_other = lax.ppermute(near, 'dp', swap)]
  transfers between devices with their start and end apart: 3 -> 6, of which waited for: 1 -> 3; matrix products, arithmetic and copies ran while one was open for 70% -> 0% of each run, Pallas kernels for 0% -> 13%
where the time goes in v1:
time: 101 us; the launch traced here: 100 us
  waiting for transfers between devices  38.5 us (38%)
  starting transfers between devices  37.4 us (37%)
  Pallas kernels  17.9 us (18%)
  local copies, waits for them, and re-layouts  5.47 us (5%)
  between operations  1.01 us (1%)
    all_to_all x1, waiting for transfers between devices, per_device(): lax.all_to_all(back, 'ctx', split_axis=0, concat_axis=0, tiled=True)  19.4 us
    all_to_all x1, starting transfers between devices, per_device(): got = lax.all_to_all(out, 'ctx', split_axis=0, concat_axis=0, tiled=True)  18.6 us
    all_to_all x1, waiting for transfers between devices, per_device(): got = lax.all_to_all(out, 'ctx', split_axis=0, concat_axis=0, tiled=True)  18.1 us
    all_to_all x1, starting transfers between devices, per_device(): lax.all_to_all(back, 'ctx', split_axis=0, concat_axis=0, tiled=True)  5.81 us
    unnamed x54, local copies, waits for them, and re-layouts  5.46 us
    ppermute x1, starting transfers between devices, per_device(): near_other = lax.ppermute(near, 'dp', swap)  4.89 us
    pallas_call x1, Pallas kernels, per_device(): pl.pallas_call(partial_kernel, grid=(steps,), out_shape=(jax.ShapeDtypeSt...  4.39 us
    pallas_call x1, Pallas kernels, per_device(): pl.pallas_call(local_kernel, grid=(steps,), out_shape=(jax.ShapeDtypeStru...  3.97 us
  transfers between devices with their start and end apart: 6, of which 3 were waited for; matrix products, arithmetic and copies ran while one was open for 0% of the time, Pallas kernels for 13%

profile of v1, /device:TPU:1, one launch (start us, length us, event | category | flops | bytes accessed | tf_op | source)
XLA Modules:
  0.0 100.3 jit_solution(14928538783641898293)
XLA Ops:
  0.6 0.0 copy-start.9
  0.6 0.0 copy-start.8
  0.7 0.8 copy.27.taps_ref
  1.5 0.0 copy-done.9
  1.5 0.0 copy-done.8
  1.5 0.0 copy-start
  1.5 0.9 copy-done
  2.5 0.9 copy-done.2
  3.4 0.9 copy-done.4
  4.4 0.9 copy-done.6
  5.3 0.0 copy-start.17
  5.3 1.8 %send.1 = bf16[32,48,128]{2,1,0:T(8,128)(2,1)} custom-call(s32[1,32]{1,0:T(1,128)S(1)} %copy-done.8, s32[1,24]{1,0:T(1,128)S(1)} %copy-done.9, bf16[256,32]{1,0:T(8,128)(2,1)S(1)} %copy.27.taps_ref, bf16[128,1024]{1,0:T(8,128)(2,1)S(1)} %copy-done.6, bf16[128,1024]{1,0:T(8,128)(2,1)S(1)} %copy-done, bf16[128,1024]{1,0:T(8,128)(2,1)S(1)} %copy-done.2, ...), custom_call_target="tpu_custom_call" | custom-call | flops 262144 | bytes 1310720 | tf_op jit(solution)/shard_map/send/pallas_call | solution.py:304
  7.1 18.6 %all-to-all-start = ((bf16[32,48,128]{2,1,0:T(8,128)(2,1)}), bf16[32,48,128]{2,1,0:T(8,128)(2,1)S(1)}, u32[]{:S(2)}, u32[]{:S(2)}) async-start(bf16[32,48,128]{2,1,0:T(8,128)(2,1)} %send.1), calls=%async_computation | async-start | bytes 786432 | tf_op jit(solution)/shard_map/all_to_all | solution.py:313
  25.8 0.0 copy-done.7
  25.8 0.0 copy-done.14
  25.8 0.0 copy-done.15
  25.8 0.0 copy-done.16
  25.8 0.0 copy-done.17
  25.8 0.0 copy-start.12
  25.9 0.0 copy-start.13
  25.9 0.0 copy-start.22
  25.9 0.0 copy-start.23
  25.9 0.0 copy-start.24
  25.9 0.0 copy-start.25
  25.9 4.4 %partial_taps.1 = (f32[32,16,128]{2,1,0:T(8,128)S(1)}, bf16[32,16,128]{2,1,0:T(8,128)(2,1)S(1)}, s32[2,32]{1,0:T(2,128)S(1)}) custom-call(s32[1,32]{1,0:T(1,128)S(1)} %copy-done.8, s32[1,24]{1,0:T(1,128)S(1)} %copy-done.9, bf16[128,1024]{1,0:T(8,128)(2,1)S(1)} %copy-done.7, bf16[128,1024]{1,0:T(8,128)(2,1)S(1)} %copy-done.1, ...), custom_call_target="tpu_custom_call" | custom-call | flops 2000000000 | bytes 1310720 | tf_op jit(solution)/shard_map/partial_taps/pallas_call | solution.py:315
  30.3 2.9 %collective-permute-start = (bf16[32,16,128]{2,1,0:T(8,128)(2,1)S(1)}, bf16[32,16,128]{2,1,0:T(8,128)(2,1)S(1)}, u32[]{:S(2)}, u32[]{:S(2)}) collective-permute-start(bf16[32,16,128]{2,1,0:T(8,128)(2,1)S(1)} %get-tuple-element.14), channel_id=1, source_target_pairs={{0,256},{256,0},{1,257},{257,1},{2,258},{258,2},{3,259},{259,3},{4... | collective-permute-start | bytes 393224 | tf_op jit(solution)/shard_map/ppermute | solution.py:330
  33.2 1.0 collective-permute-done.other_ref
  34.1 18.1 %all-to-all-done.got_ref = bf16[32,48,128]{2,1,0:T(8,128)(2,1)S(1)} async-done(((bf16[32,48,128]{2,1,0:T(8,128)(2,1)}), bf16[32,48,128]{2,1,0:T(8,128)(2,1)S(1)}, u32[]{:S(2)}, u32[]{:S(2)}) %all-to-all-start) | async-done | bytes 393248 | tf_op jit(solution)/shard_map/all_to_all | solution.py:313
  52.3 0.0 copy-done.12
  52.3 2.8 %pair.1 = bf16[32,48,128]{2,1,0:T(8,128)(2,1)} custom-call(s32[2,32]{1,0:T(2,128)S(1)} %get-tuple-element.12.table_ref, bf16[32,48,128]{2,1,0:T(8,128)(2,1)S(1)} %all-to-all-done.got_ref, bf16[256,32]{1,0:T(8,128)(2,1)S(1)} %copy.27.taps_ref, f32[32,16,128]{2,1,0:T(8,128)S(1)} %get-tuple-element.13.keep_ref, ...), custom_call_target="tpu_custom_call" | custom-call | flops 1000000000 | bytes 1310720 | tf_op jit(solution)/shard_map/pair/pallas_call | solution.py:332
  55.1 5.8 %all-to-all-start.1 = ((bf16[32,48,128]{2,1,0:T(8,128)(2,1)}), bf16[32,48,128]{2,1,0:T(8,128)(2,1)S(1)}, u32[]{:S(2)}, u32[]{:S(2)}) async-start(bf16[32,48,128]{2,1,0:T(8,128)(2,1)} %pair.1), calls=%async_computation.1 | async-start | bytes 786432 | tf_op jit(solution)/shard_map/all_to_all | solution.py:342
  60.9 0.0 copy-start.10
  60.9 0.0 copy-start.11
  60.9 3.2 %collective-permute-start.1 = (bf16[32,16,128]{2,1,0:T(8,128)(2,1)S(1)}, bf16[32,16,128]{2,1,0:T(8,128)(2,1)S(1)}, u32[]{:S(2)}, u32[]{:S(2)}) collective-permute-start(bf16[32,16,128]{2,1,0:T(8,128)(2,1)S(1)} %slice.4.own_ref), channel_id=1, source_target_pairs={{0,256},{256,0},{1,257},{257,1},{2,258},{258,2},{3,259},{259,3},{4... | collective-permute-start | bytes 393224 | tf_op jit(solution)/shard_map/ppermute | solution.py:357
  64.2 1.7 %pair_taps.1.pair_ref = f32[32,256]{1,0:T(8,128)S(1)} custom-call(s32[2,32]{1,0:T(2,128)S(1)} %get-tuple-element.12.table_ref, bf16[32,48,128]{2,1,0:T(8,128)(2,1)S(1)} %all-to-all-done.got_ref, bf16[128,256]{1,0:T(8,128)(2,1)S(1)} %copy-done.23, bf16[128,256]{1,0:T(8,128)(2,1)S(1)} %copy-done.22, bf16[256,256]{1,0:T(8,128)(2,1)S(1)} %copy-done.11, ...), custom_call_target="tpu_custom_call" | custom-call | flops 1000000000 | bytes 786432 | tf_op jit(solution)/shard_map/pair_taps/pallas_call | solution.py:344
  65.8 0.0 copy-start.19
  65.8 0.0 copy-start.20
  65.9 0.0 copy-start.21
  65.9 2.1 %collective-permute-start.3 = (f32[32,256]{1,0:T(8,128)S(1)}, f32[32,256]{1,0:T(8,128)S(1)}, u32[]{:S(2)}, u32[]{:S(2)}) collective-permute-start(f32[32,256]{1,0:T(8,128)S(1)} %pair_taps.1.pair_ref), channel_id=1, source_target_pairs={{0,256},{256,0},{1,257},{257,1},{2,258},{258,2},{3,259},{259,3},{4... | collective-permute-start | bytes 98312 | tf_op jit(solution)/shard_map/ppermute | solution.py:354
  67.9 19.4 %all-to-all-done.1.got_ref = bf16[32,48,128]{2,1,0:T(8,128)(2,1)S(1)} async-done(((bf16[32,48,128]{2,1,0:T(8,128)(2,1)}), bf16[32,48,128]{2,1,0:T(8,128)(2,1)S(1)}, u32[]{:S(2)}, u32[]{:S(2)}) %all-to-all-start.1) | async-done | bytes 393248 | tf_op jit(solution)/shard_map/all_to_all | solution.py:342
  87.4 4.9 %collective-permute-start.2 = (f32[16,128]{1,0:T(8,128)S(1)}, f32[16,128]{1,0:T(8,128)S(1)}, u32[]{:S(2)}, u32[]{:S(2)}) collective-permute-start(f32[16,128]{1,0:T(8,128)S(1)} %tap_sum.1.own_ref), channel_id=1, source_target_pairs={{0,256},{256,0},{1,257},{257,1},{2,258},{258,2},{3,259},{259,3},{4... | collective-permute-start | bytes 24584 | tf_op jit(solution)/shard_map/ppermute | solution.py:379
  92.3 0.0 collective-permute-done.1.other_ref
  92.4 4.0 %local.1 = (f32[128,1024]{1,0:T(8,128)S(1)}, f32[128,1024]{1,0:T(8,128)S(1)}) custom-call(bf16[32,16,128]{2,1,0:T(8,128)(2,1)S(1)} %slice.4.own_ref, bf16[32,16,128]{2,1,0:T(8,128)(2,1)S(1)} %collective-permute-done.1.other_ref, bf16[128,1024]{1,0:T(8,128)(2,1)S(1)} %copy-done.7, bf16[128,1024]{1,0:T(8,128)(2,1)S(1)} %copy-done.1, ...), custom_call_target="tpu_custom_call" | custom-call | flops 3000000000 | bytes 2621440 | tf_op jit(solution)/shard_map/local/pallas_call | solution.py:358
  96.3 3.1 %finish.1 = (bf16[128,1024]{1,0:T(8,128)(2,1)}, bf16[128,1024]{1,0:T(8,128)(2,1)}, bf16[128,1024]{1,0:T(8,128)(2,1)}) custom-call(s32[1,32]{1,0:T(1,128)S(1)} %copy-done.8, s32[1,24]{1,0:T(1,128)S(1)} %copy-done.9, bf16[32,48,128]{2,1,0:T(8,128)(2,1)S(1)} %all-to-all-done.1.got_ref, f32[128,1024]{1,0:T(8,128)S(1)} %get-tuple-element.15.mixed_ref, ...), custom_call_target="tpu_custom_call" | custom-call | flops 1310720 | bytes 3145728 | tf_op jit(solution)/shard_map/finish/pallas_call | solution.py:381
  99.5 0.0 collective-permute-done.3.pair_other_ref
  99.5 0.0 collective-permute-done.2.other_ref
  99.5 0.2 taps_out.1
  99.6 0.7 copy.29
  (27 shorter events, 0.1 us)
Async XLA Ops:
  0.6 0.9 copy-start.9
  0.6 0.9 copy-start.8
  1.5 1.0 copy-start
  2.5 0.9 copy-start.2
  3.4 0.9 copy-start.4
  4.4 0.9 copy-start.6
  5.3 20.4 %copy-start.7 = (bf16[128,1024]{1,0:T(8,128)(2,1)S(1)}, bf16[128,1024]{1,0:T(8,128)(2,1)}, u32[]{:S(2)}) copy-start(bf16[128,1024]{1,0:T(8,128)(2,1)} %q_ref.5) | copy-start | bytes 786436
  5.3 20.4 %copy-start.14 = (bf16[128,256]{1,0:T(8,128)(2,1)S(1)}, bf16[128,256]{1,0:T(8,128)(2,1)}, u32[]{:S(2)}) copy-start(bf16[128,256]{1,0:T(8,128)(2,1)} %constant.37.clone.inv_lo) | copy-start | bytes 196612
  5.3 20.5 %copy-start.15 = (bf16[128,256]{1,0:T(8,128)(2,1)S(1)}, bf16[128,256]{1,0:T(8,128)(2,1)}, u32[]{:S(2)}) copy-start(bf16[128,256]{1,0:T(8,128)(2,1)} %constant.36.clone.inv_hi) | copy-start | bytes 196612
  5.3 20.5 %copy-start.16 = (bf16[256,128]{1,0:T(8,128)(2,1)S(1)}, bf16[256,128]{1,0:T(8,128)(2,1)}, u32[]{:S(2)}) copy-start(bf16[256,128]{1,0:T(8,128)(2,1)} %constant.33.clone.fwd_lo) | copy-start | bytes 196612
  5.3 20.5 %copy-start.17 = (bf16[256,128]{1,0:T(8,128)(2,1)S(1)}, bf16[256,128]{1,0:T(8,128)(2,1)}, u32[]{:S(2)}) copy-start(bf16[256,128]{1,0:T(8,128)(2,1)} %constant.32.clone.fwd_hi) | copy-start | bytes 196612
  7.1 18.7 %copy-start.1 = (bf16[128,1024]{1,0:T(8,128)(2,1)S(1)}, bf16[128,1024]{1,0:T(8,128)(2,1)}, u32[]{:S(2)}) copy-start(bf16[128,1024]{1,0:T(8,128)(2,1)} %k_ref.7) | copy-start | bytes 786436
  7.1 18.7 %copy-start.3 = (bf16[128,1024]{1,0:T(8,128)(2,1)S(1)}, bf16[128,1024]{1,0:T(8,128)(2,1)}, u32[]{:S(2)}) copy-start(bf16[128,1024]{1,0:T(8,128)(2,1)} %v_ref.7) | copy-start | bytes 786436
  7.1 18.7 %copy-start.5 = (bf16[128,1024]{1,0:T(8,128)(2,1)S(1)}, bf16[128,1024]{1,0:T(8,128)(2,1)}, u32[]{:S(2)}) copy-start(bf16[128,1024]{1,0:T(8,128)(2,1)} %c_ref.7) | copy-start | bytes 786436
  7.1 45.2 %all-to-all-start = ((bf16[32,48,128]{2,1,0:T(8,128)(2,1)}), bf16[32,48,128]{2,1,0:T(8,128)(2,1)S(1)}, u32[]{:S(2)}, u32[]{:S(2)}) async-start(bf16[32,48,128]{2,1,0:T(8,128)(2,1)} %send.1), calls=%async_computation | async-start | bytes 786432 | tf_op jit(solution)/shard_map/all_to_all | solution.py:313
  25.8 26.5 %copy-start.12 = (bf16[256,256]{1,0:T(8,128)(2,1)S(1)}, bf16[256,256]{1,0:T(8,128)(2,1)}, u32[]{:S(2)}) copy-start(bf16[256,256]{1,0:T(8,128)(2,1)} %constant.41.clone.tap_lo) | copy-start | bytes 393220
  25.9 26.4 %copy-start.13 = (bf16[256,256]{1,0:T(8,128)(2,1)S(1)}, bf16[256,256]{1,0:T(8,128)(2,1)}, u32[]{:S(2)}) copy-start(bf16[256,256]{1,0:T(8,128)(2,1)} %constant.40.clone.tap_hi) | copy-start | bytes 393220
  25.9 26.4 %copy-start.22 = (bf16[128,256]{1,0:T(8,128)(2,1)S(1)}, bf16[128,256]{1,0:T(8,128)(2,1)}, u32[]{:S(2)}) copy-start(bf16[128,256]{1,0:T(8,128)(2,1)} %constant.35.clone.fwd_lo) | copy-start | bytes 196612
  25.9 26.4 %copy-start.23 = (bf16[128,256]{1,0:T(8,128)(2,1)S(1)}, bf16[128,256]{1,0:T(8,128)(2,1)}, u32[]{:S(2)}) copy-start(bf16[128,256]{1,0:T(8,128)(2,1)} %constant.34.clone.fwd_hi) | copy-start | bytes 196612
  25.9 26.4 %copy-start.24 = (bf16[256,128]{1,0:T(8,128)(2,1)S(1)}, bf16[256,128]{1,0:T(8,128)(2,1)}, u32[]{:S(2)}) copy-start(bf16[256,128]{1,0:T(8,128)(2,1)} %constant.39.clone.inv_lo) | copy-start | bytes 196612
  25.9 26.4 %copy-start.25 = (bf16[256,128]{1,0:T(8,128)(2,1)S(1)}, bf16[256,128]{1,0:T(8,128)(2,1)}, u32[]{:S(2)}) copy-start(bf16[256,128]{1,0:T(8,128)(2,1)} %constant.38.clone.inv_hi) | copy-start | bytes 196612
  30.3 3.8 %collective-permute-start = (bf16[32,16,128]{2,1,0:T(8,128)(2,1)S(1)}, bf16[32,16,128]{2,1,0:T(8,128)(2,1)S(1)}, u32[]{:S(2)}, u32[]{:S(2)}) collective-permute-start(bf16[32,16,128]{2,1,0:T(8,128)(2,1)S(1)} %get-tuple-element.14), channel_id=1, source_target_pairs={{0,256},{256,0},{1,257},{257,1},{2,258},{258,2},{3,259},{259,3},{4... | collective-permute-start | bytes 393224 | tf_op jit(solution)/shard_map/ppermute | solution.py:330
  55.1 32.3 %all-to-all-start.1 = ((bf16[32,48,128]{2,1,0:T(8,128)(2,1)}), bf16[32,48,128]{2,1,0:T(8,128)(2,1)S(1)}, u32[]{:S(2)}, u32[]{:S(2)}) async-start(bf16[32,48,128]{2,1,0:T(8,128)(2,1)} %pair.1), calls=%async_computation.1 | async-start | bytes 786432 | tf_op jit(solution)/shard_map/all_to_all | solution.py:342
  60.9 3.2 %copy-start.10 = (bf16[256,256]{1,0:T(8,128)(2,1)S(1)}, bf16[256,256]{1,0:T(8,128)(2,1)}, u32[]{:S(2)}) copy-start(bf16[256,256]{1,0:T(8,128)(2,1)} %constant.43.clone.lag_lo) | copy-start | bytes 393220
  60.9 3.2 %copy-start.11 = (bf16[256,256]{1,0:T(8,128)(2,1)S(1)}, bf16[256,256]{1,0:T(8,128)(2,1)}, u32[]{:S(2)}) copy-start(bf16[256,256]{1,0:T(8,128)(2,1)} %constant.42.clone.lag_hi) | copy-start | bytes 393220
  60.9 31.4 %collective-permute-start.1 = (bf16[32,16,128]{2,1,0:T(8,128)(2,1)S(1)}, bf16[32,16,128]{2,1,0:T(8,128)(2,1)S(1)}, u32[]{:S(2)}, u32[]{:S(2)}) collective-permute-start(bf16[32,16,128]{2,1,0:T(8,128)(2,1)S(1)} %slice.4.own_ref), channel_id=1, source_target_pairs={{0,256},{256,0},{1,257},{257,1},{2,258},{258,2},{3,259},{259,3},{4... | collective-permute-start | bytes 393224 | tf_op jit(solution)/shard_map/ppermute | solution.py:357
  65.8 26.5 %copy-start.18 = (bf16[256,128]{1,0:T(8,128)(2,1)S(1)}, bf16[256,128]{1,0:T(8,128)(2,1)}, u32[]{:S(2)}) copy-start(bf16[256,128]{1,0:T(8,128)(2,1)} %constant.47.clone.second_lo) | copy-start | bytes 196612
  65.8 26.5 %copy-start.19 = (bf16[256,128]{1,0:T(8,128)(2,1)S(1)}, bf16[256,128]{1,0:T(8,128)(2,1)}, u32[]{:S(2)}) copy-start(bf16[256,128]{1,0:T(8,128)(2,1)} %constant.46.clone.second_hi) | copy-start | bytes 196612
  65.8 26.5 %copy-start.20 = (bf16[256,128]{1,0:T(8,128)(2,1)S(1)}, bf16[256,128]{1,0:T(8,128)(2,1)}, u32[]{:S(2)}) copy-start(bf16[256,128]{1,0:T(8,128)(2,1)} %constant.45.clone.first_lo) | copy-start | bytes 196612
  65.9 26.5 %copy-start.21 = (bf16[256,128]{1,0:T(8,128)(2,1)S(1)}, bf16[256,128]{1,0:T(8,128)(2,1)}, u32[]{:S(2)}) copy-start(bf16[256,128]{1,0:T(8,128)(2,1)} %constant.44.clone.first_hi) | copy-start | bytes 196612
  65.9 33.6 %collective-permute-start.3 = (f32[32,256]{1,0:T(8,128)S(1)}, f32[32,256]{1,0:T(8,128)S(1)}, u32[]{:S(2)}, u32[]{:S(2)}) collective-permute-start(f32[32,256]{1,0:T(8,128)S(1)} %pair_taps.1.pair_ref), channel_id=1, source_target_pairs={{0,256},{256,0},{1,257},{257,1},{2,258},{258,2},{3,259},{259,3},{4... | collective-permute-start | bytes 98312 | tf_op jit(solution)/shard_map/ppermute | solution.py:354
  87.4 12.0 %collective-permute-start.2 = (f32[16,128]{1,0:T(8,128)S(1)}, f32[16,128]{1,0:T(8,128)S(1)}, u32[]{:S(2)}, u32[]{:S(2)}) collective-permute-start(f32[16,128]{1,0:T(8,128)S(1)} %tap_sum.1.own_ref), channel_id=1, source_target_pairs={{0,256},{256,0},{1,257},{257,1},{2,258},{258,2},{3,259},{259,3},{4... | collective-permute-start | bytes 24584 | tf_op jit(solution)/shard_map/ppermute | solution.py:379

commit v2 on v1

v2 whole, which is shorter than its diff:
```python
import functools

import jax
import jax.numpy as jnp
import numpy as np
from jax import lax
from jax.experimental import pallas as pl
from jax.experimental.pallas import tpu as pltpu
from jax.sharding import PartitionSpec as P

SPAN = 128
PTS = 2 * SPAN
QUARTER = SPAN // 4
F32, BF16 = jnp.float32, jnp.bfloat16


def split_bf16(matrix):
    high = matrix.astype(BF16)
    low = (matrix - high.astype(np.float64)).astype(BF16)
    return high, low


def transforms():
    freq = np.arange(SPAN)[:, None]
    point = np.arange(PTS)[None, :]
    angle = 2 * np.pi * ((freq * point) % PTS) / PTS
    real, imag = np.cos(angle), -np.sin(angle)
    imag[0] = np.where(np.arange(PTS) % 2 == 0, 1.0, -1.0)
    forward = np.concatenate([real, imag], 0)
    weight = np.full((PTS, 1), 2.0 / PTS)
    weight[0], weight[SPAN] = 1.0 / PTS, 1.0 / PTS
    inverse = (forward * weight).T
    return forward, inverse


def dot(a, b, dims=((1,), (0,))):
    return lax.dot_general(a, b, (dims, ((), ())), preferred_element_type=F32)


def halves(x):
    high = x.astype(BF16)
    return high, (x - high.astype(F32)).astype(BF16)


def spectrum_left(high, low, x):
    return dot(high, x) + dot(low, x)


def spectrum_right(x, high, low):
    return dot(x, high) + dot(x, low)


def invert_left(high, low, spec):
    s_high, s_low = halves(spec)
    return dot(high, s_high) + (dot(high, s_low) + dot(low, s_high))


def invert_right(spec, high, low):
    s_high, s_low = halves(spec)
    return dot(s_high, high) + (dot(s_low, high) + dot(s_high, low))


def multiply(ar, ai, br, bi, zero, sign):
    b_im = sign * jnp.where(zero, 0.0, bi)
    b_second = jnp.where(zero, bi, br)
    return ar * br - ai * b_im, ai * b_second + ar * b_im


def swap_blocks(parts):
    axis = parts[0].ndim - 1
    block = lax.broadcasted_iota(jnp.int32, parts[0].shape, axis) // QUARTER
    result = []
    for t in range(4):
        total = parts[t]
        for b in range(4):
            if b != t:
                moved = pltpu.roll(parts[b], (QUARTER * (b - t)) % SPAN, axis)
                total = jnp.where(block == b, moved, total)
        result.append(total)
    return result


def own_kind(slot_ref, len_ref):
    span = slot_ref[0, lax.axis_index("ctx")]

    def step(d, carry):
        pos, kind = carry
        length = len_ref[0, d]
        two = length == 2
        kind = jnp.where(two & (span == pos), 1, kind)
        kind = jnp.where(two & (span == pos + 1), 2, kind)
        return pos + length, kind

    zero = jnp.int32(0)
    return lax.fori_loop(0, len_ref.shape[1], step, (zero, zero))[1]


def send_kernel(
    slot_hbm, len_hbm, taps_hbm, q_hbm, k_hbm, v_hbm, c_hbm, out_hbm,
    slot_ref, len_ref, taps_ref, q_buf, k_buf, v_buf, c_buf, out_buf,
    small_sem, in_sem, out_sem,
):
    chunks = out_sem.shape[0]
    width = q_buf.shape[1] // chunks
    count = out_buf.shape[0] // chunks
    small = [
        pltpu.make_async_copy(src, dst, small_sem.at[i])
        for i, (src, dst) in enumerate(
            ((slot_hbm, slot_ref), (len_hbm, len_ref), (taps_hbm, taps_ref))
        )
    ]
    small[0].start()
    small[1].start()
    wide = []
    for j in range(chunks):
        cols = pl.ds(j * width, width)
        wide.append([
            pltpu.make_async_copy(src.at[:, cols], dst.at[:, cols], in_sem.at[i, j])
            for i, (src, dst) in enumerate(
                ((k_hbm, k_buf), (v_hbm, v_buf), (c_hbm, c_buf), (q_hbm, q_buf))
            )
        ])
        for copy in wide[-1]:
            copy.start()
        if j == 0:
            small[2].start()
    small[0].wait()
    small[1].wait()
    first = own_kind(slot_ref, len_ref) == 1
    small[2].wait()
    taps = taps_ref[:, 0:SPAN].astype(F32)
    quarters = swap_blocks([taps[8 * b:8 * b + 8] for b in range(4)])
    core = lax.axis_index("dp") == 0
    outs = []
    for j in range(chunks):
        for copy in wide[j]:
            copy.wait()
        cols = slice(j * width, (j + 1) * width)
        rows = slice(j * count, (j + 1) * count)
        a = jnp.where(first, k_buf[:, cols].astype(F32), c_buf[:, cols].astype(F32))
        b = jnp.where(first, v_buf[:, cols].astype(F32), q_buf[:, cols].astype(F32))
        out_buf[rows, 0:32, :] = jnp.transpose((a * b).astype(BF16)).reshape(count, 32, SPAN)
        far = int(2 * j >= chunks)
        mine = jnp.where(core, quarters[far], quarters[2 + far]).astype(BF16)
        out_buf[rows, 32:40, :] = jnp.broadcast_to(mine[None], (count, 8, SPAN))
        out = pltpu.make_async_copy(out_buf.at[rows], out_hbm.at[rows], out_sem.at[j])
        out.start()
        outs.append(out)
    for out in outs:
        out.wait()


def partial_kernel(
    slot_ref, len_ref, q_ref, k_ref, v_ref, c_ref, fwd_hi, fwd_lo, inv_hi, inv_lo,
    keep_ref, give_ref, table_ref, inverse_ref,
):
    @pl.when(pl.program_id(0) == 0)
    def _():
        slots = slot_ref.shape[1]

        def fill(r, carry):
            inverse_ref[slot_ref[0, r]] = r
            return carry

        lax.fori_loop(0, slots, fill, 0)

        def step(d, carry):
            pos, count = carry
            length = len_ref[0, d]

            @pl.when(length == 2)
            def _():
                table_ref[0, count] = inverse_ref[pos]
                table_ref[1, count] = inverse_ref[pos + 1]

            return pos + length, count + length - 1

        lax.fori_loop(0, len_ref.shape[1], step, (jnp.int32(0), jnp.int32(0)))
        table_ref[2, 0] = own_kind(slot_ref, len_ref)

    x = (k_ref[...].astype(F32) * v_ref[...].astype(F32)).astype(BF16)
    g = (c_ref[...].astype(F32) * q_ref[...].astype(F32)).astype(BF16)
    xs = spectrum_left(fwd_hi[...], fwd_lo[...], x)
    gs = spectrum_left(fwd_hi[...], fwd_lo[...], g)
    zero = lax.broadcasted_iota(jnp.int32, (SPAN, x.shape[1]), 0) == 0
    pr, pi = multiply(gs[:SPAN], gs[SPAN:], xs[:SPAN], xs[SPAN:], zero, -1.0)
    taps = invert_left(inv_hi[...], inv_lo[...], jnp.concatenate([pr, pi], 0))
    count = x.shape[1] // 32
    rows = jnp.transpose(taps).reshape(count, 4, 8, SPAN)
    quarters = swap_blocks([rows[:, b] for b in range(4)])
    core = lax.axis_index("dp") == 0
    for t in range(2):
        low = quarters[t].reshape(count * 8, SPAN)
        high = quarters[2 + t].reshape(count * 8, SPAN)
        keep_ref[t] = jnp.where(core, low, high)
        give_ref[t] = jnp.where(core, high, low).astype(BF16)


def halve_kernel(own_ref, other_ref, keep_ref, give_ref):
    far = lax.axis_index("ctx") // 16 == 1
    low = own_ref[0] + other_ref[0].astype(F32)
    high = own_ref[1] + other_ref[1].astype(F32)
    keep_ref[...] = jnp.where(far, high, low)
    give_ref[...] = jnp.where(far, low, high).astype(BF16)


def pair_spectra(table_ref, got_ref, fwd_hi, fwd_lo):
    pairs = table_ref.shape[1]
    rows = [got_ref[table_ref[k, p], 0:32, :] for k in range(2) for p in range(pairs)]
    spec = spectrum_right(jnp.concatenate(rows, 0), fwd_hi[...], fwd_lo[...])
    return spec.reshape(2, pairs, 32, PTS)


def pair_kernel(
    table_ref, got_ref, taps_ref, keep_ref, other_ref, fwd_hi, fwd_lo, inv_hi, inv_lo,
    tap_hi, tap_lo, out_ref,
):
    slots, pairs = got_ref.shape[0], table_ref.shape[1]
    hs = spectrum_right(taps_ref[...], tap_hi[...], tap_lo[...])
    hr, hi = hs[:, :SPAN], hs[:, SPAN:]
    zero = lax.broadcasted_iota(jnp.int32, hr.shape, 1) == 0
    spec = pair_spectra(table_ref, got_ref, fwd_hi, fwd_lo)
    out_ref[:, 0:32, :] = jnp.zeros((slots, 32, SPAN), BF16)
    for k in range(2):
        sr, si = spec[k, :, :, :SPAN], spec[k, :, :, SPAN:]
        pr, pi = multiply(sr, si, hr[None], hi[None], zero[None], 1.0 if k == 0 else -1.0)
        both = jnp.concatenate([pr, pi], 2).reshape(pairs * 32, PTS)
        result = invert_right(both, inv_hi[...], inv_lo[...]).astype(BF16)
        for p in range(pairs):
            out_ref[table_ref[1 - k, p], 0:32, :] = result[32 * p:32 * p + 32]
    near = (keep_ref[...] + other_ref[...].astype(F32)).astype(BF16)
    out_ref[:, 32:40, :] = near.reshape(slots, 8, SPAN)


def pair_taps_kernel(table_ref, got_ref, fwd_hi, fwd_lo, lag_hi, lag_lo, out_ref):
    spec = pair_spectra(table_ref, got_ref, fwd_hi, fwd_lo)
    zero = lax.broadcasted_iota(jnp.int32, (1, 32, SPAN), 2) == 0
    xs, gs = spec[0], spec[1]
    tr, ti = multiply(
        gs[:, :, :SPAN], gs[:, :, SPAN:], xs[:, :, :SPAN], xs[:, :, SPAN:], zero, -1.0
    )
    both = jnp.concatenate([jnp.sum(tr, 0), jnp.sum(ti, 0)], 1)
    out_ref[...] = invert_right(both, lag_hi[...], lag_lo[...])


def local_kernel(
    own_ref, side_ref, core_ref, core_side_ref, q_ref, k_ref, v_ref, c_ref,
    fwd_hi, fwd_lo, inv_hi, inv_lo, taps_hi, taps_lo, mixed_ref, series_ref,
):
    x = (k_ref[...].astype(F32) * v_ref[...].astype(F32)).astype(BF16)
    g = (c_ref[...].astype(F32) * q_ref[...].astype(F32)).astype(BF16)
    xs = spectrum_left(fwd_hi[...], fwd_lo[...], x)
    gs = spectrum_left(fwd_hi[...], fwd_lo[...], g)
    count = own_ref.shape[0] // 8
    dp, far = lax.axis_index("dp"), lax.axis_index("ctx") // 16
    own, side = own_ref[...].astype(F32), side_ref[...].astype(F32)
    core, core_side = core_ref[0].astype(F32), core_side_ref[0].astype(F32)
    quarters = []
    for t in range(4):
        same = jnp.where(far == t % 2, own, side)
        cross = jnp.where(far == t % 2, core, core_side)
        quarters.append(jnp.where(dp == t // 2, same, cross).reshape(count, 8, SPAN))
    taps = jnp.concatenate(swap_blocks(quarters), 1).reshape(count * 32, SPAN).astype(BF16)
    nt = ((1,), (1,))
    hs = dot(taps_hi[...], taps, nt) + dot(taps_lo[...], taps, nt)
    zero = lax.broadcasted_iota(jnp.int32, (SPAN, x.shape[1]), 0) == 0
    hr, hi = hs[:SPAN], hs[SPAN:]
    mr, mi = multiply(xs[:SPAN], xs[SPAN:], hr, hi, zero, 1.0)
    mixed_ref[...] = invert_left(inv_hi[...], inv_lo[...], jnp.concatenate([mr, mi], 0))
    sr, si = multiply(gs[:SPAN], gs[SPAN:], hr, hi, zero, -1.0)
    series_ref[...] = invert_left(inv_hi[...], inv_lo[...], jnp.concatenate([sr, si], 0))


def taps_kernel(got_ref, pair_ref, after_ref, out_ref):
    del after_ref
    slots = got_ref.shape[0]
    core = lax.axis_index("dp")
    sums = []
    for far in range(2):
        rows = got_ref[far * 16:far * 16 + 16, 32:40, :].astype(F32)
        sums.append(jnp.sum(rows, axis=0))
    quarters = [jnp.where(core == t // 2, sums[t % 2], 0.0) for t in range(4)]
    near = jnp.concatenate(swap_blocks(quarters), 0)
    out_ref[:, :SPAN] = pair_ref[:, :SPAN] + near
    out_ref[:, SPAN:] = pair_ref[:, SPAN:]


def finish_kernel(
    table_ref, got_ref, mixed_ref, series_ref, k_ref, v_ref, c_ref,
    gq_ref, gk_ref, gv_ref, q_buf, k_buf, v_buf, sems,
):
    chunks = sems.shape[1]
    width = q_buf.shape[1] // chunks
    count = got_ref.shape[0] // chunks
    kind = table_ref[2, 0]
    copies = []
    for j in range(chunks):
        cols = slice(j * width, (j + 1) * width)
        rows = got_ref[j * count:(j + 1) * count, 0:32, :].reshape(width, SPAN)
        pair = jnp.transpose(rows).astype(F32)
        mixed = mixed_ref[:, cols] + jnp.where(kind == 2, pair, 0.0)
        series = series_ref[:, cols] + jnp.where(kind == 1, pair, 0.0)
        mixed = mixed.astype(BF16).astype(F32)
        series = series.astype(BF16).astype(F32)
        q_buf[:, cols] = (c_ref[:, cols].astype(F32) * mixed).astype(BF16)
        k_buf[:, cols] = (series * v_ref[:, cols].astype(F32)).astype(BF16)
        v_buf[:, cols] = (series * k_ref[:, cols].astype(F32)).astype(BF16)
        for i, (buf, ref) in enumerate(((q_buf, gq_ref), (k_buf, gk_ref), (v_buf, gv_ref))):
            copy = pltpu.make_async_copy(buf.at[:, cols], ref.at[:, cols], sems.at[i, j])
            copy.start()
            copies.append(copy)
    for copy in copies:
        copy.wait()


def taps_out_kernel(scale, own_ref, other_ref, out_ref):
    out_ref[...] = ((own_ref[...] + other_ref[...]) * scale).astype(BF16)


SMEM = pl.BlockSpec(memory_space=pltpu.SMEM)
VMEM = pl.BlockSpec(memory_space=pltpu.VMEM)
HBM = pl.BlockSpec(memory_space=pltpu.HBM)
ANY = pl.BlockSpec(memory_space=pl.ANY)
DMA = pltpu.SemaphoreType.DMA


def params(mebibytes=32):
    return pltpu.CompilerParams(vmem_limit_bytes=mebibytes * 1024 * 1024)


def cost(flops, moved):
    return pl.CostEstimate(flops=int(flops), bytes_accessed=int(moved), transcendentals=0)


def per_device(query, key, value, cotangent, filter_taps, span_slot, doc_lengths):
    parts = lax.axis_size("ctx")
    tokens, width = query.shape
    area = tokens * width
    pairs = parts - doc_lengths.shape[1]
    scale = float(tokens * parts * lax.axis_size("dp")) ** (-0.5)
    forward, inverse = transforms()

    def constant(matrix):
        return [jnp.asarray(m) for m in split_bf16(matrix)]

    fwd = constant(forward[:, :SPAN])
    fwd_t = constant(forward[:, :SPAN].T)
    inv = constant(inverse[:SPAN])
    inv_t = constant(inverse[:SPAN].T)
    tap_t = constant(np.roll(forward, -SPAN, 1).T)
    lag_t = constant(np.roll(inverse, SPAN, 0).T)
    core_swap = [(0, 1), (1, 0)]
    side_swap = [(c, c ^ 16) for c in range(parts)]
    block = 256
    steps = width // block
    group = block // 32
    wide = pl.BlockSpec((tokens, block), lambda i: (0, i))
    taps_rows = filter_taps.T

    def whole(array):
        return pl.BlockSpec(array.shape, lambda i: (0,) * array.ndim)

    chunk = jax.ShapeDtypeStruct((parts, 40, SPAN), BF16)
    out = pl.pallas_call(
        send_kernel,
        out_shape=chunk,
        in_specs=[HBM] * 7,
        out_specs=HBM,
        scratch_shapes=[
            pltpu.SMEM(span_slot.shape, jnp.int32),
            pltpu.SMEM(doc_lengths.shape, jnp.int32),
            pltpu.VMEM(taps_rows.shape, BF16),
        ] + [pltpu.VMEM((tokens, width), BF16)] * 4 + [
            pltpu.VMEM(chunk.shape, BF16), DMA((3,)), DMA((4, steps)), DMA((steps,)),
        ],
        compiler_params=params(60),
        cost_estimate=cost(2 * area, 8 * area),
        name="send",
    )(span_slot, doc_lengths, taps_rows, query, key, value, cotangent)
    got = lax.all_to_all(out, "ctx", split_axis=0, concat_axis=0, tiled=True)

    two = pl.BlockSpec((2, group * 8, SPAN), lambda i: (0, i, 0))
    keep, give, table = pl.pallas_call(
        partial_kernel,
        grid=(steps,),
        out_shape=(
            jax.ShapeDtypeStruct((2, parts * 8, SPAN), F32),
            jax.ShapeDtypeStruct((2, parts * 8, SPAN), BF16),
            jax.ShapeDtypeStruct((3, pairs), jnp.int32),
        ),
        in_specs=[SMEM, SMEM] + [wide] * 4 + [whole(m) for m in fwd + inv],
        out_specs=(two, two, SMEM),
        scratch_shapes=[pltpu.SMEM((parts,), jnp.int32)],
        compiler_params=params(),
        cost_estimate=cost(2e9, 10 * area),
        name="partial_taps",
    )(span_slot, doc_lengths, query, key, value, cotangent, *fwd, *inv)
    taken = lax.ppermute(give, "dp", core_swap)

    keep, give = pl.pallas_call(
        halve_kernel,
        out_shape=(
            jax.ShapeDtypeStruct((parts * 8, SPAN), F32),
            jax.ShapeDtypeStruct((parts * 8, SPAN), BF16),
        ),
        in_specs=[VMEM, VMEM],
        out_specs=(VMEM, VMEM),
        compiler_params=params(),
        cost_estimate=cost(area, 3 * area),
        name="halve",
    )(keep, taken)
    near_other = lax.ppermute(give, "ctx", side_swap)

    back = pl.pallas_call(
        pair_kernel,
        out_shape=chunk,
        in_specs=[SMEM] + [VMEM] * 10,
        out_specs=VMEM,
        compiler_params=params(),
        cost_estimate=cost(1e9, 8 * area),
        name="pair",
    )(table, got, taps_rows, keep, near_other, *fwd_t, *inv_t, *tap_t)
    landed = lax.all_to_all(back, "ctx", split_axis=0, concat_axis=0, tiled=True)

    own = got[:, 32:40, :].reshape(parts * 8, SPAN)
    side = lax.ppermute(own, "ctx", side_swap)
    core = lax.ppermute(jnp.stack([own, side]), "dp", core_swap)
    quarter = pl.BlockSpec((group * 8, SPAN), lambda i: (i, 0))
    mixed, series = pl.pallas_call(
        local_kernel,
        grid=(steps,),
        out_shape=(jax.ShapeDtypeStruct((tokens, width), F32),) * 2,
        in_specs=[
            quarter, quarter,
            pl.BlockSpec((1, group * 8, SPAN), lambda i: (0, i, 0)),
            pl.BlockSpec((1, group * 8, SPAN), lambda i: (1, i, 0)),
        ] + [wide] * 4 + [whole(m) for m in fwd + inv + fwd],
        out_specs=(wide, wide),
        compiler_params=params(),
        cost_estimate=cost(3e9, 20 * area),
        name="local",
    )(own, side, core, core, query, key, value, cotangent, *fwd, *inv, *fwd)

    pair_taps = pl.pallas_call(
        pair_taps_kernel,
        out_shape=jax.ShapeDtypeStruct((32, PTS), F32),
        in_specs=[SMEM] + [VMEM] * 5,
        out_specs=VMEM,
        compiler_params=params(),
        cost_estimate=cost(1e9, 6 * area),
        name="pair_taps",
    )(table, got, *fwd_t, *lag_t)
    taps_own = pl.pallas_call(
        taps_kernel,
        out_shape=jax.ShapeDtypeStruct((32, PTS), F32),
        in_specs=[VMEM, VMEM, ANY],
        out_specs=VMEM,
        compiler_params=params(),
        cost_estimate=cost(area, area),
        name="taps",
    )(landed, pair_taps, mixed)
    taps_other = lax.ppermute(taps_own, "dp", core_swap)

    result = jax.ShapeDtypeStruct((tokens, width), BF16)
    grads = pl.pallas_call(
        finish_kernel,
        out_shape=(result,) * 3,
        in_specs=[SMEM] + [VMEM] * 6,
        out_specs=(HBM,) * 3,
        scratch_shapes=[pltpu.VMEM((tokens, width), BF16)] * 3 + [DMA((3, steps))],
        compiler_params=params(),
        cost_estimate=cost(10 * area, 20 * area),
        name="finish",
    )(table, landed, mixed, series, key, value, cotangent)
    grad_filter = pl.pallas_call(
        functools.partial(taps_out_kernel, scale),
        out_shape=jax.ShapeDtypeStruct((32, PTS), BF16),
        in_specs=[VMEM] * 2,
        out_specs=VMEM,
        compiler_params=params(),
        name="taps_out",
    )(taps_own, taps_other)
    return (*grads, grad_filter.T)


def solution(mesh):
    return jax.shard_map(
        per_device,
        mesh=mesh,
        in_specs=(
            P(("dp", "ctx"), "ch"),
            P(("dp", "ctx"), "ch"),
            P(("dp", "ctx"), "ch"),
            P(("dp", "ctx"), "ch"),
            P(None, ("ch", "ctx")),
            P("dp", None),
            P("dp", None),
        ),
        out_specs=(
            P(("dp", "ctx"), "ch"),
            P(("dp", "ctx"), "ch"),
            P(("dp", "ctx"), "ch"),
            P(None, ("ch", "ctx")),
        ),
        check_vma=False,
    )
```

time: 101 us -> 86.7 us (0.86)
  waiting for transfers between devices: 38.5 us -> 19.3 us
  starting transfers between devices: 37.4 us -> 48.6 us
  local copies, waits for them, and re-layouts: 5.47 us -> 0.11 us
    all_to_all x1, waiting for transfers between devices: 19.4 us -> 6.58 us  [per_device(): lax.all_to_all(back, 'ctx', split_axis=0, concat_axis=0, tiled=True)]
    all_to_all x1, waiting for transfers between devices: 18.1 us -> 7.46 us  [per_device(): got = lax.all_to_all(out, 'ctx', split_axis=0, concat_axis=0, tiled=True)]
    ppermute x4 -> x5, starting transfers between devices: 13 us -> 23.5 us  [the longest x1 6.28 us: per_device(): taps_other = lax.ppermute(taps_own, 'dp', core_swap)]
    unnamed x54 -> x38, local copies, waits for them, and re-layouts: 5.46 us -> 0.1 us
    ppermute x4 -> x5, waiting for transfers between devices: 0.97 us -> 5.26 us  [the longest x1 2.32 us: per_device(): side = lax.ppermute(own, 'ctx', side_swap)]
    pallas_call x4 -> x5, Pallas kernels: 7.68 us -> 6.38 us  [the longest x1 2.49 us: per_device(): pl.pallas_call(send_kernel, out_shape=chunk, in_specs=[HBM] * 7, out_spec...]
    pallas_call x1, Pallas kernels: 4.39 us -> 5.47 us  [per_device(): pl.pallas_call(partial_kernel, grid=(steps,), out_shape=(jax.ShapeDtypeSt...]
  transfers between devices with their start and end apart: 6 -> 7, of which waited for: 3 -> 5; matrix products, arithmetic and copies ran while one was open for 0% -> 0% of each run, Pallas kernels for 13% -> 14%
where the time goes in v2:
time: 86.7 us; the launch traced here: 86.2 us
  starting transfers between devices  48.6 us (56%)
  waiting for transfers between devices  19.3 us (22%)
  Pallas kernels  17.2 us (20%)
  between operations  0.99 us (1%)
    all_to_all x1, starting transfers between devices, per_device(): got = lax.all_to_all(out, 'ctx', split_axis=0, concat_axis=0, tiled=True)  18.6 us
    all_to_all x1, waiting for transfers between devices, per_device(): got = lax.all_to_all(out, 'ctx', split_axis=0, concat_axis=0, tiled=True)  7.46 us
    all_to_all x1, waiting for transfers between devices, per_device(): lax.all_to_all(back, 'ctx', split_axis=0, concat_axis=0, tiled=True)  6.58 us
    all_to_all x1, starting transfers between devices, per_device(): lax.all_to_all(back, 'ctx', split_axis=0, concat_axis=0, tiled=True)  6.5 us
    ppermute x1, starting transfers between devices, per_device(): taps_other = lax.ppermute(taps_own, 'dp', core_swap)  6.28 us
    pallas_call x1, Pallas kernels, per_device(): pl.pallas_call(partial_kernel, grid=(steps,), out_shape=(jax.ShapeDtypeSt...  5.47 us
    ppermute x1, starting transfers between devices, per_device(): near_other = lax.ppermute(give, 'ctx', side_swap)  5.06 us
    ppermute x1, starting transfers between devices, per_device(): side = lax.ppermute(own, 'ctx', side_swap)  4.65 us
  transfers between devices with their start and end apart: 7, of which 5 were waited for; matrix products, arithmetic and copies ran while one was open for 0% of the time, Pallas kernels for 14%

profile of v2, /device:TPU:1, one launch (start us, length us, event | category | flops | bytes accessed | tf_op | source)
XLA Modules:
  0.0 86.2 jit_solution(3739410134903908165)
XLA Ops:
  0.6 0.0 copy-start.2
  0.6 0.0 copy-start.3
  0.7 0.0 copy-start.12
  0.7 0.0 copy-start.13
  0.7 0.0 copy-start.14
  0.7 2.5 %send.1 = bf16[32,40,128]{2,1,0:T(8,128)(2,1)} custom-call(s32[1,32]{1,0:T(1,128)} %slot_hbm.1, s32[1,24]{1,0:T(1,128)} %len_hbm.1, bf16[32,256]{1,0:T(8,128)(2,1)} %bitcast.8, bf16[128,1024]{1,0:T(8,128)(2,1)} %q_ref.3, bf16[128,1024]{1,0:T(8,128)(2,1)} %k_ref.5, bf16[128,1024]{1,0:T(8,128)(2,1)} %v_ref.5, bf16[128,1024]{1,0:T(8,128)(2,1)} %c_ref.5), custom_call_target="tpu_custom_call" | custom-call | flops 262144 | bytes 1048576 | tf_op jit(solution)/shard_map/send/pallas_call | solution.py:364
  3.2 0.0 copy-start
  3.2 0.0 copy-start.1
  3.2 0.0 copy-start.5
  3.2 0.0 copy-start.6
  3.2 0.0 copy-start.11
  3.2 18.6 %all-to-all-start = ((bf16[32,40,128]{2,1,0:T(8,128)(2,1)}), bf16[32,40,128]{2,1,0:T(8,128)(2,1)S(1)}, u32[]{:S(2)}, u32[]{:S(2)}) async-start(bf16[32,40,128]{2,1,0:T(8,128)(2,1)} %send.1), calls=%async_computation | async-start | bytes 655360 | tf_op jit(solution)/shard_map/all_to_all | solution.py:380
  21.9 0.0 copy-done.2
  21.9 0.0 copy-done.3
  21.9 0.0 copy-done.12
  21.9 0.0 copy-done.13
  21.9 0.0 copy-done.14
  21.9 0.0 copy-done
  21.9 0.0 copy-done.1
  22.0 0.0 copy-done.5
  22.0 0.0 copy-done.6
  22.0 0.0 copy-start.16
  22.0 0.0 copy-start.17
  22.0 0.0 copy-start.18
  22.0 5.5 %partial_taps.1 = (f32[2,256,128]{2,1,0:T(8,128)S(1)}, bf16[2,256,128]{2,1,0:T(8,128)(2,1)S(1)}, s32[3,8]{1,0:T(4,128)S(1)}) custom-call(s32[1,32]{1,0:T(1,128)S(1)} %copy-done.5, s32[1,24]{1,0:T(1,128)S(1)} %copy-done.6, bf16[128,1024]{1,0:T(8,128)(2,1)S(1)} %copy-done.3, bf16[128,1024]{1,0:T(8,128)(2,1)S(1)} %copy-done, bf16[128,1024]{1,0:T(8,128)(2,1)S(1)} %copy-done.1, ...), custom_call_target="tpu_custom_call" | custom-call | flops 2000000000 | bytes 1310720 | tf_op jit(solution)/shard_map/partial_taps/pallas_call | solution.py:383
  27.5 2.9 %collective-permute-start = (bf16[2,256,128]{2,1,0:T(8,128)(2,1)S(1)}, bf16[2,256,128]{2,1,0:T(8,128)(2,1)S(1)}, u32[]{:S(2)}, u32[]{:S(2)}) collective-permute-start(bf16[2,256,128]{2,1,0:T(8,128)(2,1)S(1)} %get-tuple-element.16), channel_id=1, source_target_pairs={{0,256},{256,0},{1,257},{257,1},{2,258},{258,2},{3,259},{259,3},{4... | collective-permute-start | bytes 393224 | tf_op jit(solution)/shard_map/ppermute | solution.py:398
  30.4 1.0 %collective-permute-done.other_ref = bf16[2,256,128]{2,1,0:T(8,128)(2,1)S(1)} collective-permute-done((bf16[2,256,128]{2,1,0:T(8,128)(2,1)S(1)}, bf16[2,256,128]{2,1,0:T(8,128)(2,1)S(1)}, u32[]{:S(2)}, u32[]{:S(2)}) %collective-permute-start) | collective-permute-done | bytes 131104 | tf_op jit(solution)/shard_map/ppermute | solution.py:398
  31.4 5.1 %collective-permute-start.1 = (bf16[256,128]{1,0:T(8,128)(2,1)S(1)}, bf16[256,128]{1,0:T(8,128)(2,1)S(1)}, u32[]{:S(2)}, u32[]{:S(2)}) collective-permute-start(bf16[256,128]{1,0:T(8,128)(2,1)S(1)} %get-tuple-element.18), channel_id=1, source_target_pairs={{0,128},{8,136},{16,144},{24,152},{32,160},{40,168},{48,176},{56,1... | collective-permute-start | bytes 196616 | tf_op jit(solution)/shard_map/ppermute | solution.py:412
  36.5 2.0 %collective-permute-done.1.other_ref = bf16[256,128]{1,0:T(8,128)(2,1)S(1)} collective-permute-done((bf16[256,128]{1,0:T(8,128)(2,1)S(1)}, bf16[256,128]{1,0:T(8,128)(2,1)S(1)}, u32[]{:S(2)}, u32[]{:S(2)}) %collective-permute-start.1) | collective-permute-done | bytes 65568 | tf_op jit(solution)/shard_map/ppermute | solution.py:412
  38.4 7.5 %all-to-all-done.got_ref = bf16[32,40,128]{2,1,0:T(8,128)(2,1)S(1)} async-done(((bf16[32,40,128]{2,1,0:T(8,128)(2,1)}), bf16[32,40,128]{2,1,0:T(8,128)(2,1)S(1)}, u32[]{:S(2)}, u32[]{:S(2)}) %all-to-all-start) | async-done | bytes 327712 | tf_op jit(solution)/shard_map/all_to_all | solution.py:380
  45.9 0.0 copy-done.4
  45.9 0.0 copy-done.9
  45.9 0.0 copy-done.10
  45.9 0.0 copy-done.15
  45.9 2.1 %pair.1 = bf16[32,40,128]{2,1,0:T(8,128)(2,1)} custom-call(s32[3,8]{1,0:T(4,128)S(1)} %get-tuple-element.14.table_ref, bf16[32,40,128]{2,1,0:T(8,128)(2,1)S(1)} %all-to-all-done.got_ref, bf16[32,256]{1,0:T(8,128)(2,1)S(1)} %bitcast.9, f32[256,128]{1,0:T(8,128)S(1)} %get-tuple-element.17.keep_ref, bf16[256,128]{1,0:T(8,128)(2,1)S(1)} %collective-permute-done.1.other_ref, ...), custom_call_target="tpu_custom_call" | custom-call | flops 1000000000 | bytes 1048576 | tf_op jit(solution)/shard_map/pair/pallas_call | solution.py:414
  48.0 6.5 %all-to-all-start.1 = ((bf16[32,40,128]{2,1,0:T(8,128)(2,1)}), bf16[32,40,128]{2,1,0:T(8,128)(2,1)S(1)}, u32[]{:S(2)}, u32[]{:S(2)}) async-start(bf16[32,40,128]{2,1,0:T(8,128)(2,1)} %pair.1), calls=%async_computation.1 | async-start | bytes 655360 | tf_op jit(solution)/shard_map/all_to_all | solution.py:423
  54.6 4.7 %collective-permute-start.2 = (bf16[256,128]{1,0:T(8,128)(2,1)S(1)}, bf16[256,128]{1,0:T(8,128)(2,1)S(1)}, u32[]{:S(2)}, u32[]{:S(2)}) collective-permute-start(bf16[256,128]{1,0:T(8,128)(2,1)S(1)} %get-tuple-element.25.own_ref), channel_id=1, source_target_pairs={{0,128},{8,136},{16,144},{24,152},{32,160},{40,168},{48,176},{56,1... | collective-permute-start | bytes 196616 | tf_op jit(solution)/shard_map/ppermute | solution.py:426
  59.2 2.3 %collective-permute-done.2.side_ref = bf16[256,128]{1,0:T(8,128)(2,1)S(1)} collective-permute-done((bf16[256,128]{1,0:T(8,128)(2,1)S(1)}, bf16[256,128]{1,0:T(8,128)(2,1)S(1)}, u32[]{:S(2)}, u32[]{:S(2)}) %collective-permute-start.2) | collective-permute-done | bytes 65568 | tf_op jit(solution)/shard_map/ppermute | solution.py:426
  61.6 4.6 %collective-permute-start.3 = (bf16[2,256,128]{2,1,0:T(8,128)(2,1)S(1)}, bf16[2,256,128]{2,1,0:T(8,128)(2,1)S(1)}, u32[]{:S(2)}, u32[]{:S(2)}) collective-permute-start(bf16[2,256,128]{2,1,0:T(8,128)(2,1)S(1)} %pad_maximum_fusion), channel_id=1, source_target_pairs={{0,256},{256,0},{1,257},{257,1},{2,258},{258,2},{3,259},{259,3},{4... | collective-permute-start | bytes 393224 | tf_op jit(solution)/shard_map/ppermute | solution.py:427
  66.2 1.1 %pair_taps.1.pair_ref = f32[32,256]{1,0:T(8,128)S(1)} custom-call(s32[3,8]{1,0:T(4,128)S(1)} %get-tuple-element.14.table_ref, bf16[32,40,128]{2,1,0:T(8,128)(2,1)S(1)} %all-to-all-done.got_ref, bf16[128,256]{1,0:T(8,128)(2,1)S(1)} %copy-done.15, bf16[128,256]{1,0:T(8,128)(2,1)S(1)} %copy-done.16, bf16[256,256]{1,0:T(8,128)(2,1)S(1)} %copy-done.7, ...), custom_call_target="tpu_custom_call" | custom-call | flops 1000000000 | bytes 786432 | tf_op jit(solution)/shard_map/pair_taps/pallas_call | solution.py:444
  67.3 0.0 collective-permute-done.3.core_ref.core_side_ref
  67.3 3.6 %local.1 = (f32[128,1024]{1,0:T(8,128)S(1)}, f32[128,1024]{1,0:T(8,128)S(1)}) custom-call(bf16[256,128]{1,0:T(8,128)(2,1)S(1)} %get-tuple-element.25.own_ref, bf16[256,128]{1,0:T(8,128)(2,1)S(1)} %collective-permute-done.2.side_ref, bf16[2,256,128]{2,1,0:T(8,128)(2,1)S(1)} %collective-permute-done.3.core_ref.core_side_ref, ...), custom_call_target="tpu_custom_call" | custom-call | flops 3000000000 | bytes 2621440 | tf_op jit(solution)/shard_map/local/pallas_call | solution.py:429
  70.9 6.6 %all-to-all-done.1.got_ref = bf16[32,40,128]{2,1,0:T(8,128)(2,1)S(1)} async-done(((bf16[32,40,128]{2,1,0:T(8,128)(2,1)}), bf16[32,40,128]{2,1,0:T(8,128)(2,1)S(1)}, u32[]{:S(2)}, u32[]{:S(2)}) %all-to-all-start.1) | async-done | bytes 327712 | tf_op jit(solution)/shard_map/all_to_all | solution.py:423
  77.5 0.1 taps.1.own_ref
  77.6 6.3 %collective-permute-start.4 = (f32[32,256]{1,0:T(8,128)S(1)}, f32[32,256]{1,0:T(8,128)S(1)}, u32[]{:S(2)}, u32[]{:S(2)}) collective-permute-start(f32[32,256]{1,0:T(8,128)S(1)} %taps.1.own_ref), channel_id=1, source_target_pairs={{0,256},{256,0},{1,257},{257,1},{2,258},{258,2},{3,259},{259,3},{4... | collective-permute-start | bytes 98312 | tf_op jit(solution)/shard_map/ppermute | solution.py:462
  83.9 1.7 %finish.1 = (bf16[128,1024]{1,0:T(8,128)(2,1)}, bf16[128,1024]{1,0:T(8,128)(2,1)}, bf16[128,1024]{1,0:T(8,128)(2,1)}) custom-call(s32[3,8]{1,0:T(4,128)S(1)} %get-tuple-element.14.table_ref, bf16[32,40,128]{2,1,0:T(8,128)(2,1)S(1)} %all-to-all-done.1.got_ref, f32[128,1024]{1,0:T(8,128)S(1)} %get-tuple-element.19.mixed_ref.after_ref, ...), custom_call_target="tpu_custom_call" | custom-call | flops 1310720 | bytes 2621440 | tf_op jit(solution)/shard_map/finish/pallas_call | solution.py:465
  85.6 0.0 collective-permute-done.4.other_ref
  85.6 0.6 taps_out.1
  (15 shorter events, 0.1 us)
Async XLA Ops:
  0.6 21.3 %copy-start.2 = (bf16[128,1024]{1,0:T(8,128)(2,1)S(1)}, bf16[128,1024]{1,0:T(8,128)(2,1)}, u32[]{:S(2)}) copy-start(bf16[128,1024]{1,0:T(8,128)(2,1)} %c_ref.5) | copy-start | bytes 786436
  0.6 21.3 %copy-start.3 = (bf16[128,1024]{1,0:T(8,128)(2,1)S(1)}, bf16[128,1024]{1,0:T(8,128)(2,1)}, u32[]{:S(2)}) copy-start(bf16[128,1024]{1,0:T(8,128)(2,1)} %q_ref.3) | copy-start | bytes 786436
  0.7 21.3 %copy-start.12 = (bf16[256,128]{1,0:T(8,128)(2,1)S(1)}, bf16[256,128]{1,0:T(8,128)(2,1)}, u32[]{:S(2)}) copy-start(bf16[256,128]{1,0:T(8,128)(2,1)} %constant.25.clone.fwd_lo.taps_lo) | copy-start | bytes 196612
  0.7 21.3 %copy-start.13 = (bf16[128,256]{1,0:T(8,128)(2,1)S(1)}, bf16[128,256]{1,0:T(8,128)(2,1)}, u32[]{:S(2)}) copy-start(bf16[128,256]{1,0:T(8,128)(2,1)} %constant.28.clone.inv_hi) | copy-start | bytes 196612
  0.7 21.3 %copy-start.14 = (bf16[128,256]{1,0:T(8,128)(2,1)S(1)}, bf16[128,256]{1,0:T(8,128)(2,1)}, u32[]{:S(2)}) copy-start(bf16[128,256]{1,0:T(8,128)(2,1)} %constant.29.clone.inv_lo) | copy-start | bytes 196612
  3.2 18.8 %copy-start = (bf16[128,1024]{1,0:T(8,128)(2,1)S(1)}, bf16[128,1024]{1,0:T(8,128)(2,1)}, u32[]{:S(2)}) copy-start(bf16[128,1024]{1,0:T(8,128)(2,1)} %k_ref.5) | copy-start | bytes 786436
  3.2 18.8 %copy-start.1 = (bf16[128,1024]{1,0:T(8,128)(2,1)S(1)}, bf16[128,1024]{1,0:T(8,128)(2,1)}, u32[]{:S(2)}) copy-start(bf16[128,1024]{1,0:T(8,128)(2,1)} %v_ref.5) | copy-start | bytes 786436
  3.2 18.8 %copy-start.5 = (s32[1,32]{1,0:T(1,128)S(1)}, s32[1,32]{1,0:T(1,128)}, u32[]{:S(2)}) copy-start(s32[1,32]{1,0:T(1,128)} %slot_hbm.1) | copy-start | bytes 388
  3.2 18.7 %copy-start.6 = (s32[1,24]{1,0:T(1,128)S(1)}, s32[1,24]{1,0:T(1,128)}, u32[]{:S(2)}) copy-start(s32[1,24]{1,0:T(1,128)} %len_hbm.1) | copy-start | bytes 292
  3.2 18.7 %copy-start.11 = (bf16[256,128]{1,0:T(8,128)(2,1)S(1)}, bf16[256,128]{1,0:T(8,128)(2,1)}, u32[]{:S(2)}) copy-start(bf16[256,128]{1,0:T(8,128)(2,1)} %constant.24.clone.fwd_hi.taps_hi) | copy-start | bytes 196612
  3.2 42.6 %all-to-all-start = ((bf16[32,40,128]{2,1,0:T(8,128)(2,1)}), bf16[32,40,128]{2,1,0:T(8,128)(2,1)S(1)}, u32[]{:S(2)}, u32[]{:S(2)}) async-start(bf16[32,40,128]{2,1,0:T(8,128)(2,1)} %send.1), calls=%async_computation | async-start | bytes 655360 | tf_op jit(solution)/shard_map/all_to_all | solution.py:380
  22.0 23.9 %copy-start.16 = (bf16[128,256]{1,0:T(8,128)(2,1)S(1)}, bf16[128,256]{1,0:T(8,128)(2,1)}, u32[]{:S(2)}) copy-start(bf16[128,256]{1,0:T(8,128)(2,1)} %constant.27.clone.fwd_lo) | copy-start | bytes 196612
  22.0 23.9 %copy-start.17 = (bf16[256,128]{1,0:T(8,128)(2,1)S(1)}, bf16[256,128]{1,0:T(8,128)(2,1)}, u32[]{:S(2)}) copy-start(bf16[256,128]{1,0:T(8,128)(2,1)} %constant.30.clone.inv_hi) | copy-start | bytes 196612
  22.0 23.9 %copy-start.18 = (bf16[256,128]{1,0:T(8,128)(2,1)S(1)}, bf16[256,128]{1,0:T(8,128)(2,1)}, u32[]{:S(2)}) copy-start(bf16[256,128]{1,0:T(8,128)(2,1)} %constant.31.clone.inv_lo) | copy-start | bytes 196612
  27.5 3.8 %collective-permute-start = (bf16[2,256,128]{2,1,0:T(8,128)(2,1)S(1)}, bf16[2,256,128]{2,1,0:T(8,128)(2,1)S(1)}, u32[]{:S(2)}, u32[]{:S(2)}) collective-permute-start(bf16[2,256,128]{2,1,0:T(8,128)(2,1)S(1)} %get-tuple-element.16), channel_id=1, source_target_pairs={{0,256},{256,0},{1,257},{257,1},{2,258},{258,2},{3,259},{259,3},{4... | collective-permute-start | bytes 393224 | tf_op jit(solution)/shard_map/ppermute | solution.py:398
  31.3 14.6 %copy-start.4 = (bf16[256,32]{0,1:T(8,128)(2,1)S(1)}, bf16[256,32]{0,1:T(8,128)(2,1)}, u32[]{:S(2)}) copy-start(bf16[256,32]{0,1:T(8,128)(2,1)} %param.23) | copy-start | bytes 49156
  31.3 14.6 %copy-start.9 = (bf16[256,256]{1,0:T(8,128)(2,1)S(1)}, bf16[256,256]{1,0:T(8,128)(2,1)}, u32[]{:S(2)}) copy-start(bf16[256,256]{1,0:T(8,128)(2,1)} %constant.32.clone.tap_hi) | copy-start | bytes 393220
  31.3 14.6 %copy-start.10 = (bf16[256,256]{1,0:T(8,128)(2,1)S(1)}, bf16[256,256]{1,0:T(8,128)(2,1)}, u32[]{:S(2)}) copy-start(bf16[256,256]{1,0:T(8,128)(2,1)} %constant.33.clone.tap_lo) | copy-start | bytes 393220
  31.4 14.6 %copy-start.15 = (bf16[128,256]{1,0:T(8,128)(2,1)S(1)}, bf16[128,256]{1,0:T(8,128)(2,1)}, u32[]{:S(2)}) copy-start(bf16[128,256]{1,0:T(8,128)(2,1)} %constant.26.clone.fwd_hi) | copy-start | bytes 196612
  31.4 7.0 %collective-permute-start.1 = (bf16[256,128]{1,0:T(8,128)(2,1)S(1)}, bf16[256,128]{1,0:T(8,128)(2,1)S(1)}, u32[]{:S(2)}, u32[]{:S(2)}) collective-permute-start(bf16[256,128]{1,0:T(8,128)(2,1)S(1)} %get-tuple-element.18), channel_id=1, source_target_pairs={{0,128},{8,136},{16,144},{24,152},{32,160},{40,168},{48,176},{56,1... | collective-permute-start | bytes 196616 | tf_op jit(solution)/shard_map/ppermute | solution.py:412
  48.0 29.5 %all-to-all-start.1 = ((bf16[32,40,128]{2,1,0:T(8,128)(2,1)}), bf16[32,40,128]{2,1,0:T(8,128)(2,1)S(1)}, u32[]{:S(2)}, u32[]{:S(2)}) async-start(bf16[32,40,128]{2,1,0:T(8,128)(2,1)} %pair.1), calls=%async_computation.1 | async-start | bytes 655360 | tf_op jit(solution)/shard_map/all_to_all | solution.py:423
  54.6 7.0 %collective-permute-start.2 = (bf16[256,128]{1,0:T(8,128)(2,1)S(1)}, bf16[256,128]{1,0:T(8,128)(2,1)S(1)}, u32[]{:S(2)}, u32[]{:S(2)}) collective-permute-start(bf16[256,128]{1,0:T(8,128)(2,1)S(1)} %get-tuple-element.25.own_ref), channel_id=1, source_target_pairs={{0,128},{8,136},{16,144},{24,152},{32,160},{40,168},{48,176},{56,1... | collective-permute-start | bytes 196616 | tf_op jit(solution)/shard_map/ppermute | solution.py:426
  61.5 4.7 %copy-start.7 = (bf16[256,256]{1,0:T(8,128)(2,1)S(1)}, bf16[256,256]{1,0:T(8,128)(2,1)}, u32[]{:S(2)}) copy-start(bf16[256,256]{1,0:T(8,128)(2,1)} %constant.34.clone.lag_hi) | copy-start | bytes 393220
  61.5 4.7 %copy-start.8 = (bf16[256,256]{1,0:T(8,128)(2,1)S(1)}, bf16[256,256]{1,0:T(8,128)(2,1)}, u32[]{:S(2)}) copy-start(bf16[256,256]{1,0:T(8,128)(2,1)} %constant.35.clone.lag_lo) | copy-start | bytes 393220
  61.6 5.7 %collective-permute-start.3 = (bf16[2,256,128]{2,1,0:T(8,128)(2,1)S(1)}, bf16[2,256,128]{2,1,0:T(8,128)(2,1)S(1)}, u32[]{:S(2)}, u32[]{:S(2)}) collective-permute-start(bf16[2,256,128]{2,1,0:T(8,128)(2,1)S(1)} %pad_maximum_fusion), channel_id=1, source_target_pairs={{0,256},{256,0},{1,257},{257,1},{2,258},{258,2},{3,259},{259,3},{4... | collective-permute-start | bytes 393224 | tf_op jit(solution)/shard_map/ppermute | solution.py:427
  77.6 8.0 %collective-permute-start.4 = (f32[32,256]{1,0:T(8,128)S(1)}, f32[32,256]{1,0:T(8,128)S(1)}, u32[]{:S(2)}, u32[]{:S(2)}) collective-permute-start(f32[32,256]{1,0:T(8,128)S(1)} %taps.1.own_ref), channel_id=1, source_target_pairs={{0,256},{256,0},{1,257},{257,1},{2,258},{258,2},{3,259},{259,3},{4... | collective-permute-start | bytes 98312 | tf_op jit(solution)/shard_map/ppermute | solution.py:462

commit v3 on v2

--- a/solution.py
+++ b/solution.py
@@ -11,6 +11,8 @@
 SPAN = 128
 PTS = 2 * SPAN
 QUARTER = SPAN // 4
+TURN = 24
+TURN_BLOCK = TURN // 8
 F32, BF16 = jnp.float32, jnp.bfloat16
 
 
@@ -136,7 +138,8 @@
         for copy in wide[j]:
             copy.wait()
         cols = slice(j * width, (j + 1) * width)
-        rows = slice(j * count, (j + 1) * count)
+        place = j ^ TURN_BLOCK
+        rows = slice(place * count, (place + 1) * count)
         a = jnp.where(first, k_buf[:, cols].astype(F32), c_buf[:, cols].astype(F32))
         b = jnp.where(first, v_buf[:, cols].astype(F32), q_buf[:, cols].astype(F32))
         out_buf[rows, 0:32, :] = jnp.transpose((a * b).astype(BF16)).reshape(count, 32, SPAN)
@@ -206,7 +209,7 @@
 
 def pair_spectra(table_ref, got_ref, fwd_hi, fwd_lo):
     pairs = table_ref.shape[1]
-    rows = [got_ref[table_ref[k, p], 0:32, :] for k in range(2) for p in range(pairs)]
+    rows = [got_ref[table_ref[k, p] ^ TURN, 0:32, :] for k in range(2) for p in range(pairs)]
     spec = spectrum_right(jnp.concatenate(rows, 0), fwd_hi[...], fwd_lo[...])
     return spec.reshape(2, pairs, 32, PTS)
 
@@ -227,9 +230,12 @@
         both = jnp.concatenate([pr, pi], 2).reshape(pairs * 32, PTS)
         result = invert_right(both, inv_hi[...], inv_lo[...]).astype(BF16)
         for p in range(pairs):
-            out_ref[table_ref[1 - k, p], 0:32, :] = result[32 * p:32 * p + 32]
+            out_ref[table_ref[1 - k, p] ^ TURN, 0:32, :] = result[32 * p:32 * p + 32]
     near = (keep_ref[...] + other_ref[...].astype(F32)).astype(BF16)
-    out_ref[:, 32:40, :] = near.reshape(slots, 8, SPAN)
+    near = near.reshape(slots, 8, SPAN)
+    for j in range(slots // 8):
+        place = 8 * (j ^ TURN_BLOCK)
+        out_ref[place:place + 8, 32:40, :] = near[8 * j:8 * j + 8]
 
 
 def pair_taps_kernel(table_ref, got_ref, fwd_hi, fwd_lo, lag_hi, lag_lo, out_ref):
@@ -277,7 +283,8 @@
     core = lax.axis_index("dp")
     sums = []
     for far in range(2):
-        rows = got_ref[far * 16:far * 16 + 16, 32:40, :].astype(F32)
+        place = 16 * (far ^ (TURN // 16))
+        rows = got_ref[place:place + 16, 32:40, :].astype(F32)
         sums.append(jnp.sum(rows, axis=0))
     quarters = [jnp.where(core == t // 2, sums[t % 2], 0.0) for t in range(4)]
     near = jnp.concatenate(swap_blocks(quarters), 0)
@@ -296,7 +303,8 @@
     copies = []
     for j in range(chunks):
         cols = slice(j * width, (j + 1) * width)
-        rows = got_ref[j * count:(j + 1) * count, 0:32, :].reshape(width, SPAN)
+        place = (j ^ TURN_BLOCK) * count
+        rows = got_ref[place:place + count, 0:32, :].reshape(width, SPAN)
         pair = jnp.transpose(rows).astype(F32)
         mixed = mixed_ref[:, cols] + jnp.where(kind == 2, pair, 0.0)
         series = series_ref[:, cols] + jnp.where(kind == 1, pair, 0.0)
@@ -359,6 +367,12 @@
 
     def whole(array):
         return pl.BlockSpec(array.shape, lambda i: (0,) * array.ndim)
+
+    def exchange(array):
+        order = [[k ^ TURN for k in range(parts)]]
+        return lax.all_to_all(
+            array, "ctx", split_axis=0, concat_axis=0, axis_index_groups=order, tiled=True
+        )
 
     chunk = jax.ShapeDtypeStruct((parts, 40, SPAN), BF16)
     out = pl.pallas_call(
@@ -377,7 +391,7 @@
         cost_estimate=cost(2 * area, 8 * area),
         name="send",
     )(span_slot, doc_lengths, taps_rows, query, key, value, cotangent)
-    got = lax.all_to_all(out, "ctx", split_axis=0, concat_axis=0, tiled=True)
+    got = exchange(out)
 
     two = pl.BlockSpec((2, group * 8, SPAN), lambda i: (0, i, 0))
     keep, give, table = pl.pallas_call(
@@ -420,20 +434,20 @@
         cost_estimate=cost(1e9, 8 * area),
         name="pair",
     )(table, got, taps_rows, keep, near_other, *fwd_t, *inv_t, *tap_t)
-    landed = lax.all_to_all(back, "ctx", split_axis=0, concat_axis=0, tiled=True)
+    landed = exchange(back)
 
     own = got[:, 32:40, :].reshape(parts * 8, SPAN)
     side = lax.ppermute(own, "ctx", side_swap)
     core = lax.ppermute(jnp.stack([own, side]), "dp", core_swap)
-    quarter = pl.BlockSpec((group * 8, SPAN), lambda i: (i, 0))
+    quarter = pl.BlockSpec((group * 8, SPAN), lambda i: (i ^ TURN_BLOCK, 0))
     mixed, series = pl.pallas_call(
         local_kernel,
         grid=(steps,),
         out_shape=(jax.ShapeDtypeStruct((tokens, width), F32),) * 2,
         in_specs=[
             quarter, quarter,
-            pl.BlockSpec((1, group * 8, SPAN), lambda i: (0, i, 0)),
-            pl.BlockSpec((1, group * 8, SPAN), lambda i: (1, i, 0)),
+            pl.BlockSpec((1, group * 8, SPAN), lambda i: (0, i ^ TURN_BLOCK, 0)),
+            pl.BlockSpec((1, group * 8, SPAN), lambda i: (1, i ^ TURN_BLOCK, 0)),
         ] + [wide] * 4 + [whole(m) for m in fwd + inv + fwd],
         out_specs=(wide, wide),
         compiler_params=params(),

time: 86.7 us -> 79.6 us (0.918)
  waiting for transfers between devices: 19.3 us -> 10.1 us
  starting transfers between devices: 48.6 us -> 50.7 us
    all_to_all x2, waiting for transfers between devices: 14 us -> 0.01 us  [exchange(): lax.all_to_all(array, 'ctx', split_axis=0, concat_axis=0, axis_index_grou...]
    all_to_all x2, starting transfers between devices: 25.1 us -> 36 us  [exchange(): lax.all_to_all(array, 'ctx', split_axis=0, concat_axis=0, axis_index_grou...]
    ppermute x1, starting transfers between devices: 6.28 us -> 2.14 us  [per_device(): taps_other = lax.ppermute(taps_own, 'dp', core_swap)]
    ppermute x1, starting transfers between devices: 5.06 us -> 2.28 us  [per_device(): near_other = lax.ppermute(give, 'ctx', side_swap)]
    ppermute x1, starting transfers between devices: 4.65 us -> 2.15 us  [per_device(): side = lax.ppermute(own, 'ctx', side_swap)]
    ppermute x1, waiting for transfers between devices: 2.32 us -> 4.76 us  [per_device(): side = lax.ppermute(own, 'ctx', side_swap)]
    ppermute x1, waiting for transfers between devices: 1.97 us -> 4.36 us  [per_device(): near_other = lax.ppermute(give, 'ctx', side_swap)]
  transfers between devices with their start and end apart: 7 -> 7, of which waited for: 5 -> 3; matrix products, arithmetic and copies ran while one was open for 0% -> 0% of each run, Pallas kernels for 14% -> 15%
where the time goes in v3:
time: 79.6 us; the launch traced here: 79.1 us
  starting transfers between devices  50.7 us (64%)
  Pallas kernels  17.2 us (22%)
  waiting for transfers between devices  10.1 us (13%)
  between operations  1 us (1%)
    all_to_all x2, starting transfers between devices, exchange(): lax.all_to_all(array, 'ctx', split_axis=0, concat_axis=0, axis_index_grou...  36 us
    pallas_call x1, Pallas kernels, per_device(): pl.pallas_call(partial_kernel, grid=(steps,), out_shape=(jax.ShapeDtypeSt...  5.47 us
    ppermute x1, starting transfers between devices, per_device(): core = lax.ppermute(jnp.stack([own, side]), 'dp', core_swap)  5.02 us
    ppermute x1, waiting for transfers between devices, per_device(): side = lax.ppermute(own, 'ctx', side_swap)  4.76 us
    ppermute x1, waiting for transfers between devices, per_device(): near_other = lax.ppermute(give, 'ctx', side_swap)  4.36 us
    pallas_call x1, Pallas kernels, per_device(): pl.pallas_call(local_kernel, grid=(steps,), out_shape=(jax.ShapeDtypeStru...  3.65 us
    ppermute x1, starting transfers between devices, per_device(): taken = lax.ppermute(give, 'dp', core_swap)  3.15 us
    pallas_call x1, Pallas kernels, per_device(): pl.pallas_call(send_kernel, out_shape=chunk, in_specs=[HBM] * 7, out_spec...  2.49 us
  transfers between devices with their start and end apart: 7, of which 3 were waited for; matrix products, arithmetic and copies ran while one was open for 0% of the time, Pallas kernels for 15%

profile of v3, /device:TPU:1, one launch (start us, length us, event | category | flops | bytes accessed | tf_op | source)
XLA Modules:
  0.0 79.1 jit_solution(7199901592224210231)
XLA Ops:
  0.6 0.0 copy-start.2
  0.6 0.0 copy-start.3
  0.7 0.0 copy-start.12
  0.7 0.0 copy-start.13
  0.7 0.0 copy-start.14
  0.7 2.5 %send.1 = bf16[32,40,128]{2,1,0:T(8,128)(2,1)} custom-call(s32[1,32]{1,0:T(1,128)} %slot_hbm.1, s32[1,24]{1,0:T(1,128)} %len_hbm.1, bf16[32,256]{1,0:T(8,128)(2,1)} %bitcast.8, bf16[128,1024]{1,0:T(8,128)(2,1)} %q_ref.3, bf16[128,1024]{1,0:T(8,128)(2,1)} %k_ref.5, bf16[128,1024]{1,0:T(8,128)(2,1)} %v_ref.5, bf16[128,1024]{1,0:T(8,128)(2,1)} %c_ref.5), custom_call_target="tpu_custom_call" | custom-call | flops 262144 | bytes 1048576 | tf_op jit(solution)/shard_map/send/pallas_call | solution.py:378
  3.2 0.0 copy-start
  3.2 0.0 copy-start.1
  3.2 0.0 copy-start.5
  3.2 0.0 copy-start.6
  3.2 0.0 copy-start.11
  3.3 21.9 %all-to-all-start = ((bf16[32,40,128]{2,1,0:T(8,128)(2,1)}), bf16[32,40,128]{2,1,0:T(8,128)(2,1)S(1)}, u32[]{:S(2)}, u32[]{:S(2)}) async-start(bf16[32,40,128]{2,1,0:T(8,128)(2,1)} %send.1), calls=%async_computation | async-start | bytes 655360 | tf_op jit(solution)/shard_map/all_to_all | solution.py:373
  25.2 0.0 copy-done.2
  25.2 0.0 copy-done.3
  25.2 0.0 copy-done.12
  25.2 0.0 copy-done.13
  25.2 0.0 copy-done.14
  25.2 0.0 copy-done
  25.2 0.0 copy-done.1
  25.2 0.0 copy-done.5
  25.2 0.0 copy-done.6
  25.3 0.0 copy-done.11
  25.3 0.0 copy-start.16
  25.3 0.0 copy-start.17
  25.3 0.0 copy-start.18
  25.3 5.5 %partial_taps.1 = (f32[2,256,128]{2,1,0:T(8,128)S(1)}, bf16[2,256,128]{2,1,0:T(8,128)(2,1)S(1)}, s32[3,8]{1,0:T(4,128)S(1)}) custom-call(s32[1,32]{1,0:T(1,128)S(1)} %copy-done.5, s32[1,24]{1,0:T(1,128)S(1)} %copy-done.6, bf16[128,1024]{1,0:T(8,128)(2,1)S(1)} %copy-done.3, bf16[128,1024]{1,0:T(8,128)(2,1)S(1)} %copy-done, bf16[128,1024]{1,0:T(8,128)(2,1)S(1)} %copy-done.1, ...), custom_call_target="tpu_custom_call" | custom-call | flops 2000000000 | bytes 1310720 | tf_op jit(solution)/shard_map/partial_taps/pallas_call | solution.py:397
  30.8 3.1 %collective-permute-start = (bf16[2,256,128]{2,1,0:T(8,128)(2,1)S(1)}, bf16[2,256,128]{2,1,0:T(8,128)(2,1)S(1)}, u32[]{:S(2)}, u32[]{:S(2)}) collective-permute-start(bf16[2,256,128]{2,1,0:T(8,128)(2,1)S(1)} %get-tuple-element.16), channel_id=1, source_target_pairs={{0,256},{256,0},{1,257},{257,1},{2,258},{258,2},{3,259},{259,3},{4... | collective-permute-start | bytes 393224 | tf_op jit(solution)/shard_map/ppermute | solution.py:412
  33.9 1.0 %collective-permute-done.other_ref = bf16[2,256,128]{2,1,0:T(8,128)(2,1)S(1)} collective-permute-done((bf16[2,256,128]{2,1,0:T(8,128)(2,1)S(1)}, bf16[2,256,128]{2,1,0:T(8,128)(2,1)S(1)}, u32[]{:S(2)}, u32[]{:S(2)}) %collective-permute-start) | collective-permute-done | bytes 131104 | tf_op jit(solution)/shard_map/ppermute | solution.py:412
  35.0 2.3 %collective-permute-start.1 = (bf16[256,128]{1,0:T(8,128)(2,1)S(1)}, bf16[256,128]{1,0:T(8,128)(2,1)S(1)}, u32[]{:S(2)}, u32[]{:S(2)}) collective-permute-start(bf16[256,128]{1,0:T(8,128)(2,1)S(1)} %get-tuple-element.18), channel_id=1, source_target_pairs={{0,128},{8,136},{16,144},{24,152},{32,160},{40,168},{48,176},{56,1... | collective-permute-start | bytes 196616 | tf_op jit(solution)/shard_map/ppermute | solution.py:426
  37.2 4.4 %collective-permute-done.1.other_ref = bf16[256,128]{1,0:T(8,128)(2,1)S(1)} collective-permute-done((bf16[256,128]{1,0:T(8,128)(2,1)S(1)}, bf16[256,128]{1,0:T(8,128)(2,1)S(1)}, u32[]{:S(2)}, u32[]{:S(2)}) %collective-permute-start.1) | collective-permute-done | bytes 65568 | tf_op jit(solution)/shard_map/ppermute | solution.py:426
  41.6 0.0 all-to-all-done.got_ref
  41.6 0.0 copy-done.16
  41.6 0.0 copy-done.17
  41.6 0.0 copy-done.18
  41.7 2.1 %pair.1 = bf16[32,40,128]{2,1,0:T(8,128)(2,1)} custom-call(s32[3,8]{1,0:T(4,128)S(1)} %get-tuple-element.14.table_ref, bf16[32,40,128]{2,1,0:T(8,128)(2,1)S(1)} %all-to-all-done.got_ref, bf16[32,256]{1,0:T(8,128)(2,1)S(1)} %bitcast.9, f32[256,128]{1,0:T(8,128)S(1)} %get-tuple-element.17.keep_ref, bf16[256,128]{1,0:T(8,128)(2,1)S(1)} %collective-permute-done.1.other_ref, ...), custom_call_target="tpu_custom_call" | custom-call | flops 1000000000 | bytes 1048576 | tf_op jit(solution)/shard_map/pair/pallas_call | solution.py:428
  43.7 14.1 %all-to-all-start.1 = ((bf16[32,40,128]{2,1,0:T(8,128)(2,1)}), bf16[32,40,128]{2,1,0:T(8,128)(2,1)S(1)}, u32[]{:S(2)}, u32[]{:S(2)}) async-start(bf16[32,40,128]{2,1,0:T(8,128)(2,1)} %pair.1), calls=%async_computation.1 | async-start | bytes 655360 | tf_op jit(solution)/shard_map/all_to_all | solution.py:373
  57.8 2.2 %collective-permute-start.2 = (bf16[256,128]{1,0:T(8,128)(2,1)S(1)}, bf16[256,128]{1,0:T(8,128)(2,1)S(1)}, u32[]{:S(2)}, u32[]{:S(2)}) collective-permute-start(bf16[256,128]{1,0:T(8,128)(2,1)S(1)} %get-tuple-element.25.own_ref), channel_id=1, source_target_pairs={{0,128},{8,136},{16,144},{24,152},{32,160},{40,168},{48,176},{56,1... | collective-permute-start | bytes 196616 | tf_op jit(solution)/shard_map/ppermute | solution.py:440
  60.0 4.8 %collective-permute-done.2.side_ref = bf16[256,128]{1,0:T(8,128)(2,1)S(1)} collective-permute-done((bf16[256,128]{1,0:T(8,128)(2,1)S(1)}, bf16[256,128]{1,0:T(8,128)(2,1)S(1)}, u32[]{:S(2)}, u32[]{:S(2)}) %collective-permute-start.2) | collective-permute-done | bytes 65568 | tf_op jit(solution)/shard_map/ppermute | solution.py:440
  64.8 5.0 %collective-permute-start.3 = (bf16[2,256,128]{2,1,0:T(8,128)(2,1)S(1)}, bf16[2,256,128]{2,1,0:T(8,128)(2,1)S(1)}, u32[]{:S(2)}, u32[]{:S(2)}) collective-permute-start(bf16[2,256,128]{2,1,0:T(8,128)(2,1)S(1)} %pad_maximum_fusion), channel_id=1, source_target_pairs={{0,256},{256,0},{1,257},{257,1},{2,258},{258,2},{3,259},{259,3},{4... | collective-permute-start | bytes 393224 | tf_op jit(solution)/shard_map/ppermute | solution.py:441
  69.8 1.1 %pair_taps.1.pair_ref = f32[32,256]{1,0:T(8,128)S(1)} custom-call(s32[3,8]{1,0:T(4,128)S(1)} %get-tuple-element.14.table_ref, bf16[32,40,128]{2,1,0:T(8,128)(2,1)S(1)} %all-to-all-done.got_ref, bf16[128,256]{1,0:T(8,128)(2,1)S(1)} %copy-done.15, bf16[128,256]{1,0:T(8,128)(2,1)S(1)} %copy-done.16, bf16[256,256]{1,0:T(8,128)(2,1)S(1)} %copy-done.7, ...), custom_call_target="tpu_custom_call" | custom-call | flops 1000000000 | bytes 786432 | tf_op jit(solution)/shard_map/pair_taps/pallas_call | solution.py:458
  70.9 0.0 collective-permute-done.3.core_ref.core_side_ref
  70.9 3.7 %local.1 = (f32[128,1024]{1,0:T(8,128)S(1)}, f32[128,1024]{1,0:T(8,128)S(1)}) custom-call(bf16[256,128]{1,0:T(8,128)(2,1)S(1)} %get-tuple-element.25.own_ref, bf16[256,128]{1,0:T(8,128)(2,1)S(1)} %collective-permute-done.2.side_ref, bf16[2,256,128]{2,1,0:T(8,128)(2,1)S(1)} %collective-permute-done.3.core_ref.core_side_ref, ...), custom_call_target="tpu_custom_call" | custom-call | flops 3000000000 | bytes 2621440 | tf_op jit(solution)/shard_map/local/pallas_call | solution.py:443
  74.5 0.0 all-to-all-done.1.got_ref
  74.6 0.1 taps.1.own_ref
  74.7 2.1 %collective-permute-start.4 = (f32[32,256]{1,0:T(8,128)S(1)}, f32[32,256]{1,0:T(8,128)S(1)}, u32[]{:S(2)}, u32[]{:S(2)}) collective-permute-start(f32[32,256]{1,0:T(8,128)S(1)} %taps.1.own_ref), channel_id=1, source_target_pairs={{0,256},{256,0},{1,257},{257,1},{2,258},{258,2},{3,259},{259,3},{4... | collective-permute-start | bytes 98312 | tf_op jit(solution)/shard_map/ppermute | solution.py:476
  76.8 1.7 %finish.1 = (bf16[128,1024]{1,0:T(8,128)(2,1)}, bf16[128,1024]{1,0:T(8,128)(2,1)}, bf16[128,1024]{1,0:T(8,128)(2,1)}) custom-call(s32[3,8]{1,0:T(4,128)S(1)} %get-tuple-element.14.table_ref, bf16[32,40,128]{2,1,0:T(8,128)(2,1)S(1)} %all-to-all-done.1.got_ref, f32[128,1024]{1,0:T(8,128)S(1)} %get-tuple-element.19.mixed_ref.after_ref, ...), custom_call_target="tpu_custom_call" | custom-call | flops 1310720 | bytes 2621440 | tf_op jit(solution)/shard_map/finish/pallas_call | solution.py:479
  78.5 0.0 collective-permute-done.4.other_ref
  78.5 0.6 taps_out.1
  (15 shorter events, 0.1 us)
Async XLA Ops:
  0.6 24.5 %copy-start.2 = (bf16[128,1024]{1,0:T(8,128)(2,1)S(1)}, bf16[128,1024]{1,0:T(8,128)(2,1)}, u32[]{:S(2)}) copy-start(bf16[128,1024]{1,0:T(8,128)(2,1)} %c_ref.5) | copy-start | bytes 786436
  0.6 24.5 %copy-start.3 = (bf16[128,1024]{1,0:T(8,128)(2,1)S(1)}, bf16[128,1024]{1,0:T(8,128)(2,1)}, u32[]{:S(2)}) copy-start(bf16[128,1024]{1,0:T(8,128)(2,1)} %q_ref.3) | copy-start | bytes 786436
  0.7 24.5 %copy-start.12 = (bf16[256,128]{1,0:T(8,128)(2,1)S(1)}, bf16[256,128]{1,0:T(8,128)(2,1)}, u32[]{:S(2)}) copy-start(bf16[256,128]{1,0:T(8,128)(2,1)} %constant.25.clone.fwd_lo.taps_lo) | copy-start | bytes 196612
  0.7 24.5 %copy-start.13 = (bf16[128,256]{1,0:T(8,128)(2,1)S(1)}, bf16[128,256]{1,0:T(8,128)(2,1)}, u32[]{:S(2)}) copy-start(bf16[128,256]{1,0:T(8,128)(2,1)} %constant.28.clone.inv_hi) | copy-start | bytes 196612
  0.7 24.5 %copy-start.14 = (bf16[128,256]{1,0:T(8,128)(2,1)S(1)}, bf16[128,256]{1,0:T(8,128)(2,1)}, u32[]{:S(2)}) copy-start(bf16[128,256]{1,0:T(8,128)(2,1)} %constant.29.clone.inv_lo) | copy-start | bytes 196612
  3.2 22.0 %copy-start = (bf16[128,1024]{1,0:T(8,128)(2,1)S(1)}, bf16[128,1024]{1,0:T(8,128)(2,1)}, u32[]{:S(2)}) copy-start(bf16[128,1024]{1,0:T(8,128)(2,1)} %k_ref.5) | copy-start | bytes 786436
  3.2 22.0 %copy-start.1 = (bf16[128,1024]{1,0:T(8,128)(2,1)S(1)}, bf16[128,1024]{1,0:T(8,128)(2,1)}, u32[]{:S(2)}) copy-start(bf16[128,1024]{1,0:T(8,128)(2,1)} %v_ref.5) | copy-start | bytes 786436
  3.2 22.0 %copy-start.5 = (s32[1,32]{1,0:T(1,128)S(1)}, s32[1,32]{1,0:T(1,128)}, u32[]{:S(2)}) copy-start(s32[1,32]{1,0:T(1,128)} %slot_hbm.1) | copy-start | bytes 388
  3.2 22.0 %copy-start.6 = (s32[1,24]{1,0:T(1,128)S(1)}, s32[1,24]{1,0:T(1,128)}, u32[]{:S(2)}) copy-start(s32[1,24]{1,0:T(1,128)} %len_hbm.1) | copy-start | bytes 292
  3.2 22.0 %copy-start.11 = (bf16[256,128]{1,0:T(8,128)(2,1)S(1)}, bf16[256,128]{1,0:T(8,128)(2,1)}, u32[]{:S(2)}) copy-start(bf16[256,128]{1,0:T(8,128)(2,1)} %constant.24.clone.fwd_hi.taps_hi) | copy-start | bytes 196612
  3.3 38.4 %all-to-all-start = ((bf16[32,40,128]{2,1,0:T(8,128)(2,1)}), bf16[32,40,128]{2,1,0:T(8,128)(2,1)S(1)}, u32[]{:S(2)}, u32[]{:S(2)}) async-start(bf16[32,40,128]{2,1,0:T(8,128)(2,1)} %send.1), calls=%async_computation | async-start | bytes 655360 | tf_op jit(solution)/shard_map/all_to_all | solution.py:373
  25.3 16.3 %copy-start.16 = (bf16[128,256]{1,0:T(8,128)(2,1)S(1)}, bf16[128,256]{1,0:T(8,128)(2,1)}, u32[]{:S(2)}) copy-start(bf16[128,256]{1,0:T(8,128)(2,1)} %constant.27.clone.fwd_lo) | copy-start | bytes 196612
  25.3 16.3 %copy-start.17 = (bf16[256,128]{1,0:T(8,128)(2,1)S(1)}, bf16[256,128]{1,0:T(8,128)(2,1)}, u32[]{:S(2)}) copy-start(bf16[256,128]{1,0:T(8,128)(2,1)} %constant.30.clone.inv_hi) | copy-start | bytes 196612
  25.3 16.3 %copy-start.18 = (bf16[256,128]{1,0:T(8,128)(2,1)S(1)}, bf16[256,128]{1,0:T(8,128)(2,1)}, u32[]{:S(2)}) copy-start(bf16[256,128]{1,0:T(8,128)(2,1)} %constant.31.clone.inv_lo) | copy-start | bytes 196612
  30.8 4.1 %collective-permute-start = (bf16[2,256,128]{2,1,0:T(8,128)(2,1)S(1)}, bf16[2,256,128]{2,1,0:T(8,128)(2,1)S(1)}, u32[]{:S(2)}, u32[]{:S(2)}) collective-permute-start(bf16[2,256,128]{2,1,0:T(8,128)(2,1)S(1)} %get-tuple-element.16), channel_id=1, source_target_pairs={{0,256},{256,0},{1,257},{257,1},{2,258},{258,2},{3,259},{259,3},{4... | collective-permute-start | bytes 393224 | tf_op jit(solution)/shard_map/ppermute | solution.py:412
  34.9 6.7 %copy-start.4 = (bf16[256,32]{0,1:T(8,128)(2,1)S(1)}, bf16[256,32]{0,1:T(8,128)(2,1)}, u32[]{:S(2)}) copy-start(bf16[256,32]{0,1:T(8,128)(2,1)} %param.23) | copy-start | bytes 49156
  34.9 6.7 %copy-start.9 = (bf16[256,256]{1,0:T(8,128)(2,1)S(1)}, bf16[256,256]{1,0:T(8,128)(2,1)}, u32[]{:S(2)}) copy-start(bf16[256,256]{1,0:T(8,128)(2,1)} %constant.32.clone.tap_hi) | copy-start | bytes 393220
  34.9 6.7 %copy-start.10 = (bf16[256,256]{1,0:T(8,128)(2,1)S(1)}, bf16[256,256]{1,0:T(8,128)(2,1)}, u32[]{:S(2)}) copy-start(bf16[256,256]{1,0:T(8,128)(2,1)} %constant.33.clone.tap_lo) | copy-start | bytes 393220
  34.9 6.7 %copy-start.15 = (bf16[128,256]{1,0:T(8,128)(2,1)S(1)}, bf16[128,256]{1,0:T(8,128)(2,1)}, u32[]{:S(2)}) copy-start(bf16[128,256]{1,0:T(8,128)(2,1)} %constant.26.clone.fwd_hi) | copy-start | bytes 196612
  35.0 6.6 %collective-permute-start.1 = (bf16[256,128]{1,0:T(8,128)(2,1)S(1)}, bf16[256,128]{1,0:T(8,128)(2,1)S(1)}, u32[]{:S(2)}, u32[]{:S(2)}) collective-permute-start(bf16[256,128]{1,0:T(8,128)(2,1)S(1)} %get-tuple-element.18), channel_id=1, source_target_pairs={{0,128},{8,136},{16,144},{24,152},{32,160},{40,168},{48,176},{56,1... | collective-permute-start | bytes 196616 | tf_op jit(solution)/shard_map/ppermute | solution.py:426
  43.7 30.8 %all-to-all-start.1 = ((bf16[32,40,128]{2,1,0:T(8,128)(2,1)}), bf16[32,40,128]{2,1,0:T(8,128)(2,1)S(1)}, u32[]{:S(2)}, u32[]{:S(2)}) async-start(bf16[32,40,128]{2,1,0:T(8,128)(2,1)} %pair.1), calls=%async_computation.1 | async-start | bytes 655360 | tf_op jit(solution)/shard_map/all_to_all | solution.py:373
  57.8 6.9 %collective-permute-start.2 = (bf16[256,128]{1,0:T(8,128)(2,1)S(1)}, bf16[256,128]{1,0:T(8,128)(2,1)S(1)}, u32[]{:S(2)}, u32[]{:S(2)}) collective-permute-start(bf16[256,128]{1,0:T(8,128)(2,1)S(1)} %get-tuple-element.25.own_ref), channel_id=1, source_target_pairs={{0,128},{8,136},{16,144},{24,152},{32,160},{40,168},{48,176},{56,1... | collective-permute-start | bytes 196616 | tf_op jit(solution)/shard_map/ppermute | solution.py:440
  64.8 5.1 %copy-start.7 = (bf16[256,256]{1,0:T(8,128)(2,1)S(1)}, bf16[256,256]{1,0:T(8,128)(2,1)}, u32[]{:S(2)}) copy-start(bf16[256,256]{1,0:T(8,128)(2,1)} %constant.34.clone.lag_hi) | copy-start | bytes 393220
  64.8 5.1 %copy-start.8 = (bf16[256,256]{1,0:T(8,128)(2,1)S(1)}, bf16[256,256]{1,0:T(8,128)(2,1)}, u32[]{:S(2)}) copy-start(bf16[256,256]{1,0:T(8,128)(2,1)} %constant.35.clone.lag_lo) | copy-start | bytes 393220
  64.8 6.1 %collective-permute-start.3 = (bf16[2,256,128]{2,1,0:T(8,128)(2,1)S(1)}, bf16[2,256,128]{2,1,0:T(8,128)(2,1)S(1)}, u32[]{:S(2)}, u32[]{:S(2)}) collective-permute-start(bf16[2,256,128]{2,1,0:T(8,128)(2,1)S(1)} %pad_maximum_fusion), channel_id=1, source_target_pairs={{0,256},{256,0},{1,257},{257,1},{2,258},{258,2},{3,259},{259,3},{4... | collective-permute-start | bytes 393224 | tf_op jit(solution)/shard_map/ppermute | solution.py:441
  74.7 3.8 %collective-permute-start.4 = (f32[32,256]{1,0:T(8,128)S(1)}, f32[32,256]{1,0:T(8,128)S(1)}, u32[]{:S(2)}, u32[]{:S(2)}) collective-permute-start(f32[32,256]{1,0:T(8,128)S(1)} %taps.1.own_ref), channel_id=1, source_target_pairs={{0,256},{256,0},{1,257},{257,1},{2,258},{258,2},{3,259},{259,3},{4... | collective-permute-start | bytes 98312 | tf_op jit(solution)/shard_map/ppermute | solution.py:476

commit v4 on v3

v4 whole, which is shorter than its diff:
```python
import functools

import jax
import jax.numpy as jnp
import numpy as np
from jax import lax
from jax.experimental import pallas as pl
from jax.experimental.pallas import tpu as pltpu
from jax.sharding import PartitionSpec as P

SPAN = 128
PTS = 2 * SPAN
QUARTER = SPAN // 4
BLOCK = 256
TURN_OUT, TURN_BACK = 28, 24
F32, BF16 = jnp.float32, jnp.bfloat16


def split_bf16(matrix):
    high = matrix.astype(BF16)
    low = (matrix - high.astype(np.float64)).astype(BF16)
    return high, low


def transforms():
    freq = np.arange(SPAN)[:, None]
    point = np.arange(PTS)[None, :]
    angle = 2 * np.pi * ((freq * point) % PTS) / PTS
    real, imag = np.cos(angle), -np.sin(angle)
    imag[0] = np.where(np.arange(PTS) % 2 == 0, 1.0, -1.0)
    forward = np.concatenate([real, imag], 0)
    weight = np.full((PTS, 1), 2.0 / PTS)
    weight[0], weight[SPAN] = 1.0 / PTS, 1.0 / PTS
    inverse = (forward * weight).T
    return forward, inverse


def dot(a, b, dims=((1,), (0,))):
    return lax.dot_general(a, b, (dims, ((), ())), preferred_element_type=F32)


def halves(x):
    high = x.astype(BF16)
    return high, (x - high.astype(F32)).astype(BF16)


def spectrum_left(high, low, x):
    return dot(high, x) + dot(low, x)


def spectrum_right(x, high, low):
    return dot(x, high) + dot(x, low)


def invert_left(high, low, spec):
    s_high, s_low = halves(spec)
    return dot(high, s_high) + (dot(high, s_low) + dot(low, s_high))


def invert_right(spec, high, low):
    s_high, s_low = halves(spec)
    return dot(s_high, high) + (dot(s_low, high) + dot(s_high, low))


def multiply(ar, ai, br, bi, zero, sign):
    b_im = sign * jnp.where(zero, 0.0, bi)
    b_second = jnp.where(zero, bi, br)
    return ar * br - ai * b_im, ai * b_second + ar * b_im


def swap_blocks(parts):
    axis = parts[0].ndim - 1
    block = lax.broadcasted_iota(jnp.int32, parts[0].shape, axis) // QUARTER
    result = []
    for t in range(4):
        total = parts[t]
        for b in range(4):
            if b != t:
                moved = pltpu.roll(parts[b], (QUARTER * (b - t)) % SPAN, axis)
                total = jnp.where(block == b, moved, total)
        result.append(total)
    return result


def own_kind(slot_ref, len_ref):
    span = slot_ref[0, lax.axis_index("ctx")]

    def step(d, carry):
        pos, kind = carry
        length = len_ref[0, d]
        two = length == 2
        kind = jnp.where(two & (span == pos), 1, kind)
        kind = jnp.where(two & (span == pos + 1), 2, kind)
        return pos + length, kind

    zero = jnp.int32(0)
    return lax.fori_loop(0, len_ref.shape[1], step, (zero, zero))[1]


def send_kernel(
    slot_hbm, len_hbm, taps_hbm, q_hbm, k_hbm, v_hbm, c_hbm, out_hbm,
    slot_ref, len_ref, taps_ref, q_buf, k_buf, v_buf, c_buf, out_buf,
    small_sem, in_sem, out_sem,
):
    chunks = out_sem.shape[0]
    width = q_buf.shape[1] // chunks
    count = out_buf.shape[0] // chunks
    small = [
        pltpu.make_async_copy(src, dst, small_sem.at[i])
        for i, (src, dst) in enumerate(
            ((slot_hbm, slot_ref), (len_hbm, len_ref), (taps_hbm, taps_ref))
        )
    ]
    small[0].start()
    small[1].start()
    wide = []
    for j in range(chunks):
        cols = pl.ds(j * width, width)
        wide.append([
            pltpu.make_async_copy(src.at[:, cols], dst.at[:, cols], in_sem.at[i, j])
            for i, (src, dst) in enumerate(
                ((k_hbm, k_buf), (v_hbm, v_buf), (c_hbm, c_buf), (q_hbm, q_buf))
            )
        ])
        for copy in wide[-1]:
            copy.start()
        if j == 0:
            small[2].start()
    small[0].wait()
    small[1].wait()
    first = own_kind(slot_ref, len_ref) == 1
    small[2].wait()
    taps = taps_ref[:, 0:SPAN].astype(F32)
    quarters = swap_blocks([taps[8 * b:8 * b + 8] for b in range(4)])
    core = lax.axis_index("dp") == 0
    outs = []
    for j in range(chunks):
        for copy in wide[j]:
            copy.wait()
        cols = slice(j * width, (j + 1) * width)
        a = jnp.where(first, k_buf[:, cols].astype(F32), c_buf[:, cols].astype(F32))
        b = jnp.where(first, v_buf[:, cols].astype(F32), q_buf[:, cols].astype(F32))
        series = jnp.transpose((a * b).astype(BF16)).reshape(count, 32, SPAN)
        far = int(2 * j >= chunks)
        mine = jnp.where(core, quarters[far], quarters[2 + far]).astype(BF16)
        for piece in range(0, count, 4):
            rows = pl.ds((j * count + piece) ^ TURN_OUT, 4)
            out_buf[rows, 0:32, :] = series[piece:piece + 4]
            out_buf[rows, 32:40, :] = jnp.broadcast_to(mine[None], (4, 8, SPAN))
        rows = pl.ds((j * count) ^ (TURN_OUT // count * count), count)
        out = pltpu.make_async_copy(out_buf.at[rows], out_hbm.at[rows], out_sem.at[j])
        out.start()
        outs.append(out)
    for out in outs:
        out.wait()


def partial_kernel(
    q_ref, k_ref, v_ref, c_ref, fwd_hi, fwd_lo, inv_hi, inv_lo, give_ref
):
    blocks = q_ref.shape[1] // BLOCK
    count = BLOCK // 32
    zero = lax.broadcasted_iota(jnp.int32, (SPAN, BLOCK), 0) == 0
    for j in range(blocks):
        cols = slice(j * BLOCK, (j + 1) * BLOCK)
        x = (k_ref[:, cols].astype(F32) * v_ref[:, cols].astype(F32)).astype(BF16)
        g = (c_ref[:, cols].astype(F32) * q_ref[:, cols].astype(F32)).astype(BF16)
        xs = spectrum_left(fwd_hi[...], fwd_lo[...], x)
        gs = spectrum_left(fwd_hi[...], fwd_lo[...], g)
        pr, pi = multiply(gs[:SPAN], gs[SPAN:], xs[:SPAN], xs[SPAN:], zero, -1.0)
        taps = invert_left(inv_hi[...], inv_lo[...], jnp.concatenate([pr, pi], 0))
        rows = jnp.transpose(taps).reshape(count, 4, 8, SPAN)
        quarters = swap_blocks([rows[:, b] for b in range(4)])
        for t in range(4):
            packed = quarters[t].reshape(count * 8, SPAN).astype(BF16)
            give_ref[t, j * count * 8:(j + 1) * count * 8, :] = packed


def tables_kernel(
    slot_ref, len_ref, taps_ref, tap_hi, tap_lo, after_ref, table_ref, spec_ref, inverse_ref
):
    del after_ref
    spec_ref[...] = spectrum_right(taps_ref[...], tap_hi[...], tap_lo[...])

    def fill(r, carry):
        inverse_ref[slot_ref[0, r]] = r
        return carry

    lax.fori_loop(0, slot_ref.shape[1], fill, 0)

    def step(d, carry):
        pos, count = carry
        length = len_ref[0, d]

        @pl.when(length == 2)
        def _():
            table_ref[0, count] = inverse_ref[pos]
            table_ref[1, count] = inverse_ref[pos + 1]

        return pos + length, count + length - 1

    lax.fori_loop(0, len_ref.shape[1], step, (jnp.int32(0), jnp.int32(0)))
    table_ref[2, 0] = own_kind(slot_ref, len_ref)


def share_kernel(own_ref, other_ref, keep_ref, side_ref, next_ref, cross_ref):
    ctx = lax.axis_index("ctx")
    far, odd = ctx // 16, ctx % 2

    def total(t):
        return own_ref[t].astype(F32) + other_ref[t].astype(F32)

    keep_ref[...] = total(2 * far + odd)
    side_ref[...] = total(2 * (1 - far) + odd).astype(BF16)
    next_ref[...] = total(2 * far + 1 - odd).astype(BF16)
    cross_ref[...] = total(2 * (1 - far) + 1 - odd).astype(BF16)


def pair_spectra(table_ref, got_ref, fwd_hi, fwd_lo):
    pairs = table_ref.shape[1]
    rows = [got_ref[table_ref[k, p] ^ TURN_OUT, 0:32, :] for k in range(2) for p in range(pairs)]
    spec = spectrum_right(jnp.concatenate(rows, 0), fwd_hi[...], fwd_lo[...])
    return spec.reshape(2, pairs, 32, PTS)


def pair_kernel(
    table_ref, got_ref, spec_ref, keep_ref, side_ref, next_ref, cross_ref,
    fwd_hi, fwd_lo, inv_hi, inv_lo, out_ref,
):
    slots, pairs = got_ref.shape[0], table_ref.shape[1]
    hr, hi = spec_ref[:, :SPAN], spec_ref[:, SPAN:]
    zero = lax.broadcasted_iota(jnp.int32, hr.shape, 1) == 0
    spec = pair_spectra(table_ref, got_ref, fwd_hi, fwd_lo)
    out_ref[:, 0:32, :] = jnp.zeros((slots, 32, SPAN), BF16)
    for k in range(2):
        sr, si = spec[k, :, :, :SPAN], spec[k, :, :, SPAN:]
        pr, pi = multiply(sr, si, hr[None], hi[None], zero[None], 1.0 if k == 0 else -1.0)
        both = jnp.concatenate([pr, pi], 2).reshape(pairs * 32, PTS)
        result = invert_right(both, inv_hi[...], inv_lo[...]).astype(BF16)
        for p in range(pairs):
            out_ref[table_ref[1 - k, p] ^ TURN_BACK, 0:32, :] = result[32 * p:32 * p + 32]
    near = keep_ref[...] + side_ref[...].astype(F32)
    near = (near + (next_ref[...].astype(F32) + cross_ref[...].astype(F32))).astype(BF16)
    near = near.reshape(slots, 8, SPAN)
    for j in range(slots // 8):
        place = 8 * (j ^ (TURN_BACK // 8))
        out_ref[place:place + 8, 32:40, :] = near[8 * j:8 * j + 8]


def pair_taps_kernel(table_ref, got_ref, fwd_hi, fwd_lo, lag_hi, lag_lo, out_ref):
    spec = pair_spectra(table_ref, got_ref, fwd_hi, fwd_lo)
    zero = lax.broadcasted_iota(jnp.int32, (1, 32, SPAN), 2) == 0
    xs, gs = spec[0], spec[1]
    tr, ti = multiply(
        gs[:, :, :SPAN], gs[:, :, SPAN:], xs[:, :, :SPAN], xs[:, :, SPAN:], zero, -1.0
    )
    both = jnp.concatenate([jnp.sum(tr, 0), jnp.sum(ti, 0)], 1)
    taps = invert_right(both, lag_hi[...], lag_lo[...]).astype(BF16)
    out_ref[0:32, :] = taps[:, :SPAN]
    out_ref[32:64, :] = taps[:, SPAN:]


def local_kernel(
    own_ref, core_ref, q_ref, k_ref, v_ref, c_ref, fwd_hi, fwd_lo, inv_hi, inv_lo,
    mixed_ref, series_ref,
):
    blocks = q_ref.shape[1] // BLOCK
    count = BLOCK // 32
    dp, far = lax.axis_index("dp"), lax.axis_index("ctx") // 16
    zero = lax.broadcasted_iota(jnp.int32, (SPAN, BLOCK), 0) == 0
    nt = ((1,), (1,))
    for j in range(blocks):
        cols = slice(j * BLOCK, (j + 1) * BLOCK)
        x = (k_ref[:, cols].astype(F32) * v_ref[:, cols].astype(F32)).astype(BF16)
        g = (c_ref[:, cols].astype(F32) * q_ref[:, cols].astype(F32)).astype(BF16)
        xs = spectrum_left(fwd_hi[...], fwd_lo[...], x)
        gs = spectrum_left(fwd_hi[...], fwd_lo[...], g)

        def rows(ref, start):
            places = [start + 32 * (b ^ (TURN_OUT // 4)) for b in (2 * j, 2 * j + 1)]
            return jnp.concatenate([ref[p:p + 32, :].astype(F32) for p in places], 0)

        own, side = rows(own_ref, 0), rows(own_ref, 256)
        core, cross = rows(core_ref, 0), rows(core_ref, 256)
        quarters = []
        for t in range(4):
            here = jnp.where(far == t % 2, own, side)
            there = jnp.where(far == t % 2, core, cross)
            quarters.append(jnp.where(dp == t // 2, here, there).reshape(count, 8, SPAN))
        taps = jnp.concatenate(swap_blocks(quarters), 1).reshape(BLOCK, SPAN).astype(BF16)
        hs = dot(fwd_hi[...], taps, nt) + dot(fwd_lo[...], taps, nt)
        hr, hi = hs[:SPAN], hs[SPAN:]
        mr, mi = multiply(xs[:SPAN], xs[SPAN:], hr, hi, zero, 1.0)
        spec = jnp.concatenate([mr, mi], 0)
        mixed_ref[:, cols] = invert_left(inv_hi[...], inv_lo[...], spec)
        sr, si = multiply(gs[:SPAN], gs[SPAN:], hr, hi, zero, -1.0)
        spec = jnp.concatenate([sr, si], 0)
        series_ref[:, cols] = invert_left(inv_hi[...], inv_lo[...], spec)


def finish_kernel(
    scale, table_ref, got_ref, mixed_ref, series_ref, k_ref, v_ref, c_ref, own_ref, core_ref,
    gq_ref, gk_ref, gv_ref, gf_ref, q_buf, k_buf, v_buf, f_buf, sems, f_sem,
):
    chunks = sems.shape[1]
    width = q_buf.shape[1] // chunks
    slots = got_ref.shape[0]
    count = slots // chunks
    kind = table_ref[2, 0]
    copies = []

    def filter_taps():
        quarters = []
        for t in range(4):
            sources = [s ^ TURN_BACK for s in range(slots) if 2 * (s // 16) + s % 2 == t]
            quarters.append(sum(got_ref[s, 32:40, :].astype(F32) for s in sources))
        near = jnp.concatenate(swap_blocks(quarters), 0)
        pair = own_ref[512:576, :].astype(F32) + core_ref[512:576, :].astype(F32)
        f_buf[:, :SPAN] = ((near + pair[:32]) * scale).astype(BF16)
        f_buf[:, SPAN:] = (pair[32:] * scale).astype(BF16)
        copy = pltpu.make_async_copy(f_buf, gf_ref, f_sem.at[0])
        copy.start()
        copies.append(copy)

    for j in range(chunks):
        cols = slice(j * width, (j + 1) * width)
        place = (j ^ (TURN_BACK // count)) * count
        rows = got_ref[place:place + count, 0:32, :].reshape(width, SPAN)
        pair = jnp.transpose(rows).astype(F32)
        mixed = mixed_ref[:, cols] + jnp.where(kind == 2, pair, 0.0)
        series = series_ref[:, cols] + jnp.where(kind == 1, pair, 0.0)
        mixed = mixed.astype(BF16).astype(F32)
        series = series.astype(BF16).astype(F32)
        q_buf[:, cols] = (c_ref[:, cols].astype(F32) * mixed).astype(BF16)
        k_buf[:, cols] = (series * v_ref[:, cols].astype(F32)).astype(BF16)
        v_buf[:, cols] = (series * k_ref[:, cols].astype(F32)).astype(BF16)
        for i, (buf, ref) in enumerate(((q_buf, gq_ref), (k_buf, gk_ref), (v_buf, gv_ref))):
            copy = pltpu.make_async_copy(buf.at[:, cols], ref.at[:, cols], sems.at[i, j])
            copy.start()
            copies.append(copy)
        if j == 1:
            filter_taps()
    for copy in copies:
        copy.wait()


SMEM = pl.BlockSpec(memory_space=pltpu.SMEM)
VMEM = pl.BlockSpec(memory_space=pltpu.VMEM)
HBM = pl.BlockSpec(memory_space=pltpu.HBM)
ANY = pl.BlockSpec(memory_space=pl.ANY)
DMA = pltpu.SemaphoreType.DMA


def params(mebibytes=32):
    return pltpu.CompilerParams(vmem_limit_bytes=mebibytes * 1024 * 1024)


def cost(flops, moved):
    return pl.CostEstimate(flops=int(flops), bytes_accessed=int(moved), transcendentals=0)


def per_device(query, key, value, cotangent, filter_taps, span_slot, doc_lengths):
    parts = lax.axis_size("ctx")
    tokens, width = query.shape
    area = tokens * width
    pairs = parts - doc_lengths.shape[1]
    scale = float(tokens * parts * lax.axis_size("dp")) ** (-0.5)
    forward, inverse = transforms()

    def constant(matrix):
        return [jnp.asarray(m) for m in split_bf16(matrix)]

    fwd = constant(forward[:, :SPAN])
    fwd_t = constant(forward[:, :SPAN].T)
    inv = constant(inverse[:SPAN])
    inv_t = constant(inverse[:SPAN].T)
    tap_t = constant(np.roll(forward, -SPAN, 1).T)
    lag_t = constant(np.roll(inverse, SPAN, 0).T)
    core_swap = [(0, 1), (1, 0)]
    side_swap = [(c, c ^ 16) for c in range(parts)]
    cross_swap = [(c, c ^ 17) for c in range(parts)]
    next_swap = [(c, c ^ 1) for c in range(parts)]
    steps = width // BLOCK
    taps_rows = filter_taps.T

    def exchange(array, turn):
        order = [[k ^ turn for k in range(parts)]]
        return lax.all_to_all(
            array, "ctx", split_axis=0, concat_axis=0, axis_index_groups=order, tiled=True
        )

    chunk = jax.ShapeDtypeStruct((parts, 40, SPAN), BF16)
    out = pl.pallas_call(
        send_kernel,
        out_shape=chunk,
        in_specs=[HBM] * 7,
        out_specs=HBM,
        scratch_shapes=[
            pltpu.SMEM(span_slot.shape, jnp.int32),
            pltpu.SMEM(doc_lengths.shape, jnp.int32),
            pltpu.VMEM(taps_rows.shape, BF16),
        ] + [pltpu.VMEM((tokens, width), BF16)] * 4 + [
            pltpu.VMEM(chunk.shape, BF16), DMA((3,)), DMA((4, 2)), DMA((2,)),
        ],
        compiler_params=params(60),
        cost_estimate=cost(2 * area, 8 * area),
        name="send",
    )(span_slot, doc_lengths, taps_rows, query, key, value, cotangent)
    got = exchange(out, TURN_OUT)

    give = pl.pallas_call(
        partial_kernel,
        out_shape=jax.ShapeDtypeStruct((4, parts * 8, SPAN), BF16),
        in_specs=[VMEM] * 8,
        out_specs=VMEM,
        compiler_params=params(),
        cost_estimate=cost(2e9, 10 * area),
        name="partial_taps",
    )(query, key, value, cotangent, *fwd, *inv)
    taken = lax.ppermute(give, "dp", core_swap)
    quarter = jax.ShapeDtypeStruct((parts * 8, SPAN), BF16)
    keep, side, near, cross = pl.pallas_call(
        share_kernel,
        out_shape=(jax.ShapeDtypeStruct(quarter.shape, F32), quarter, quarter, quarter),
        in_specs=[VMEM, VMEM],
        out_specs=(VMEM,) * 4,
        compiler_params=params(),
        cost_estimate=cost(area, 3 * area),
        name="share",
    )(give, taken)
    table, tap_spec = pl.pallas_call(
        tables_kernel,
        out_shape=(
            jax.ShapeDtypeStruct((3, pairs), jnp.int32),
            jax.ShapeDtypeStruct((32, PTS), F32),
        ),
        in_specs=[SMEM, SMEM, VMEM, VMEM, VMEM, ANY],
        out_specs=(SMEM, VMEM),
        scratch_shapes=[pltpu.SMEM((parts,), jnp.int32)],
        compiler_params=params(),
        cost_estimate=cost(area, area),
        name="tables",
    )(span_slot, doc_lengths, taps_rows, *tap_t, cross)
    side = lax.ppermute(side, "ctx", side_swap)
    near = lax.ppermute(near, "ctx", next_swap)
    cross = lax.ppermute(cross, "ctx", cross_swap)

    back = pl.pallas_call(
        pair_kernel,
        out_shape=chunk,
        in_specs=[SMEM] + [VMEM] * 10,
        out_specs=VMEM,
        compiler_params=params(),
        cost_estimate=cost(1e9, 8 * area),
        name="pair",
    )(table, got, tap_spec, keep, side, near, cross, *fwd_t, *inv_t)
    landed = exchange(back, TURN_BACK)

    own = got[:, 32:40, :].reshape(parts * 8, SPAN)
    pair_taps = pl.pallas_call(
        pair_taps_kernel,
        out_shape=jax.ShapeDtypeStruct((64, SPAN), BF16),
        in_specs=[SMEM] + [VMEM] * 5,
        out_specs=VMEM,
        compiler_params=params(),
        cost_estimate=cost(1e9, 6 * area),
        name="pair_taps",
    )(table, got, *fwd_t, *lag_t)
    own = jnp.concatenate([own, lax.ppermute(own, "ctx", side_swap), pair_taps], 0)
    core = lax.ppermute(own, "dp", core_swap)
    mixed, series = pl.pallas_call(
        local_kernel,
        out_shape=(jax.ShapeDtypeStruct((tokens, width), F32),) * 2,
        in_specs=[VMEM] * 10,
        out_specs=(VMEM, VMEM),
        compiler_params=params(),
        cost_estimate=cost(3e9, 20 * area),
        name="local",
    )(own, core, query, key, value, cotangent, *fwd, *inv)

    result = jax.ShapeDtypeStruct((tokens, width), BF16)
    *grads, grad_filter = pl.pallas_call(
        functools.partial(finish_kernel, scale),
        out_shape=(result,) * 3 + (jax.ShapeDtypeStruct((32, PTS), BF16),),
        in_specs=[SMEM] + [VMEM] * 8,
        out_specs=(HBM,) * 4,
        scratch_shapes=[pltpu.VMEM((tokens, width), BF16)] * 3
        + [pltpu.VMEM((32, PTS), BF16), DMA((3, steps)), DMA((1,))],
        compiler_params=params(),
        cost_estimate=cost(10 * area, 20 * area),
        name="finish",
    )(table, landed, mixed, series, key, value, cotangent, own, core)
    return (*grads, grad_filter.T)


def solution(mesh):
    return jax.shard_map(
        per_device,
        mesh=mesh,
        in_specs=(
            P(("dp", "ctx"), "ch"),
            P(("dp", "ctx"), "ch"),
            P(("dp", "ctx"), "ch"),
            P(("dp", "ctx"), "ch"),
            P(None, ("ch", "ctx")),
            P("dp", None),
            P("dp", None),
        ),
        out_specs=(
            P(("dp", "ctx"), "ch"),
            P(("dp", "ctx"), "ch"),
            P(("dp", "ctx"), "ch"),
            P(None, ("ch", "ctx")),
        ),
        check_vma=False,
    )
```

time: 79.6 us -> 75.6 us (0.950)
  Pallas kernels: 17.2 us -> 13.2 us
  waiting for transfers between devices: 10.1 us -> 7.39 us
  starting transfers between devices: 50.7 us -> 53.3 us
    ppermute x4 -> x5, starting transfers between devices: 11.6 us -> 17.1 us  [the longest x1 4.81 us: per_device(): core = lax.ppermute(own, 'dp', core_swap)]
    pallas_call x7 -> x6, Pallas kernels: 12.6 us -> 8.85 us  [the longest x1 2.17 us: per_device(): pl.pallas_call(local_kernel, out_shape=(jax.ShapeDtypeStruct((tokens, wid...]
    all_to_all x2, starting transfers between devices: 36 us -> 32.9 us  [exchange(): lax.all_to_all(array, 'ctx', split_axis=0, concat_axis=0, axis_index_grou...]
    ppermute x4 -> x5, waiting for transfers between devices: 9.13 us -> 6.25 us  [the longest x1 3.68 us: per_device(): lax.ppermute(own, 'ctx', side_swap)]
  transfers between devices with their start and end apart: 7 -> 8, of which waited for: 3 -> 4; matrix products, arithmetic and copies ran while one was open for 0% -> 0% of each run, Pallas kernels for 15% -> 10%
where the time goes in v4:
time: 75.6 us; the launch traced here: 75 us
  starting transfers between devices  53.3 us (71%)
  Pallas kernels  13.2 us (17%)
  waiting for transfers between devices  7.39 us (10%)
  between operations  1.04 us (1%)
    all_to_all x2, starting transfers between devices, exchange(): lax.all_to_all(array, 'ctx', split_axis=0, concat_axis=0, axis_index_grou...  32.9 us
    ppermute x1, starting transfers between devices, per_device(): core = lax.ppermute(own, 'dp', core_swap)  4.81 us
    ppermute x1, starting transfers between devices, per_device(): cross = lax.ppermute(cross, 'ctx', cross_swap)  4.8 us
    ppermute x1, waiting for transfers between devices, per_device(): lax.ppermute(own, 'ctx', side_swap)  3.68 us
    ppermute x1, starting transfers between devices, per_device(): taken = lax.ppermute(give, 'dp', core_swap)  3.27 us
    ppermute x1, starting transfers between devices, per_device(): near = lax.ppermute(near, 'ctx', next_swap)  3.09 us
    ppermute x1, starting transfers between devices, per_device(): lax.ppermute(own, 'ctx', side_swap)  2.28 us
    pallas_call x1, Pallas kernels, per_device(): pl.pallas_call(send_kernel, out_shape=chunk, in_specs=[HBM] * 7, out_spec...  2.26 us
  transfers between devices with their start and end apart: 8, of which 4 were waited for; matrix products, arithmetic and copies ran while one was open for 0% of the time, Pallas kernels for 10%

profile of v4, /device:TPU:1, one launch (start us, length us, event | category | flops | bytes accessed | tf_op | source)
XLA Modules:
  0.0 75.0 jit_solution(11668941341635096984)
XLA Ops:
  0.6 0.0 copy-start.2
  0.6 0.0 copy-start.3
  0.7 0.0 copy-start.13
  0.7 0.0 copy-start.14
  0.7 2.3 %send.1 = bf16[32,40,128]{2,1,0:T(8,128)(2,1)} custom-call(s32[1,32]{1,0:T(1,128)} %slot_hbm.1, s32[1,24]{1,0:T(1,128)} %len_hbm.1, bf16[32,256]{1,0:T(8,128)(2,1)} %bitcast.4, bf16[128,1024]{1,0:T(8,128)(2,1)} %q_ref.3, bf16[128,1024]{1,0:T(8,128)(2,1)} %k_ref.5, bf16[128,1024]{1,0:T(8,128)(2,1)} %v_ref.5, bf16[128,1024]{1,0:T(8,128)(2,1)} %c_ref.5), custom_call_target="tpu_custom_call" | custom-call | flops 262144 | bytes 1048576 | tf_op jit(solution)/shard_map/send/pallas_call | solution.py:393
  2.9 0.0 copy-start
  3.0 0.0 copy-start.1
  3.0 0.0 copy-start.11
  3.0 0.0 copy-start.12
  3.0 18.8 %all-to-all-start = ((bf16[32,40,128]{2,1,0:T(8,128)(2,1)}), bf16[32,40,128]{2,1,0:T(8,128)(2,1)S(1)}, u32[]{:S(2)}, u32[]{:S(2)}) async-start(bf16[32,40,128]{2,1,0:T(8,128)(2,1)} %send.1), calls=%async_computation | async-start | bytes 655360 | tf_op jit(solution)/shard_map/all_to_all | solution.py:388
  21.8 0.0 copy-done.2
  21.8 0.0 copy-done.3
  21.8 0.0 copy-done.13
  21.8 0.0 copy-done.14
  21.8 0.0 copy-done
  21.8 0.0 copy-done.1
  21.8 1.9 %partial_taps.1.own_ref = bf16[4,256,128]{2,1,0:T(8,128)(2,1)S(1)} custom-call(bf16[128,1024]{1,0:T(8,128)(2,1)S(1)} %copy-done.3, bf16[128,1024]{1,0:T(8,128)(2,1)S(1)} %copy-done, bf16[128,1024]{1,0:T(8,128)(2,1)S(1)} %copy-done.1, bf16[128,1024]{1,0:T(8,128)(2,1)S(1)} %copy-done.2, bf16[256,128]{1,0:T(8,128)(2,1)S(1)} %copy-done.14, ...), custom_call_target="tpu_custom_call" | custom-call | flops 2000000000 | bytes 1310720 | tf_op jit(solution)/shard_map/partial_taps/pallas_call | solution.py:411
  23.7 0.0 copy-start.4
  23.8 0.0 copy-start.5
  23.8 3.3 %collective-permute-start = (bf16[4,256,128]{2,1,0:T(8,128)(2,1)S(1)}, bf16[4,256,128]{2,1,0:T(8,128)(2,1)S(1)}, u32[]{:S(2)}, u32[]{:S(2)}) collective-permute-start(bf16[4,256,128]{2,1,0:T(8,128)(2,1)S(1)} %partial_taps.1.own_ref), channel_id=1, source_target_pairs={{0,256},{256,0},{1,257},{257,1},{2,258},{258,2},{3,259},{259,3},{4... | collective-permute-start | bytes 786440 | tf_op jit(solution)/shard_map/ppermute | solution.py:420
  27.1 1.1 %collective-permute-done.other_ref = bf16[4,256,128]{2,1,0:T(8,128)(2,1)S(1)} collective-permute-done((bf16[4,256,128]{2,1,0:T(8,128)(2,1)S(1)}, bf16[4,256,128]{2,1,0:T(8,128)(2,1)S(1)}, u32[]{:S(2)}, u32[]{:S(2)}) %collective-permute-start) | collective-permute-done | bytes 262176 | tf_op jit(solution)/shard_map/ppermute | solution.py:420
  28.2 0.1 share.1
  28.3 2.1 %collective-permute-start.1 = (bf16[256,128]{1,0:T(8,128)(2,1)S(1)}, bf16[256,128]{1,0:T(8,128)(2,1)S(1)}, u32[]{:S(2)}, u32[]{:S(2)}) collective-permute-start(bf16[256,128]{1,0:T(8,128)(2,1)S(1)} %get-tuple-element.20), channel_id=1, source_target_pairs={{0,128},{8,136},{16,144},{24,152},{32,160},{40,168},{48,176},{56,1... | collective-permute-start | bytes 196616 | tf_op jit(solution)/shard_map/ppermute | solution.py:444
  30.4 0.0 copy-start.7
  30.4 0.0 copy-start.8
  30.4 3.1 %collective-permute-start.2 = (bf16[256,128]{1,0:T(8,128)(2,1)S(1)}, bf16[256,128]{1,0:T(8,128)(2,1)S(1)}, u32[]{:S(2)}, u32[]{:S(2)}) collective-permute-start(bf16[256,128]{1,0:T(8,128)(2,1)S(1)} %get-tuple-element.21), channel_id=1, source_target_pairs={{0,8},{8,0},{16,24},{24,16},{32,40},{40,32},{48,56},{56,48},{64,72... | collective-permute-start | bytes 196616 | tf_op jit(solution)/shard_map/ppermute | solution.py:445
  33.5 0.0 copy-start.15
  33.5 0.0 copy-start.16
  33.5 0.0 copy-start.17
  33.5 0.0 copy-start.18
  33.6 4.8 %collective-permute-start.3 = (bf16[256,128]{1,0:T(8,128)(2,1)S(1)}, bf16[256,128]{1,0:T(8,128)(2,1)S(1)}, u32[]{:S(2)}, u32[]{:S(2)}) collective-permute-start(bf16[256,128]{1,0:T(8,128)(2,1)S(1)} %get-tuple-element.16.after_ref), channel_id=1, source_target_pairs={{0,136},{8,128},{16,152},{24,144},{32,168},{40,160},{48,184},{56,1... | collective-permute-start | bytes 196616 | tf_op jit(solution)/shard_map/ppermute | solution.py:446
  38.4 1.9 %tables.1 = (s32[3,8]{1,0:T(4,128)S(1)}, f32[32,256]{1,0:T(8,128)S(1)}) custom-call(s32[1,32]{1,0:T(1,128)S(1)} %copy-done.7, s32[1,24]{1,0:T(1,128)S(1)} %copy-done.8, bf16[32,256]{1,0:T(8,128)(2,1)S(1)} %bitcast.5, bf16[256,256]{1,0:T(8,128)(2,1)S(1)} %copy-done.5, bf16[256,256]{1,0:T(8,128)(2,1)S(1)} %copy-done.4, ...), custom_call_target="tpu_custom_call" | custom-call | flops 131072 | bytes 131072 | tf_op jit(solution)/shard_map/tables/pallas_call | solution.py:431
  40.4 0.0 collective-permute-done.1.side_ref
  40.4 0.0 collective-permute-done.2.next_ref
  40.4 1.6 %collective-permute-done.3.cross_ref = bf16[256,128]{1,0:T(8,128)(2,1)S(1)} collective-permute-done((bf16[256,128]{1,0:T(8,128)(2,1)S(1)}, bf16[256,128]{1,0:T(8,128)(2,1)S(1)}, u32[]{:S(2)}, u32[]{:S(2)}) %collective-permute-start.3) | collective-permute-done | bytes 65568 | tf_op jit(solution)/shard_map/ppermute | solution.py:446
  42.0 0.0 all-to-all-done.got_ref
  42.0 0.0 copy-done.15
  42.0 2.0 %pair.1 = bf16[32,40,128]{2,1,0:T(8,128)(2,1)} custom-call(s32[3,8]{1,0:T(4,128)S(1)} %get-tuple-element.17.table_ref, bf16[32,40,128]{2,1,0:T(8,128)(2,1)S(1)} %all-to-all-done.got_ref, f32[32,256]{1,0:T(8,128)S(1)} %get-tuple-element.18.spec_ref, f32[256,128]{1,0:T(8,128)S(1)} %get-tuple-element.19.keep_ref, ...), custom_call_target="tpu_custom_call" | custom-call | flops 1000000000 | bytes 1048576 | tf_op jit(solution)/shard_map/pair/pallas_call | solution.py:448
  44.0 14.2 %all-to-all-start.1 = ((bf16[32,40,128]{2,1,0:T(8,128)(2,1)}), bf16[32,40,128]{2,1,0:T(8,128)(2,1)S(1)}, u32[]{:S(2)}, u32[]{:S(2)}) async-start(bf16[32,40,128]{2,1,0:T(8,128)(2,1)} %pair.1), calls=%async_computation.1 | async-start | bytes 655360 | tf_op jit(solution)/shard_map/all_to_all | solution.py:388
  58.2 0.0 copy-start.9
  58.3 2.3 %collective-permute-start.4 = (bf16[256,128]{1,0:T(8,128)(2,1)S(1)}, bf16[256,128]{1,0:T(8,128)(2,1)S(1)}, u32[]{:S(2)}, u32[]{:S(2)}) collective-permute-start(bf16[256,128]{1,0:T(8,128)(2,1)S(1)} %slice_bitcast_fusion), channel_id=1, source_target_pairs={{0,128},{8,136},{16,144},{24,152},{32,160},{40,168},{48,176},{56,1... | collective-permute-start | bytes 196616 | tf_op jit(solution)/shard_map/ppermute | solution.py:469
  60.6 1.1 %pair_taps.1 = bf16[64,128]{1,0:T(8,128)(2,1)S(1)} custom-call(s32[3,8]{1,0:T(4,128)S(1)} %get-tuple-element.17.table_ref, bf16[32,40,128]{2,1,0:T(8,128)(2,1)S(1)} %all-to-all-done.got_ref, bf16[128,256]{1,0:T(8,128)(2,1)S(1)} %copy-done.16, bf16[128,256]{1,0:T(8,128)(2,1)S(1)} %copy-done.15, bf16[256,256]{1,0:T(8,128)(2,1)S(1)} %copy-done.10, ...), custom_call_target="tpu_custom_call" | custom-call | flops 1000000000 | bytes 786432 | tf_op jit(solution)/shard_map/pair_taps/pallas_call | solution.py:460
  61.6 3.7 %collective-permute-done.4 = bf16[256,128]{1,0:T(8,128)(2,1)S(1)} collective-permute-done((bf16[256,128]{1,0:T(8,128)(2,1)S(1)}, bf16[256,128]{1,0:T(8,128)(2,1)S(1)}, u32[]{:S(2)}, u32[]{:S(2)}) %collective-permute-start.4) | collective-permute-done | bytes 65568 | tf_op jit(solution)/shard_map/ppermute | solution.py:469
  65.3 4.8 %collective-permute-start.5 = (bf16[576,128]{1,0:T(8,128)(2,1)S(1)}, bf16[576,128]{1,0:T(8,128)(2,1)S(1)}, u32[]{:S(2)}, u32[]{:S(2)}) collective-permute-start(bf16[576,128]{1,0:T(8,128)(2,1)S(1)} %pad_maximum_fusion.own_ref), channel_id=1, source_target_pairs={{0,256},{256,0},{1,257},{257,1},{2,258},{258,2},{3,259},{259,3},{4... | collective-permute-start | bytes 442376 | tf_op jit(solution)/shard_map/ppermute | solution.py:470
  70.1 1.0 %collective-permute-done.5.core_ref = bf16[576,128]{1,0:T(8,128)(2,1)S(1)} collective-permute-done((bf16[576,128]{1,0:T(8,128)(2,1)S(1)}, bf16[576,128]{1,0:T(8,128)(2,1)S(1)}, u32[]{:S(2)}, u32[]{:S(2)}) %collective-permute-start.5) | collective-permute-done | bytes 147488 | tf_op jit(solution)/shard_map/ppermute | solution.py:470
  71.1 2.2 %local.1 = (f32[128,1024]{1,0:T(8,128)S(1)}, f32[128,1024]{1,0:T(8,128)S(1)}) custom-call(bf16[576,128]{1,0:T(8,128)(2,1)S(1)} %pad_maximum_fusion.own_ref, bf16[576,128]{1,0:T(8,128)(2,1)S(1)} %collective-permute-done.5.core_ref, bf16[128,1024]{1,0:T(8,128)(2,1)S(1)} %copy-done.3, bf16[128,1024]{1,0:T(8,128)(2,1)S(1)} %copy-done, ...), custom_call_target="tpu_custom_call" | custom-call | flops 3000000000 | bytes 2621440 | tf_op jit(solution)/shard_map/local/pallas_call | solution.py:471
  73.3 0.0 all-to-all-done.1.got_ref
  73.3 1.7 %finish.1 = (bf16[128,1024]{1,0:T(8,128)(2,1)}, bf16[128,1024]{1,0:T(8,128)(2,1)}, bf16[128,1024]{1,0:T(8,128)(2,1)}, bf16[32,256]{1,0:T(8,128)(2,1)}) custom-call(s32[3,8]{1,0:T(4,128)S(1)} %get-tuple-element.17.table_ref, bf16[32,40,128]{2,1,0:T(8,128)(2,1)S(1)} %all-to-all-done.1.got_ref, f32[128,1024]{1,0:T(8,128)S(1)} %get-tuple-element.22.mixed_ref, ...), custom_call_target="tpu_custom_call" | custom-call | flops 1310720 | bytes 2621440 | tf_op jit(solution)/shard_map/finish/pallas_call | solution.py:482
  (16 shorter events, 0.0 us)
Async XLA Ops:
  0.6 21.1 %copy-start.2 = (bf16[128,1024]{1,0:T(8,128)(2,1)S(1)}, bf16[128,1024]{1,0:T(8,128)(2,1)}, u32[]{:S(2)}) copy-start(bf16[128,1024]{1,0:T(8,128)(2,1)} %c_ref.5) | copy-start | bytes 786436
  0.6 21.1 %copy-start.3 = (bf16[128,1024]{1,0:T(8,128)(2,1)S(1)}, bf16[128,1024]{1,0:T(8,128)(2,1)}, u32[]{:S(2)}) copy-start(bf16[128,1024]{1,0:T(8,128)(2,1)} %q_ref.3) | copy-start | bytes 786436
  0.7 21.1 %copy-start.13 = (bf16[256,128]{1,0:T(8,128)(2,1)S(1)}, bf16[256,128]{1,0:T(8,128)(2,1)}, u32[]{:S(2)}) copy-start(bf16[256,128]{1,0:T(8,128)(2,1)} %constant.25.clone.fwd_lo) | copy-start | bytes 196612
  0.7 21.1 %copy-start.14 = (bf16[256,128]{1,0:T(8,128)(2,1)S(1)}, bf16[256,128]{1,0:T(8,128)(2,1)}, u32[]{:S(2)}) copy-start(bf16[256,128]{1,0:T(8,128)(2,1)} %constant.24.clone.fwd_hi) | copy-start | bytes 196612
  2.9 18.9 %copy-start = (bf16[128,1024]{1,0:T(8,128)(2,1)S(1)}, bf16[128,1024]{1,0:T(8,128)(2,1)}, u32[]{:S(2)}) copy-start(bf16[128,1024]{1,0:T(8,128)(2,1)} %k_ref.5) | copy-start | bytes 786436
  3.0 18.8 %copy-start.1 = (bf16[128,1024]{1,0:T(8,128)(2,1)S(1)}, bf16[128,1024]{1,0:T(8,128)(2,1)}, u32[]{:S(2)}) copy-start(bf16[128,1024]{1,0:T(8,128)(2,1)} %v_ref.5) | copy-start | bytes 786436
  3.0 18.8 %copy-start.11 = (bf16[128,256]{1,0:T(8,128)(2,1)S(1)}, bf16[128,256]{1,0:T(8,128)(2,1)}, u32[]{:S(2)}) copy-start(bf16[128,256]{1,0:T(8,128)(2,1)} %constant.29.clone.inv_lo) | copy-start | bytes 196612
  3.0 18.8 %copy-start.12 = (bf16[128,256]{1,0:T(8,128)(2,1)S(1)}, bf16[128,256]{1,0:T(8,128)(2,1)}, u32[]{:S(2)}) copy-start(bf16[128,256]{1,0:T(8,128)(2,1)} %constant.28.clone.inv_hi) | copy-start | bytes 196612
  3.0 39.0 %all-to-all-start = ((bf16[32,40,128]{2,1,0:T(8,128)(2,1)}), bf16[32,40,128]{2,1,0:T(8,128)(2,1)S(1)}, u32[]{:S(2)}, u32[]{:S(2)}) async-start(bf16[32,40,128]{2,1,0:T(8,128)(2,1)} %send.1), calls=%async_computation | async-start | bytes 655360 | tf_op jit(solution)/shard_map/all_to_all | solution.py:388
  23.7 14.6 %copy-start.4 = (bf16[256,256]{1,0:T(8,128)(2,1)S(1)}, bf16[256,256]{1,0:T(8,128)(2,1)}, u32[]{:S(2)}) copy-start(bf16[256,256]{1,0:T(8,128)(2,1)} %constant.33.clone.tap_lo) | copy-start | bytes 393220
  23.8 14.6 %copy-start.5 = (bf16[256,256]{1,0:T(8,128)(2,1)S(1)}, bf16[256,256]{1,0:T(8,128)(2,1)}, u32[]{:S(2)}) copy-start(bf16[256,256]{1,0:T(8,128)(2,1)} %constant.32.clone.tap_hi) | copy-start | bytes 393220
  23.8 4.4 %collective-permute-start = (bf16[4,256,128]{2,1,0:T(8,128)(2,1)S(1)}, bf16[4,256,128]{2,1,0:T(8,128)(2,1)S(1)}, u32[]{:S(2)}, u32[]{:S(2)}) collective-permute-start(bf16[4,256,128]{2,1,0:T(8,128)(2,1)S(1)} %partial_taps.1.own_ref), channel_id=1, source_target_pairs={{0,256},{256,0},{1,257},{257,1},{2,258},{258,2},{3,259},{259,3},{4... | collective-permute-start | bytes 786440 | tf_op jit(solution)/shard_map/ppermute | solution.py:420
  28.2 10.2 %copy-start.6 = (bf16[256,32]{0,1:T(8,128)(2,1)S(1)}, bf16[256,32]{0,1:T(8,128)(2,1)}, u32[]{:S(2)}) copy-start(bf16[256,32]{0,1:T(8,128)(2,1)} %param.23) | copy-start | bytes 49156
  28.3 12.1 %collective-permute-start.1 = (bf16[256,128]{1,0:T(8,128)(2,1)S(1)}, bf16[256,128]{1,0:T(8,128)(2,1)S(1)}, u32[]{:S(2)}, u32[]{:S(2)}) collective-permute-start(bf16[256,128]{1,0:T(8,128)(2,1)S(1)} %get-tuple-element.20), channel_id=1, source_target_pairs={{0,128},{8,136},{16,144},{24,152},{32,160},{40,168},{48,176},{56,1... | collective-permute-start | bytes 196616 | tf_op jit(solution)/shard_map/ppermute | solution.py:444
  30.4 8.0 %copy-start.7 = (s32[1,32]{1,0:T(1,128)S(1)}, s32[1,32]{1,0:T(1,128)}, u32[]{:S(2)}) copy-start(s32[1,32]{1,0:T(1,128)} %slot_hbm.1) | copy-start | bytes 388
  30.4 8.0 %copy-start.8 = (s32[1,24]{1,0:T(1,128)S(1)}, s32[1,24]{1,0:T(1,128)}, u32[]{:S(2)}) copy-start(s32[1,24]{1,0:T(1,128)} %len_hbm.1) | copy-start | bytes 292
  30.4 10.0 %collective-permute-start.2 = (bf16[256,128]{1,0:T(8,128)(2,1)S(1)}, bf16[256,128]{1,0:T(8,128)(2,1)S(1)}, u32[]{:S(2)}, u32[]{:S(2)}) collective-permute-start(bf16[256,128]{1,0:T(8,128)(2,1)S(1)} %get-tuple-element.21), channel_id=1, source_target_pairs={{0,8},{8,0},{16,24},{24,16},{32,40},{40,32},{48,56},{56,48},{64,72... | collective-permute-start | bytes 196616 | tf_op jit(solution)/shard_map/ppermute | solution.py:445
  33.5 8.5 %copy-start.15 = (bf16[128,256]{1,0:T(8,128)(2,1)S(1)}, bf16[128,256]{1,0:T(8,128)(2,1)}, u32[]{:S(2)}) copy-start(bf16[128,256]{1,0:T(8,128)(2,1)} %constant.27.clone.fwd_lo) | copy-start | bytes 196612
  33.5 8.4 %copy-start.16 = (bf16[128,256]{1,0:T(8,128)(2,1)S(1)}, bf16[128,256]{1,0:T(8,128)(2,1)}, u32[]{:S(2)}) copy-start(bf16[128,256]{1,0:T(8,128)(2,1)} %constant.26.clone.fwd_hi) | copy-start | bytes 196612
  33.5 8.4 %copy-start.17 = (bf16[256,128]{1,0:T(8,128)(2,1)S(1)}, bf16[256,128]{1,0:T(8,128)(2,1)}, u32[]{:S(2)}) copy-start(bf16[256,128]{1,0:T(8,128)(2,1)} %constant.31.clone.inv_lo) | copy-start | bytes 196612
  33.5 8.4 %copy-start.18 = (bf16[256,128]{1,0:T(8,128)(2,1)S(1)}, bf16[256,128]{1,0:T(8,128)(2,1)}, u32[]{:S(2)}) copy-start(bf16[256,128]{1,0:T(8,128)(2,1)} %constant.30.clone.inv_hi) | copy-start | bytes 196612
  33.6 8.4 %collective-permute-start.3 = (bf16[256,128]{1,0:T(8,128)(2,1)S(1)}, bf16[256,128]{1,0:T(8,128)(2,1)S(1)}, u32[]{:S(2)}, u32[]{:S(2)}) collective-permute-start(bf16[256,128]{1,0:T(8,128)(2,1)S(1)} %get-tuple-element.16.after_ref), channel_id=1, source_target_pairs={{0,136},{8,128},{16,152},{24,144},{32,168},{40,160},{48,184},{56,1... | collective-permute-start | bytes 196616 | tf_op jit(solution)/shard_map/ppermute | solution.py:446
  44.0 16.5 %copy-start.10 = (bf16[256,256]{1,0:T(8,128)(2,1)S(1)}, bf16[256,256]{1,0:T(8,128)(2,1)}, u32[]{:S(2)}) copy-start(bf16[256,256]{1,0:T(8,128)(2,1)} %constant.34.clone.lag_hi) | copy-start | bytes 393220
  44.0 29.3 %all-to-all-start.1 = ((bf16[32,40,128]{2,1,0:T(8,128)(2,1)}), bf16[32,40,128]{2,1,0:T(8,128)(2,1)S(1)}, u32[]{:S(2)}, u32[]{:S(2)}) async-start(bf16[32,40,128]{2,1,0:T(8,128)(2,1)} %pair.1), calls=%async_computation.1 | async-start | bytes 655360 | tf_op jit(solution)/shard_map/all_to_all | solution.py:388
  58.2 2.3 %copy-start.9 = (bf16[256,256]{1,0:T(8,128)(2,1)S(1)}, bf16[256,256]{1,0:T(8,128)(2,1)}, u32[]{:S(2)}) copy-start(bf16[256,256]{1,0:T(8,128)(2,1)} %constant.35.clone.lag_lo) | copy-start | bytes 393220
  58.3 7.0 %collective-permute-start.4 = (bf16[256,128]{1,0:T(8,128)(2,1)S(1)}, bf16[256,128]{1,0:T(8,128)(2,1)S(1)}, u32[]{:S(2)}, u32[]{:S(2)}) collective-permute-start(bf16[256,128]{1,0:T(8,128)(2,1)S(1)} %slice_bitcast_fusion), channel_id=1, source_target_pairs={{0,128},{8,136},{16,144},{24,152},{32,160},{40,168},{48,176},{56,1... | collective-permute-start | bytes 196616 | tf_op jit(solution)/shard_map/ppermute | solution.py:469
  65.3 5.8 %collective-permute-start.5 = (bf16[576,128]{1,0:T(8,128)(2,1)S(1)}, bf16[576,128]{1,0:T(8,128)(2,1)S(1)}, u32[]{:S(2)}, u32[]{:S(2)}) collective-permute-start(bf16[576,128]{1,0:T(8,128)(2,1)S(1)} %pad_maximum_fusion.own_ref), channel_id=1, source_target_pairs={{0,256},{256,0},{1,257},{257,1},{2,258},{258,2},{3,259},{259,3},{4... | collective-permute-start | bytes 442376 | tf_op jit(solution)/shard_map/ppermute | solution.py:470

commit v5 on v4

--- a/solution.py
+++ b/solution.py
@@ -11,7 +11,7 @@
 SPAN = 128
 PTS = 2 * SPAN
 QUARTER = SPAN // 4
-BLOCK = 256
+BLOCK = 1024
 TURN_OUT, TURN_BACK = 28, 24
 F32, BF16 = jnp.float32, jnp.bfloat16
 
@@ -44,22 +44,25 @@
     return high, (x - high.astype(F32)).astype(BF16)
 
 
-def spectrum_left(high, low, x):
-    return dot(high, x) + dot(low, x)
-
-
-def spectrum_right(x, high, low):
-    return dot(x, high) + dot(x, low)
-
-
-def invert_left(high, low, spec):
+def spectrum_left(both, x):
+    return dot(both, jnp.concatenate([x, x], 0))
+
+
+def spectrum_right(x, both):
+    return dot(jnp.concatenate([x, x], 1), both)
+
+
+def invert_left(both, spec):
     s_high, s_low = halves(spec)
-    return dot(high, s_high) + (dot(high, s_low) + dot(low, s_high))
-
-
-def invert_right(spec, high, low):
+    main = dot(both, s_high)
+    return main[:SPAN] + (main[SPAN:] + dot(both[:SPAN], s_low))
+
+
+def invert_right(spec, both):
     s_high, s_low = halves(spec)
-    return dot(s_high, high) + (dot(s_low, high) + dot(s_high, low))
+    main = dot(s_high, both)
+    count = both.shape[1] // 2
+    return main[:, :count] + (main[:, count:] + dot(s_low, both[:, :count]))
 
 
 def multiply(ar, ai, br, bi, zero, sign):
@@ -94,7 +97,7 @@
         return pos + length, kind
 
     zero = jnp.int32(0)
-    return lax.fori_loop(0, len_ref.shape[1], step, (zero, zero))[1]
+    return lax.fori_loop(0, len_ref.shape[1], step, (zero, zero), unroll=True)[1]
 
 
 def send_kernel(
@@ -156,7 +159,7 @@
 
 
 def partial_kernel(
-    q_ref, k_ref, v_ref, c_ref, fwd_hi, fwd_lo, inv_hi, inv_lo, give_ref
+    q_ref, k_ref, v_ref, c_ref, fwd, inv, give_ref
 ):
     blocks = q_ref.shape[1] // BLOCK
     count = BLOCK // 32
@@ -165,10 +168,10 @@
         cols = slice(j * BLOCK, (j + 1) * BLOCK)
         x = (k_ref[:, cols].astype(F32) * v_ref[:, cols].astype(F32)).astype(BF16)
         g = (c_ref[:, cols].astype(F32) * q_ref[:, cols].astype(F32)).astype(BF16)
-        xs = spectrum_left(fwd_hi[...], fwd_lo[...], x)
-        gs = spectrum_left(fwd_hi[...], fwd_lo[...], g)
+        xs = spectrum_left(fwd[...], x)
+        gs = spectrum_left(fwd[...], g)
         pr, pi = multiply(gs[:SPAN], gs[SPAN:], xs[:SPAN], xs[SPAN:], zero, -1.0)
-        taps = invert_left(inv_hi[...], inv_lo[...], jnp.concatenate([pr, pi], 0))
+        taps = invert_left(inv[...], jnp.concatenate([pr, pi], 0))
         rows = jnp.transpose(taps).reshape(count, 4, 8, SPAN)
         quarters = swap_blocks([rows[:, b] for b in range(4)])
         for t in range(4):
@@ -177,29 +180,28 @@
 
 
 def tables_kernel(
-    slot_ref, len_ref, taps_ref, tap_hi, tap_lo, after_ref, table_ref, spec_ref, inverse_ref
+    slot_ref, len_ref, taps_ref, tap, after_ref, table_ref, spec_ref, inverse_ref
 ):
     del after_ref
-    spec_ref[...] = spectrum_right(taps_ref[...], tap_hi[...], tap_lo[...])
+    spec_ref[...] = spectrum_right(taps_ref[...], tap[...])
+
+    slots = slot_ref.shape[1]
 
     def fill(r, carry):
         inverse_ref[slot_ref[0, r]] = r
         return carry
 
-    lax.fori_loop(0, slot_ref.shape[1], fill, 0)
+    lax.fori_loop(0, slots, fill, 0, unroll=True)
 
     def step(d, carry):
         pos, count = carry
         length = len_ref[0, d]
-
-        @pl.when(length == 2)
-        def _():
-            table_ref[0, count] = inverse_ref[pos]
-            table_ref[1, count] = inverse_ref[pos + 1]
-
+        table_ref[0, count] = inverse_ref[pos]
+        table_ref[1, count] = inverse_ref[jnp.minimum(pos + 1, slots - 1)]
         return pos + length, count + length - 1
 
-    lax.fori_loop(0, len_ref.shape[1], step, (jnp.int32(0), jnp.int32(0)))
+    zero = jnp.int32(0)
+    lax.fori_loop(0, len_ref.shape[1], step, (zero, zero), unroll=True)
     table_ref[2, 0] = own_kind(slot_ref, len_ref)
 
 
@@ -216,68 +218,91 @@
     cross_ref[...] = total(2 * (1 - far) + 1 - odd).astype(BF16)
 
 
-def pair_spectra(table_ref, got_ref, fwd_hi, fwd_lo):
-    pairs = table_ref.shape[1]
+def pair_spectra(table_ref, got_ref, fwd):
+    pairs = table_ref.shape[1] // 2
     rows = [got_ref[table_ref[k, p] ^ TURN_OUT, 0:32, :] for k in range(2) for p in range(pairs)]
-    spec = spectrum_right(jnp.concatenate(rows, 0), fwd_hi[...], fwd_lo[...])
+    spec = spectrum_right(jnp.concatenate(rows, 0), fwd[...])
     return spec.reshape(2, pairs, 32, PTS)
 
 
 def pair_kernel(
-    table_ref, got_ref, spec_ref, keep_ref, side_ref, next_ref, cross_ref,
-    fwd_hi, fwd_lo, inv_hi, inv_lo, out_ref,
-):
-    slots, pairs = got_ref.shape[0], table_ref.shape[1]
+    table_ref, got_ref, spec_ref, fwd, inv, out_ref
+):
+    slots, pairs = got_ref.shape[0], table_ref.shape[1] // 2
     hr, hi = spec_ref[:, :SPAN], spec_ref[:, SPAN:]
     zero = lax.broadcasted_iota(jnp.int32, hr.shape, 1) == 0
-    spec = pair_spectra(table_ref, got_ref, fwd_hi, fwd_lo)
-    out_ref[:, 0:32, :] = jnp.zeros((slots, 32, SPAN), BF16)
+    spec = pair_spectra(table_ref, got_ref, fwd)
+    out_ref[...] = jnp.zeros((slots, 32, SPAN), BF16)
     for k in range(2):
         sr, si = spec[k, :, :, :SPAN], spec[k, :, :, SPAN:]
         pr, pi = multiply(sr, si, hr[None], hi[None], zero[None], 1.0 if k == 0 else -1.0)
         both = jnp.concatenate([pr, pi], 2).reshape(pairs * 32, PTS)
-        result = invert_right(both, inv_hi[...], inv_lo[...]).astype(BF16)
+        result = invert_right(both, inv[...]).astype(BF16)
         for p in range(pairs):
-            out_ref[table_ref[1 - k, p] ^ TURN_BACK, 0:32, :] = result[32 * p:32 * p + 32]
-    near = keep_ref[...] + side_ref[...].astype(F32)
-    near = (near + (next_ref[...].astype(F32) + cross_ref[...].astype(F32))).astype(BF16)
-    near = near.reshape(slots, 8, SPAN)
-    for j in range(slots // 8):
-        place = 8 * (j ^ (TURN_BACK // 8))
-        out_ref[place:place + 8, 32:40, :] = near[8 * j:8 * j + 8]
-
-
-def pair_taps_kernel(table_ref, got_ref, fwd_hi, fwd_lo, lag_hi, lag_lo, out_ref):
-    spec = pair_spectra(table_ref, got_ref, fwd_hi, fwd_lo)
+            out_ref[table_ref[1 - k, p] ^ TURN_BACK] = result[32 * p:32 * p + 32]
+
+
+def load_kernel(
+    pair_ref, keep_ref, side_ref, next_ref, cross_ref, out_hbm, out_buf, sems
+):
+    slots = pair_ref.shape[0]
+    half = slots // 2
+    copies = []
+    for h in range(2):
+        source = slice(h * half * 8, (h + 1) * half * 8)
+        near = keep_ref[source] + side_ref[source].astype(F32)
+        near = near + (next_ref[source].astype(F32) + cross_ref[source].astype(F32))
+        near = near.astype(BF16).reshape(half, 8, SPAN)
+        start = (h * half) ^ (TURN_BACK // half * half)
+        rows = slice(start, start + half)
+        out_buf[rows, 0:32, :] = pair_ref[rows]
+        for piece in range(0, half, 8):
+            place = (h * half + piece) ^ TURN_BACK
+            out_buf[place:place + 8, 32:40, :] = near[piece:piece + 8]
+        copy = pltpu.make_async_copy(out_buf.at[rows], out_hbm.at[rows], sems.at[h])
+        copy.start()
+        copies.append(copy)
+    for copy in copies:
+        copy.wait()
+
+
+def pair_taps_kernel(
+    table_ref, got_ref, q_ref, k_ref, v_ref, c_ref, fwd, own_fwd, lag,
+    out_ref, xs_ref, gs_ref,
+):
+    for j in range(q_ref.shape[1] // BLOCK):
+        cols = slice(j * BLOCK, (j + 1) * BLOCK)
+        x = (k_ref[:, cols].astype(F32) * v_ref[:, cols].astype(F32)).astype(BF16)
+        g = (c_ref[:, cols].astype(F32) * q_ref[:, cols].astype(F32)).astype(BF16)
+        xs_ref[:, cols] = spectrum_left(own_fwd[...], x)
+        gs_ref[:, cols] = spectrum_left(own_fwd[...], g)
+    spec = pair_spectra(table_ref, got_ref, fwd)
     zero = lax.broadcasted_iota(jnp.int32, (1, 32, SPAN), 2) == 0
     xs, gs = spec[0], spec[1]
     tr, ti = multiply(
         gs[:, :, :SPAN], gs[:, :, SPAN:], xs[:, :, :SPAN], xs[:, :, SPAN:], zero, -1.0
     )
     both = jnp.concatenate([jnp.sum(tr, 0), jnp.sum(ti, 0)], 1)
-    taps = invert_right(both, lag_hi[...], lag_lo[...]).astype(BF16)
+    taps = invert_right(both, lag[...]).astype(BF16)
     out_ref[0:32, :] = taps[:, :SPAN]
     out_ref[32:64, :] = taps[:, SPAN:]
 
 
 def local_kernel(
-    own_ref, core_ref, q_ref, k_ref, v_ref, c_ref, fwd_hi, fwd_lo, inv_hi, inv_lo,
-    mixed_ref, series_ref,
-):
-    blocks = q_ref.shape[1] // BLOCK
+    own_ref, core_ref, xs_ref, gs_ref, fwd, inv, mixed_ref, series_ref
+):
+    blocks = xs_ref.shape[1] // BLOCK
     count = BLOCK // 32
     dp, far = lax.axis_index("dp"), lax.axis_index("ctx") // 16
     zero = lax.broadcasted_iota(jnp.int32, (SPAN, BLOCK), 0) == 0
     nt = ((1,), (1,))
     for j in range(blocks):
         cols = slice(j * BLOCK, (j + 1) * BLOCK)
-        x = (k_ref[:, cols].astype(F32) * v_ref[:, cols].astype(F32)).astype(BF16)
-        g = (c_ref[:, cols].astype(F32) * q_ref[:, cols].astype(F32)).astype(BF16)
-        xs = spectrum_left(fwd_hi[...], fwd_lo[...], x)
-        gs = spectrum_left(fwd_hi[...], fwd_lo[...], g)
+        xs, gs = xs_ref[:, cols], gs_ref[:, cols]
 
         def rows(ref, start):
-            places = [start + 32 * (b ^ (TURN_OUT // 4)) for b in (2 * j, 2 * j + 1)]
+            blocks = range(j * BLOCK // SPAN, (j + 1) * BLOCK // SPAN)
+            places = [start + 32 * (b ^ (TURN_OUT // 4)) for b in blocks]
             return jnp.concatenate([ref[p:p + 32, :].astype(F32) for p in places], 0)
 
         own, side = rows(own_ref, 0), rows(own_ref, 256)
@@ -288,14 +313,14 @@
             there = jnp.where(far == t % 2, core, cross)
             quarters.append(jnp.where(dp == t // 2, here, there).reshape(count, 8, SPAN))
         taps = jnp.concatenate(swap_blocks(quarters), 1).reshape(BLOCK, SPAN).astype(BF16)
-        hs = dot(fwd_hi[...], taps, nt) + dot(fwd_lo[...], taps, nt)
+        hs = dot(fwd[...], jnp.concatenate([taps, taps], 1), nt)
         hr, hi = hs[:SPAN], hs[SPAN:]
         mr, mi = multiply(xs[:SPAN], xs[SPAN:], hr, hi, zero, 1.0)
         spec = jnp.concatenate([mr, mi], 0)
-        mixed_ref[:, cols] = invert_left(inv_hi[...], inv_lo[...], spec)
+        mixed_ref[:, cols] = invert_left(inv[...], spec)
         sr, si = multiply(gs[:SPAN], gs[SPAN:], hr, hi, zero, -1.0)
         spec = jnp.concatenate([sr, si], 0)
-        series_ref[:, cols] = invert_left(inv_hi[...], inv_lo[...], spec)
+        series_ref[:, cols] = invert_left(inv[...], spec)
 
 
 def finish_kernel(
@@ -367,20 +392,20 @@
     scale = float(tokens * parts * lax.axis_size("dp")) ** (-0.5)
     forward, inverse = transforms()
 
-    def constant(matrix):
-        return [jnp.asarray(m) for m in split_bf16(matrix)]
-
-    fwd = constant(forward[:, :SPAN])
-    fwd_t = constant(forward[:, :SPAN].T)
-    inv = constant(inverse[:SPAN])
-    inv_t = constant(inverse[:SPAN].T)
-    tap_t = constant(np.roll(forward, -SPAN, 1).T)
-    lag_t = constant(np.roll(inverse, SPAN, 0).T)
+    def constant(matrix, axis):
+        return jnp.asarray(np.concatenate(split_bf16(matrix), axis))
+
+    fwd = constant(forward[:, :SPAN], 1)
+    fwd_t = constant(forward[:, :SPAN].T, 0)
+    inv = constant(inverse[:SPAN], 0)
+    inv_t = constant(inverse[:SPAN].T, 1)
+    tap_t = constant(np.roll(forward, -SPAN, 1).T, 0)
+    lag_t = constant(np.roll(inverse, SPAN, 0).T, 1)
     core_swap = [(0, 1), (1, 0)]
     side_swap = [(c, c ^ 16) for c in range(parts)]
     cross_swap = [(c, c ^ 17) for c in range(parts)]
     next_swap = [(c, c ^ 1) for c in range(parts)]
-    steps = width // BLOCK
+    steps = width // 256
     taps_rows = filter_taps.T
 
     def exchange(array, turn):
@@ -411,12 +436,12 @@
     give = pl.pallas_call(
         partial_kernel,
         out_shape=jax.ShapeDtypeStruct((4, parts * 8, SPAN), BF16),
-        in_specs=[VMEM] * 8,
+        in_specs=[VMEM] * 6,
         out_specs=VMEM,
         compiler_params=params(),
         cost_estimate=cost(2e9, 10 * area),
         name="partial_taps",
-    )(query, key, value, cotangent, *fwd, *inv)
+    )(query, key, value, cotangent, fwd, inv)
     taken = lax.ppermute(give, "dp", core_swap)
     quarter = jax.ShapeDtypeStruct((parts * 8, SPAN), BF16)
     keep, side, near, cross = pl.pallas_call(
@@ -431,52 +456,63 @@
     table, tap_spec = pl.pallas_call(
         tables_kernel,
         out_shape=(
-            jax.ShapeDtypeStruct((3, pairs), jnp.int32),
+            jax.ShapeDtypeStruct((3, 2 * pairs), jnp.int32),
             jax.ShapeDtypeStruct((32, PTS), F32),
         ),
-        in_specs=[SMEM, SMEM, VMEM, VMEM, VMEM, ANY],
+        in_specs=[SMEM, SMEM, VMEM, VMEM, ANY],
         out_specs=(SMEM, VMEM),
         scratch_shapes=[pltpu.SMEM((parts,), jnp.int32)],
         compiler_params=params(),
         cost_estimate=cost(area, area),
         name="tables",
-    )(span_slot, doc_lengths, taps_rows, *tap_t, cross)
+    )(span_slot, doc_lengths, taps_rows, tap_t, give)
     side = lax.ppermute(side, "ctx", side_swap)
     near = lax.ppermute(near, "ctx", next_swap)
     cross = lax.ppermute(cross, "ctx", cross_swap)
 
     back = pl.pallas_call(
         pair_kernel,
-        out_shape=chunk,
-        in_specs=[SMEM] + [VMEM] * 10,
+        out_shape=jax.ShapeDtypeStruct((parts, 32, SPAN), BF16),
+        in_specs=[SMEM] + [VMEM] * 4,
         out_specs=VMEM,
         compiler_params=params(),
         cost_estimate=cost(1e9, 8 * area),
         name="pair",
-    )(table, got, tap_spec, keep, side, near, cross, *fwd_t, *inv_t)
+    )(table, got, tap_spec, fwd_t, inv_t)
+    back = pl.pallas_call(
+        load_kernel,
+        out_shape=chunk,
+        in_specs=[VMEM] * 5,
+        out_specs=HBM,
+        scratch_shapes=[pltpu.VMEM(chunk.shape, BF16), DMA((2,))],
+        compiler_params=params(),
+        cost_estimate=cost(area, 4 * area),
+        name="load",
+    )(back, keep, side, near, cross)
     landed = exchange(back, TURN_BACK)
 
     own = got[:, 32:40, :].reshape(parts * 8, SPAN)
-    pair_taps = pl.pallas_call(
+    pair_taps, xs, gs = pl.pallas_call(
         pair_taps_kernel,
-        out_shape=jax.ShapeDtypeStruct((64, SPAN), BF16),
-        in_specs=[SMEM] + [VMEM] * 5,
-        out_specs=VMEM,
+        out_shape=(jax.ShapeDtypeStruct((64, SPAN), BF16),)
+        + (jax.ShapeDtypeStruct((PTS, width), F32),) * 2,
+        in_specs=[SMEM] + [VMEM] * 8,
+        out_specs=(VMEM,) * 3,
         compiler_params=params(),
         cost_estimate=cost(1e9, 6 * area),
         name="pair_taps",
-    )(table, got, *fwd_t, *lag_t)
+    )(table, got, query, key, value, cotangent, fwd_t, fwd, lag_t)
     own = jnp.concatenate([own, lax.ppermute(own, "ctx", side_swap), pair_taps], 0)
     core = lax.ppermute(own, "dp", core_swap)
     mixed, series = pl.pallas_call(
         local_kernel,
         out_shape=(jax.ShapeDtypeStruct((tokens, width), F32),) * 2,
-        in_specs=[VMEM] * 10,
+        in_specs=[VMEM] * 6,
         out_specs=(VMEM, VMEM),
         compiler_params=params(),
         cost_estimate=cost(3e9, 20 * area),
         name="local",
-    )(own, core, query, key, value, cotangent, *fwd, *inv)
+    )(own, core, xs, gs, fwd, inv)
 
     result = jax.ShapeDtypeStruct((tokens, width), BF16)
     *grads, grad_filter = pl.pallas_call(

time: 75.6 us -> 74.4 us (0.984)
  Pallas kernels: 13.2 us -> 11.1 us
  starting transfers between devices: 53.3 us -> 54.6 us
    all_to_all x2, waiting for transfers between devices: 0.01 us -> 2.58 us  [exchange(): lax.all_to_all(array, 'ctx', split_axis=0, concat_axis=0, axis_index_grou...]
    ppermute x1, waiting for transfers between devices: 1.58 us -> 0.01 us  [per_device(): cross = lax.ppermute(cross, 'ctx', cross_swap)]
    ppermute x1, waiting for transfers between devices: 1.14 us -> 0.01 us  [per_device(): taken = lax.ppermute(give, 'dp', core_swap)]
    ppermute x1, starting transfers between devices: 4.81 us -> 5.82 us  [per_device(): core = lax.ppermute(own, 'dp', core_swap)]
    pallas_call x1, Pallas kernels: 2.17 us -> 1.29 us  [per_device(): pl.pallas_call(local_kernel, out_shape=(jax.ShapeDtypeStruct((tokens, wid...]
    pallas_call x3 -> x4, Pallas kernels: 5.04 us -> 4.54 us  [the longest x1 1.42 us: per_device(): pl.pallas_call(tables_kernel, out_shape=(jax.ShapeDtypeStruct((3, 2 * pai...]
  transfers between devices with their start and end apart: 8 -> 8, of which waited for: 4 -> 3; matrix products, arithmetic and copies ran while one was open for 0% -> 0% of each run, Pallas kernels for 10% -> 9%
where the time goes in v5:
time: 74.4 us; the launch traced here: 73.9 us
  starting transfers between devices  54.6 us (73%)
  Pallas kernels  11.1 us (15%)
  waiting for transfers between devices  7.16 us (10%)
  between operations  0.99 us (1%)
    all_to_all x2, starting transfers between devices, exchange(): lax.all_to_all(array, 'ctx', split_axis=0, concat_axis=0, axis_index_grou...  33.6 us
    ppermute x1, starting transfers between devices, per_device(): core = lax.ppermute(own, 'dp', core_swap)  5.82 us
    ppermute x1, starting transfers between devices, per_device(): cross = lax.ppermute(cross, 'ctx', cross_swap)  4.66 us
    ppermute x1, waiting for transfers between devices, per_device(): lax.ppermute(own, 'ctx', side_swap)  3.58 us
    ppermute x1, starting transfers between devices, per_device(): taken = lax.ppermute(give, 'dp', core_swap)  3.14 us
    ppermute x1, starting transfers between devices, per_device(): near = lax.ppermute(near, 'ctx', next_swap)  3.09 us
    all_to_all x2, waiting for transfers between devices, exchange(): lax.all_to_all(array, 'ctx', split_axis=0, concat_axis=0, axis_index_grou...  2.58 us
    pallas_call x1, Pallas kernels, per_device(): pl.pallas_call(send_kernel, out_shape=chunk, in_specs=[HBM] * 7, out_spec...  2.26 us
  transfers between devices with their start and end apart: 8, of which 3 were waited for; matrix products, arithmetic and copies ran while one was open for 0% of the time, Pallas kernels for 9%

profile of v5, /device:TPU:1, one launch (start us, length us, event | category | flops | bytes accessed | tf_op | source)
XLA Modules:
  0.0 73.9 jit_solution(1648049147490824117)
XLA Ops:
  0.6 0.0 copy-start.2
  0.6 0.0 copy-start.4
  0.7 0.0 copy-start.10
  0.7 2.3 %send.1 = bf16[32,40,128]{2,1,0:T(8,128)(2,1)} custom-call(s32[1,32]{1,0:T(1,128)} %slot_hbm.1, s32[1,24]{1,0:T(1,128)} %len_hbm.1, bf16[32,256]{1,0:T(8,128)(2,1)} %bitcast.4, bf16[128,1024]{1,0:T(8,128)(2,1)} %q_ref.3, bf16[128,1024]{1,0:T(8,128)(2,1)} %k_ref.5, bf16[128,1024]{1,0:T(8,128)(2,1)} %v_ref.5, bf16[128,1024]{1,0:T(8,128)(2,1)} %c_ref.5), custom_call_target="tpu_custom_call" | custom-call | flops 262144 | bytes 1048576 | tf_op jit(solution)/shard_map/send/pallas_call | solution.py:418
  2.9 0.0 copy-start
  2.9 0.0 copy-start.1
  3.0 0.0 copy-start.9
  3.0 18.8 %all-to-all-start = ((bf16[32,40,128]{2,1,0:T(8,128)(2,1)}), bf16[32,40,128]{2,1,0:T(8,128)(2,1)S(1)}, u32[]{:S(2)}, u32[]{:S(2)}) async-start(bf16[32,40,128]{2,1,0:T(8,128)(2,1)} %send.1), calls=%async_computation | async-start | bytes 655360 | tf_op jit(solution)/shard_map/all_to_all | solution.py:413
  21.7 0.0 copy-done.2
  21.7 0.0 copy-done.4
  21.8 0.0 copy-done.10
  21.8 0.0 copy-done
  21.8 0.0 copy-done.1
  21.8 0.0 copy-done.9
  21.8 0.0 copy-start.3
  21.8 0.0 copy-start.5
  21.8 0.0 copy-start.6
  21.8 0.0 copy-start.7
  21.8 1.2 %partial_taps.1.after_ref.own_ref = bf16[4,256,128]{2,1,0:T(8,128)(2,1)S(1)} custom-call(bf16[128,1024]{1,0:T(8,128)(2,1)S(1)} %copy-done.4, bf16[128,1024]{1,0:T(8,128)(2,1)S(1)} %copy-done, bf16[128,1024]{1,0:T(8,128)(2,1)S(1)} %copy-done.1, bf16[128,1024]{1,0:T(8,128)(2,1)S(1)} %copy-done.2, bf16[256,256]{1,0:T(8,128)(2,1)S(1)} %copy-done.9, ...), custom_call_target="tpu_custom_call" | custom-call | flops 2000000000 | bytes 1310720 | tf_op jit(solution)/shard_map/partial_taps/pallas_call | solution.py:436
  23.0 3.1 %collective-permute-start = (bf16[4,256,128]{2,1,0:T(8,128)(2,1)S(1)}, bf16[4,256,128]{2,1,0:T(8,128)(2,1)S(1)}, u32[]{:S(2)}, u32[]{:S(2)}) collective-permute-start(bf16[4,256,128]{2,1,0:T(8,128)(2,1)S(1)} %partial_taps.1.after_ref.own_ref), channel_id=1, source_target_pairs={{0,256},{256,0},{1,257},{257,1},{2,258},{258,2},{3,259},{259,3},{4... | collective-permute-start | bytes 786440 | tf_op jit(solution)/shard_map/ppermute | solution.py:445
  26.2 0.0 copy-done.3
  26.2 0.0 copy-done.5
  26.2 0.0 copy-done.6
  26.2 1.4 %tables.1 = (s32[3,16]{1,0:T(4,128)S(1)}, f32[32,256]{1,0:T(8,128)S(1)}) custom-call(s32[1,32]{1,0:T(1,128)S(1)} %copy-done.6, s32[1,24]{1,0:T(1,128)S(1)} %copy-done.7, bf16[32,256]{1,0:T(8,128)(2,1)S(1)} %bitcast.5, bf16[512,256]{1,0:T(8,128)(2,1)S(1)} %copy-done.3, bf16[4,256,128]{2,1,0:T(8,128)(2,1)S(1)} %partial_taps.1.after_ref.own_ref), custom_call_target="tpu_custom_call" | custom-call | flops 131072 | bytes 131072 | tf_op jit(solution)/shard_map/tables/pallas_call | solution.py:456
  27.6 0.0 copy-start.11
  27.6 0.0 copy-start.12
  27.7 0.0 collective-permute-done.other_ref
  27.7 0.1 share.1
  27.8 2.1 %collective-permute-start.1 = (bf16[256,128]{1,0:T(8,128)(2,1)S(1)}, bf16[256,128]{1,0:T(8,128)(2,1)S(1)}, u32[]{:S(2)}, u32[]{:S(2)}) collective-permute-start(bf16[256,128]{1,0:T(8,128)(2,1)S(1)} %get-tuple-element.22), channel_id=1, source_target_pairs={{0,128},{8,136},{16,144},{24,152},{32,160},{40,168},{48,176},{56,1... | collective-permute-start | bytes 196616 | tf_op jit(solution)/shard_map/ppermute | solution.py:469
  29.9 3.1 %collective-permute-start.2 = (bf16[256,128]{1,0:T(8,128)(2,1)S(1)}, bf16[256,128]{1,0:T(8,128)(2,1)S(1)}, u32[]{:S(2)}, u32[]{:S(2)}) collective-permute-start(bf16[256,128]{1,0:T(8,128)(2,1)S(1)} %get-tuple-element.23), channel_id=1, source_target_pairs={{0,8},{8,0},{16,24},{24,16},{32,40},{40,32},{48,56},{56,48},{64,72... | collective-permute-start | bytes 196616 | tf_op jit(solution)/shard_map/ppermute | solution.py:470
  33.0 4.7 %collective-permute-start.3 = (bf16[256,128]{1,0:T(8,128)(2,1)S(1)}, bf16[256,128]{1,0:T(8,128)(2,1)S(1)}, u32[]{:S(2)}, u32[]{:S(2)}) collective-permute-start(bf16[256,128]{1,0:T(8,128)(2,1)S(1)} %get-tuple-element.24), channel_id=1, source_target_pairs={{0,136},{8,128},{16,152},{24,144},{32,168},{40,160},{48,184},{56,1... | collective-permute-start | bytes 196616 | tf_op jit(solution)/shard_map/ppermute | solution.py:471
  37.7 2.6 %all-to-all-done.got_ref = bf16[32,40,128]{2,1,0:T(8,128)(2,1)S(1)} async-done(((bf16[32,40,128]{2,1,0:T(8,128)(2,1)}), bf16[32,40,128]{2,1,0:T(8,128)(2,1)S(1)}, u32[]{:S(2)}, u32[]{:S(2)}) %all-to-all-start) | async-done | bytes 327712 | tf_op jit(solution)/shard_map/all_to_all | solution.py:413
  40.2 1.1 %pair.1.pair_ref = bf16[32,32,128]{2,1,0:T(8,128)(2,1)S(1)} custom-call(s32[3,16]{1,0:T(4,128)S(1)} %get-tuple-element.19.table_ref, bf16[32,40,128]{2,1,0:T(8,128)(2,1)S(1)} %all-to-all-done.got_ref, f32[32,256]{1,0:T(8,128)S(1)} %get-tuple-element.20.spec_ref, bf16[256,256]{1,0:T(8,128)(2,1)S(1)} %copy-done.11, bf16[256,256]{1,0:T(8,128)(2,1)S(1)} %copy-done.12), custom_call_target="tpu_custom_call" | custom-call | flops 1000000000 | bytes 1048576 | tf_op jit(solution)/shard_map/pair/pallas_call | solution.py:473
  41.3 0.0 collective-permute-done.1.side_ref
  41.3 0.0 collective-permute-done.2.next_ref
  41.4 0.0 collective-permute-done.3.cross_ref
  41.4 0.8 %load.1 = bf16[32,40,128]{2,1,0:T(8,128)(2,1)} custom-call(bf16[32,32,128]{2,1,0:T(8,128)(2,1)S(1)} %pair.1.pair_ref, f32[256,128]{1,0:T(8,128)S(1)} %get-tuple-element.21.keep_ref, bf16[256,128]{1,0:T(8,128)(2,1)S(1)} %collective-permute-done.1.side_ref, bf16[256,128]{1,0:T(8,128)(2,1)S(1)} %collective-permute-done.2.next_ref, ...), custom_call_target="tpu_custom_call" | custom-call | flops 131072 | bytes 524288 | tf_op jit(solution)/shard_map/load/pallas_call | solution.py:482
  42.2 0.0 copy-start.8
  42.2 14.9 %all-to-all-start.1 = ((bf16[32,40,128]{2,1,0:T(8,128)(2,1)}), bf16[32,40,128]{2,1,0:T(8,128)(2,1)S(1)}, u32[]{:S(2)}, u32[]{:S(2)}) async-start(bf16[32,40,128]{2,1,0:T(8,128)(2,1)} %load.1), calls=%async_computation.1 | async-start | bytes 655360 | tf_op jit(solution)/shard_map/all_to_all | solution.py:413
  57.0 2.2 %collective-permute-start.4 = (bf16[256,128]{1,0:T(8,128)(2,1)S(1)}, bf16[256,128]{1,0:T(8,128)(2,1)S(1)}, u32[]{:S(2)}, u32[]{:S(2)}) collective-permute-start(bf16[256,128]{1,0:T(8,128)(2,1)S(1)} %slice_bitcast_fusion), channel_id=1, source_target_pairs={{0,128},{8,136},{16,144},{24,152},{32,160},{40,168},{48,176},{56,1... | collective-permute-start | bytes 196616 | tf_op jit(solution)/shard_map/ppermute | solution.py:505
  59.2 0.0 copy-done.8
  59.2 1.3 %pair_taps.1 = (bf16[64,128]{1,0:T(8,128)(2,1)S(1)}, f32[256,1024]{1,0:T(8,128)S(1)}, f32[256,1024]{1,0:T(8,128)S(1)}) custom-call(s32[3,16]{1,0:T(4,128)S(1)} %get-tuple-element.19.table_ref, bf16[32,40,128]{2,1,0:T(8,128)(2,1)S(1)} %all-to-all-done.got_ref, bf16[128,1024]{1,0:T(8,128)(2,1)S(1)} %copy-done.4, bf16[128,1024]{1,0:T(8,128)(2,1)S(1)} %copy-done, ...), custom_call_target="tpu_custom_call" | custom-call | flops 1000000000 | bytes 786432 | tf_op jit(solution)/shard_map/pair_taps/pallas_call | solution.py:495
  60.5 3.6 %collective-permute-done.4 = bf16[256,128]{1,0:T(8,128)(2,1)S(1)} collective-permute-done((bf16[256,128]{1,0:T(8,128)(2,1)S(1)}, bf16[256,128]{1,0:T(8,128)(2,1)S(1)}, u32[]{:S(2)}, u32[]{:S(2)}) %collective-permute-start.4) | collective-permute-done | bytes 65568 | tf_op jit(solution)/shard_map/ppermute | solution.py:505
  64.1 5.8 %collective-permute-start.5 = (bf16[576,128]{1,0:T(8,128)(2,1)S(1)}, bf16[576,128]{1,0:T(8,128)(2,1)S(1)}, u32[]{:S(2)}, u32[]{:S(2)}) collective-permute-start(bf16[576,128]{1,0:T(8,128)(2,1)S(1)} %pad_maximum_fusion.own_ref), channel_id=1, source_target_pairs={{0,256},{256,0},{1,257},{257,1},{2,258},{258,2},{3,259},{259,3},{4... | collective-permute-start | bytes 442376 | tf_op jit(solution)/shard_map/ppermute | solution.py:506
  69.9 1.0 %collective-permute-done.5.core_ref = bf16[576,128]{1,0:T(8,128)(2,1)S(1)} collective-permute-done((bf16[576,128]{1,0:T(8,128)(2,1)S(1)}, bf16[576,128]{1,0:T(8,128)(2,1)S(1)}, u32[]{:S(2)}, u32[]{:S(2)}) %collective-permute-start.5) | collective-permute-done | bytes 147488 | tf_op jit(solution)/shard_map/ppermute | solution.py:506
  70.9 1.3 %local.1 = (f32[128,1024]{1,0:T(8,128)S(1)}, f32[128,1024]{1,0:T(8,128)S(1)}) custom-call(bf16[576,128]{1,0:T(8,128)(2,1)S(1)} %pad_maximum_fusion.own_ref, bf16[576,128]{1,0:T(8,128)(2,1)S(1)} %collective-permute-done.5.core_ref, f32[256,1024]{1,0:T(8,128)S(1)} %get-tuple-element.26.xs_ref, f32[256,1024]{1,0:T(8,128)S(1)} %get-tuple-element.27.gs_ref, ...), custom_call_target="tpu_custom_call" | custom-call | flops 3000000000 | bytes 2621440 | tf_op jit(solution)/shard_map/local/pallas_call | solution.py:507
  72.2 0.0 all-to-all-done.1.got_ref
  72.2 1.7 %finish.1 = (bf16[128,1024]{1,0:T(8,128)(2,1)}, bf16[128,1024]{1,0:T(8,128)(2,1)}, bf16[128,1024]{1,0:T(8,128)(2,1)}, bf16[32,256]{1,0:T(8,128)(2,1)}) custom-call(s32[3,16]{1,0:T(4,128)S(1)} %get-tuple-element.19.table_ref, bf16[32,40,128]{2,1,0:T(8,128)(2,1)S(1)} %all-to-all-done.1.got_ref, f32[128,1024]{1,0:T(8,128)S(1)} %get-tuple-element.28.mixed_ref, ...), custom_call_target="tpu_custom_call" | custom-call | flops 1310720 | bytes 2621440 | tf_op jit(solution)/shard_map/finish/pallas_call | solution.py:518
  (5 shorter events, 0.0 us)
Async XLA Ops:
  0.6 21.1 %copy-start.2 = (bf16[128,1024]{1,0:T(8,128)(2,1)S(1)}, bf16[128,1024]{1,0:T(8,128)(2,1)}, u32[]{:S(2)}) copy-start(bf16[128,1024]{1,0:T(8,128)(2,1)} %c_ref.5) | copy-start | bytes 786436
  0.6 21.1 %copy-start.4 = (bf16[128,1024]{1,0:T(8,128)(2,1)S(1)}, bf16[128,1024]{1,0:T(8,128)(2,1)}, u32[]{:S(2)}) copy-start(bf16[128,1024]{1,0:T(8,128)(2,1)} %q_ref.3) | copy-start | bytes 786436
  0.7 21.1 %copy-start.10 = (bf16[256,256]{1,0:T(8,128)(2,1)S(1)}, bf16[256,256]{1,0:T(8,128)(2,1)}, u32[]{:S(2)}) copy-start(bf16[256,256]{1,0:T(8,128)(2,1)} %constant.14.clone.inv) | copy-start | bytes 393220
  2.9 18.8 %copy-start = (bf16[128,1024]{1,0:T(8,128)(2,1)S(1)}, bf16[128,1024]{1,0:T(8,128)(2,1)}, u32[]{:S(2)}) copy-start(bf16[128,1024]{1,0:T(8,128)(2,1)} %k_ref.5) | copy-start | bytes 786436
  2.9 18.8 %copy-start.1 = (bf16[128,1024]{1,0:T(8,128)(2,1)S(1)}, bf16[128,1024]{1,0:T(8,128)(2,1)}, u32[]{:S(2)}) copy-start(bf16[128,1024]{1,0:T(8,128)(2,1)} %v_ref.5) | copy-start | bytes 786436
  3.0 18.8 %copy-start.9 = (bf16[256,256]{1,0:T(8,128)(2,1)S(1)}, bf16[256,256]{1,0:T(8,128)(2,1)}, u32[]{:S(2)}) copy-start(bf16[256,256]{1,0:T(8,128)(2,1)} %constant.12.clone.fwd.own_fwd) | copy-start | bytes 393220
  3.0 37.3 %all-to-all-start = ((bf16[32,40,128]{2,1,0:T(8,128)(2,1)}), bf16[32,40,128]{2,1,0:T(8,128)(2,1)S(1)}, u32[]{:S(2)}, u32[]{:S(2)}) async-start(bf16[32,40,128]{2,1,0:T(8,128)(2,1)} %send.1), calls=%async_computation | async-start | bytes 655360 | tf_op jit(solution)/shard_map/all_to_all | solution.py:413
  21.8 4.4 %copy-start.3 = (bf16[512,256]{1,0:T(8,128)(2,1)S(1)}, bf16[512,256]{1,0:T(8,128)(2,1)}, u32[]{:S(2)}) copy-start(bf16[512,256]{1,0:T(8,128)(2,1)} %constant.16.clone.tap) | copy-start | bytes 786436
  21.8 4.4 %copy-start.5 = (bf16[256,32]{0,1:T(8,128)(2,1)S(1)}, bf16[256,32]{0,1:T(8,128)(2,1)}, u32[]{:S(2)}) copy-start(bf16[256,32]{0,1:T(8,128)(2,1)} %param.17) | copy-start | bytes 49156
  21.8 4.4 %copy-start.6 = (s32[1,32]{1,0:T(1,128)S(1)}, s32[1,32]{1,0:T(1,128)}, u32[]{:S(2)}) copy-start(s32[1,32]{1,0:T(1,128)} %slot_hbm.1) | copy-start | bytes 388
  21.8 4.4 %copy-start.7 = (s32[1,24]{1,0:T(1,128)S(1)}, s32[1,24]{1,0:T(1,128)}, u32[]{:S(2)}) copy-start(s32[1,24]{1,0:T(1,128)} %len_hbm.1) | copy-start | bytes 292
  23.0 4.6 %collective-permute-start = (bf16[4,256,128]{2,1,0:T(8,128)(2,1)S(1)}, bf16[4,256,128]{2,1,0:T(8,128)(2,1)S(1)}, u32[]{:S(2)}, u32[]{:S(2)}) collective-permute-start(bf16[4,256,128]{2,1,0:T(8,128)(2,1)S(1)} %partial_taps.1.after_ref.own_ref), channel_id=1, source_target_pairs={{0,256},{256,0},{1,257},{257,1},{2,258},{258,2},{3,259},{259,3},{4... | collective-permute-start | bytes 786440 | tf_op jit(solution)/shard_map/ppermute | solution.py:445
  27.6 12.6 %copy-start.11 = (bf16[256,256]{1,0:T(8,128)(2,1)S(1)}, bf16[256,256]{1,0:T(8,128)(2,1)}, u32[]{:S(2)}) copy-start(bf16[256,256]{1,0:T(8,128)(2,1)} %constant.13.clone.fwd) | copy-start | bytes 393220
  27.6 12.6 %copy-start.12 = (bf16[256,256]{1,0:T(8,128)(2,1)S(1)}, bf16[256,256]{1,0:T(8,128)(2,1)}, u32[]{:S(2)}) copy-start(bf16[256,256]{1,0:T(8,128)(2,1)} %constant.15.clone.inv) | copy-start | bytes 393220
  27.8 13.6 %collective-permute-start.1 = (bf16[256,128]{1,0:T(8,128)(2,1)S(1)}, bf16[256,128]{1,0:T(8,128)(2,1)S(1)}, u32[]{:S(2)}, u32[]{:S(2)}) collective-permute-start(bf16[256,128]{1,0:T(8,128)(2,1)S(1)} %get-tuple-element.22), channel_id=1, source_target_pairs={{0,128},{8,136},{16,144},{24,152},{32,160},{40,168},{48,176},{56,1... | collective-permute-start | bytes 196616 | tf_op jit(solution)/shard_map/ppermute | solution.py:469
  29.9 11.5 %collective-permute-start.2 = (bf16[256,128]{1,0:T(8,128)(2,1)S(1)}, bf16[256,128]{1,0:T(8,128)(2,1)S(1)}, u32[]{:S(2)}, u32[]{:S(2)}) collective-permute-start(bf16[256,128]{1,0:T(8,128)(2,1)S(1)} %get-tuple-element.23), channel_id=1, source_target_pairs={{0,8},{8,0},{16,24},{24,16},{32,40},{40,32},{48,56},{56,48},{64,72... | collective-permute-start | bytes 196616 | tf_op jit(solution)/shard_map/ppermute | solution.py:470
  33.0 8.4 %collective-permute-start.3 = (bf16[256,128]{1,0:T(8,128)(2,1)S(1)}, bf16[256,128]{1,0:T(8,128)(2,1)S(1)}, u32[]{:S(2)}, u32[]{:S(2)}) collective-permute-start(bf16[256,128]{1,0:T(8,128)(2,1)S(1)} %get-tuple-element.24), channel_id=1, source_target_pairs={{0,136},{8,128},{16,152},{24,144},{32,168},{40,160},{48,184},{56,1... | collective-permute-start | bytes 196616 | tf_op jit(solution)/shard_map/ppermute | solution.py:471
  42.2 17.1 %copy-start.8 = (bf16[256,512]{1,0:T(8,128)(2,1)S(1)}, bf16[256,512]{1,0:T(8,128)(2,1)}, u32[]{:S(2)}) copy-start(bf16[256,512]{1,0:T(8,128)(2,1)} %constant.17.clone.lag) | copy-start | bytes 786436
  42.2 30.0 %all-to-all-start.1 = ((bf16[32,40,128]{2,1,0:T(8,128)(2,1)}), bf16[32,40,128]{2,1,0:T(8,128)(2,1)S(1)}, u32[]{:S(2)}, u32[]{:S(2)}) async-start(bf16[32,40,128]{2,1,0:T(8,128)(2,1)} %load.1), calls=%async_computation.1 | async-start | bytes 655360 | tf_op jit(solution)/shard_map/all_to_all | solution.py:413
  57.0 7.0 %collective-permute-start.4 = (bf16[256,128]{1,0:T(8,128)(2,1)S(1)}, bf16[256,128]{1,0:T(8,128)(2,1)S(1)}, u32[]{:S(2)}, u32[]{:S(2)}) collective-permute-start(bf16[256,128]{1,0:T(8,128)(2,1)S(1)} %slice_bitcast_fusion), channel_id=1, source_target_pairs={{0,128},{8,136},{16,144},{24,152},{32,160},{40,168},{48,176},{56,1... | collective-permute-start | bytes 196616 | tf_op jit(solution)/shard_map/ppermute | solution.py:505
  64.1 6.8 %collective-permute-start.5 = (bf16[576,128]{1,0:T(8,128)(2,1)S(1)}, bf16[576,128]{1,0:T(8,128)(2,1)S(1)}, u32[]{:S(2)}, u32[]{:S(2)}) collective-permute-start(bf16[576,128]{1,0:T(8,128)(2,1)S(1)} %pad_maximum_fusion.own_ref), channel_id=1, source_target_pairs={{0,256},{256,0},{1,257},{257,1},{2,258},{258,2},{3,259},{259,3},{4... | collective-permute-start | bytes 442376 | tf_op jit(solution)/shard_map/ppermute | solution.py:506

commit v6 on v5

--- a/solution.py
+++ b/solution.py
@@ -12,7 +12,7 @@
 PTS = 2 * SPAN
 QUARTER = SPAN // 4
 BLOCK = 1024
-TURN_OUT, TURN_BACK = 28, 24
+TURN_OUT, TURN_BACK = 26, 24
 F32, BF16 = jnp.float32, jnp.bfloat16
 
 
@@ -146,10 +146,10 @@
         series = jnp.transpose((a * b).astype(BF16)).reshape(count, 32, SPAN)
         far = int(2 * j >= chunks)
         mine = jnp.where(core, quarters[far], quarters[2 + far]).astype(BF16)
-        for piece in range(0, count, 4):
-            rows = pl.ds((j * count + piece) ^ TURN_OUT, 4)
-            out_buf[rows, 0:32, :] = series[piece:piece + 4]
-            out_buf[rows, 32:40, :] = jnp.broadcast_to(mine[None], (4, 8, SPAN))
+        for piece in range(0, count, 2):
+            rows = pl.ds((j * count + piece) ^ TURN_OUT, 2)
+            out_buf[rows, 0:32, :] = series[piece:piece + 2]
+            out_buf[rows, 32:40, :] = jnp.broadcast_to(mine[None], (2, 8, SPAN))
         rows = pl.ds((j * count) ^ (TURN_OUT // count * count), count)
         out = pltpu.make_async_copy(out_buf.at[rows], out_hbm.at[rows], out_sem.at[j])
         out.start()
@@ -301,9 +301,9 @@
         xs, gs = xs_ref[:, cols], gs_ref[:, cols]
 
         def rows(ref, start):
-            blocks = range(j * BLOCK // SPAN, (j + 1) * BLOCK // SPAN)
-            places = [start + 32 * (b ^ (TURN_OUT // 4)) for b in blocks]
-            return jnp.concatenate([ref[p:p + 32, :].astype(F32) for p in places], 0)
+            blocks = range(j * BLOCK // 64, (j + 1) * BLOCK // 64)
+            places = [start + 16 * (b ^ (TURN_OUT // 2)) for b in blocks]
+            return jnp.concatenate([ref[p:p + 16, :].astype(F32) for p in places], 0)
 
         own, side = rows(own_ref, 0), rows(own_ref, 256)
         core, cross = rows(core_ref, 0), rows(core_ref, 256)
@@ -488,7 +488,7 @@
         compiler_params=params(),
         cost_estimate=cost(area, 4 * area),
         name="load",
-    )(back, keep, side, near, cross)
+    )(back, keep, cross, near, side)
     landed = exchange(back, TURN_BACK)
 
     own = got[:, 32:40, :].reshape(parts * 8, SPAN)

time: 74.4 us -> 73.6 us (0.989)
    ppermute x1, starting transfers between devices: 2.12 us -> 4.65 us  [per_device(): side = lax.ppermute(side, 'ctx', side_swap)]
    ppermute x1, starting transfers between devices: 4.66 us -> 3.04 us  [per_device(): cross = lax.ppermute(cross, 'ctx', cross_swap)]
    all_to_all x2, waiting for transfers between devices: 2.58 us -> 1.27 us  [exchange(): lax.all_to_all(array, 'ctx', split_axis=0, concat_axis=0, axis_index_grou...]
    ppermute x1, starting transfers between devices: 5.82 us -> 4.86 us  [per_device(): core = lax.ppermute(own, 'dp', core_swap)]
    ppermute x1, waiting for transfers between devices: 0.01 us -> 0.91 us  [per_device(): near = lax.ppermute(near, 'ctx', next_swap)]
    ppermute x1, starting transfers between devices: 3.09 us -> 2.19 us  [per_device(): near = lax.ppermute(near, 'ctx', next_swap)]
    all_to_all x2, starting transfers between devices: 33.6 us -> 34.4 us  [exchange(): lax.all_to_all(array, 'ctx', split_axis=0, concat_axis=0, axis_index_grou...]
  transfers between devices with their start and end apart: 8 -> 8, of which waited for: 3 -> 5; matrix products, arithmetic and copies ran while one was open for 0% -> 0% of each run, Pallas kernels for 9% -> 9%
where the time goes in v6:
time: 73.6 us; the launch traced here: 73.1 us
  starting transfers between devices  54.4 us (74%)
  Pallas kernels  11.1 us (15%)
  waiting for transfers between devices  6.62 us (9%)
  between operations  0.97 us (1%)
    all_to_all x2, starting transfers between devices, exchange(): lax.all_to_all(array, 'ctx', split_axis=0, concat_axis=0, axis_index_grou...  34.4 us
    ppermute x1, starting transfers between devices, per_device(): core = lax.ppermute(own, 'dp', core_swap)  4.86 us
    ppermute x1, starting transfers between devices, per_device(): side = lax.ppermute(side, 'ctx', side_swap)  4.65 us
    ppermute x1, waiting for transfers between devices, per_device(): lax.ppermute(own, 'ctx', side_swap)  3.44 us
    ppermute x1, starting transfers between devices, per_device(): taken = lax.ppermute(give, 'dp', core_swap)  3.14 us
    ppermute x1, starting transfers between devices, per_device(): cross = lax.ppermute(cross, 'ctx', cross_swap)  3.04 us
    pallas_call x1, Pallas kernels, per_device(): pl.pallas_call(send_kernel, out_shape=chunk, in_specs=[HBM] * 7, out_spec...  2.26 us
    ppermute x1, starting transfers between devices, per_device(): near = lax.ppermute(near, 'ctx', next_swap)  2.19 us
  transfers between devices with their start and end apart: 8, of which 5 were waited for; matrix products, arithmetic and copies ran while one was open for 0% of the time, Pallas kernels for 9%

profile of v6, /device:TPU:1, one launch (start us, length us, event | category | flops | bytes accessed | tf_op | source)
XLA Modules:
  0.0 73.1 jit_solution(11013121942163471368)
XLA Ops:
  0.6 0.0 copy-start.2
  0.6 0.0 copy-start.4
  0.7 0.0 copy-start.10
  0.7 2.3 %send.1 = bf16[32,40,128]{2,1,0:T(8,128)(2,1)} custom-call(s32[1,32]{1,0:T(1,128)} %slot_hbm.1, s32[1,24]{1,0:T(1,128)} %len_hbm.1, bf16[32,256]{1,0:T(8,128)(2,1)} %bitcast.4, bf16[128,1024]{1,0:T(8,128)(2,1)} %q_ref.3, bf16[128,1024]{1,0:T(8,128)(2,1)} %k_ref.5, bf16[128,1024]{1,0:T(8,128)(2,1)} %v_ref.5, bf16[128,1024]{1,0:T(8,128)(2,1)} %c_ref.5), custom_call_target="tpu_custom_call" | custom-call | flops 262144 | bytes 1048576 | tf_op jit(solution)/shard_map/send/pallas_call | solution.py:418
  2.9 0.0 copy-start
  2.9 0.0 copy-start.1
  3.0 0.0 copy-start.9
  3.0 20.1 %all-to-all-start = ((bf16[32,40,128]{2,1,0:T(8,128)(2,1)}), bf16[32,40,128]{2,1,0:T(8,128)(2,1)S(1)}, u32[]{:S(2)}, u32[]{:S(2)}) async-start(bf16[32,40,128]{2,1,0:T(8,128)(2,1)} %send.1), calls=%async_computation | async-start | bytes 655360 | tf_op jit(solution)/shard_map/all_to_all | solution.py:413
  23.1 0.0 copy-done.2
  23.1 0.0 copy-done.4
  23.1 0.0 copy-done.10
  23.1 0.0 copy-done
  23.1 0.0 copy-done.1
  23.2 0.0 copy-start.3
  23.2 0.0 copy-start.5
  23.2 0.0 copy-start.6
  23.2 0.0 copy-start.7
  23.2 1.2 %partial_taps.1.after_ref.own_ref = bf16[4,256,128]{2,1,0:T(8,128)(2,1)S(1)} custom-call(bf16[128,1024]{1,0:T(8,128)(2,1)S(1)} %copy-done.4, bf16[128,1024]{1,0:T(8,128)(2,1)S(1)} %copy-done, bf16[128,1024]{1,0:T(8,128)(2,1)S(1)} %copy-done.1, bf16[128,1024]{1,0:T(8,128)(2,1)S(1)} %copy-done.2, bf16[256,256]{1,0:T(8,128)(2,1)S(1)} %copy-done.9, ...), custom_call_target="tpu_custom_call" | custom-call | flops 2000000000 | bytes 1310720 | tf_op jit(solution)/shard_map/partial_taps/pallas_call | solution.py:436
  24.4 3.1 %collective-permute-start = (bf16[4,256,128]{2,1,0:T(8,128)(2,1)S(1)}, bf16[4,256,128]{2,1,0:T(8,128)(2,1)S(1)}, u32[]{:S(2)}, u32[]{:S(2)}) collective-permute-start(bf16[4,256,128]{2,1,0:T(8,128)(2,1)S(1)} %partial_taps.1.after_ref.own_ref), channel_id=1, source_target_pairs={{0,256},{256,0},{1,257},{257,1},{2,258},{258,2},{3,259},{259,3},{4... | collective-permute-start | bytes 786440 | tf_op jit(solution)/shard_map/ppermute | solution.py:445
  27.5 0.0 copy-done.3
  27.5 0.0 copy-done.5
  27.6 0.0 copy-done.6
  27.6 0.0 copy-done.7
  27.6 1.4 %tables.1 = (s32[3,16]{1,0:T(4,128)S(1)}, f32[32,256]{1,0:T(8,128)S(1)}) custom-call(s32[1,32]{1,0:T(1,128)S(1)} %copy-done.6, s32[1,24]{1,0:T(1,128)S(1)} %copy-done.7, bf16[32,256]{1,0:T(8,128)(2,1)S(1)} %bitcast.5, bf16[512,256]{1,0:T(8,128)(2,1)S(1)} %copy-done.3, bf16[4,256,128]{2,1,0:T(8,128)(2,1)S(1)} %partial_taps.1.after_ref.own_ref), custom_call_target="tpu_custom_call" | custom-call | flops 131072 | bytes 131072 | tf_op jit(solution)/shard_map/tables/pallas_call | solution.py:456
  29.0 0.0 copy-start.11
  29.0 0.0 copy-start.12
  29.0 0.0 collective-permute-done.other_ref
  29.0 0.1 share.1
  29.1 3.0 %collective-permute-start.1 = (bf16[256,128]{1,0:T(8,128)(2,1)S(1)}, bf16[256,128]{1,0:T(8,128)(2,1)S(1)}, u32[]{:S(2)}, u32[]{:S(2)}) collective-permute-start(bf16[256,128]{1,0:T(8,128)(2,1)S(1)} %get-tuple-element.22), channel_id=1, source_target_pairs={{0,136},{8,128},{16,152},{24,144},{32,168},{40,160},{48,184},{56,1... | collective-permute-start | bytes 196616 | tf_op jit(solution)/shard_map/ppermute | solution.py:471
  32.2 2.2 %collective-permute-start.2 = (bf16[256,128]{1,0:T(8,128)(2,1)S(1)}, bf16[256,128]{1,0:T(8,128)(2,1)S(1)}, u32[]{:S(2)}, u32[]{:S(2)}) collective-permute-start(bf16[256,128]{1,0:T(8,128)(2,1)S(1)} %get-tuple-element.23), channel_id=1, source_target_pairs={{0,8},{8,0},{16,24},{24,16},{32,40},{40,32},{48,56},{56,48},{64,72... | collective-permute-start | bytes 196616 | tf_op jit(solution)/shard_map/ppermute | solution.py:470
  34.4 4.6 %collective-permute-start.3 = (bf16[256,128]{1,0:T(8,128)(2,1)S(1)}, bf16[256,128]{1,0:T(8,128)(2,1)S(1)}, u32[]{:S(2)}, u32[]{:S(2)}) collective-permute-start(bf16[256,128]{1,0:T(8,128)(2,1)S(1)} %get-tuple-element.24), channel_id=1, source_target_pairs={{0,128},{8,136},{16,144},{24,152},{32,160},{40,168},{48,176},{56,1... | collective-permute-start | bytes 196616 | tf_op jit(solution)/shard_map/ppermute | solution.py:469
  39.0 0.4 all-to-all-done.got_ref
  39.4 0.0 copy-done.12
  39.4 1.1 %pair.1.pair_ref = bf16[32,32,128]{2,1,0:T(8,128)(2,1)S(1)} custom-call(s32[3,16]{1,0:T(4,128)S(1)} %get-tuple-element.19.table_ref, bf16[32,40,128]{2,1,0:T(8,128)(2,1)S(1)} %all-to-all-done.got_ref, f32[32,256]{1,0:T(8,128)S(1)} %get-tuple-element.20.spec_ref, bf16[256,256]{1,0:T(8,128)(2,1)S(1)} %copy-done.11, bf16[256,256]{1,0:T(8,128)(2,1)S(1)} %copy-done.12), custom_call_target="tpu_custom_call" | custom-call | flops 1000000000 | bytes 1048576 | tf_op jit(solution)/shard_map/pair/pallas_call | solution.py:473
  40.5 0.0 collective-permute-done.1.side_ref
  40.5 0.9 %collective-permute-done.2.next_ref = bf16[256,128]{1,0:T(8,128)(2,1)S(1)} collective-permute-done((bf16[256,128]{1,0:T(8,128)(2,1)S(1)}, bf16[256,128]{1,0:T(8,128)(2,1)S(1)}, u32[]{:S(2)}, u32[]{:S(2)}) %collective-permute-start.2) | collective-permute-done | bytes 65568 | tf_op jit(solution)/shard_map/ppermute | solution.py:470
  41.4 0.0 collective-permute-done.3.cross_ref
  41.4 0.8 %load.1 = bf16[32,40,128]{2,1,0:T(8,128)(2,1)} custom-call(bf16[32,32,128]{2,1,0:T(8,128)(2,1)S(1)} %pair.1.pair_ref, f32[256,128]{1,0:T(8,128)S(1)} %get-tuple-element.21.keep_ref, bf16[256,128]{1,0:T(8,128)(2,1)S(1)} %collective-permute-done.1.side_ref, bf16[256,128]{1,0:T(8,128)(2,1)S(1)} %collective-permute-done.2.next_ref, ...), custom_call_target="tpu_custom_call" | custom-call | flops 131072 | bytes 524288 | tf_op jit(solution)/shard_map/load/pallas_call | solution.py:482
  42.2 0.0 copy-start.8
  42.2 14.2 %all-to-all-start.1 = ((bf16[32,40,128]{2,1,0:T(8,128)(2,1)}), bf16[32,40,128]{2,1,0:T(8,128)(2,1)S(1)}, u32[]{:S(2)}, u32[]{:S(2)}) async-start(bf16[32,40,128]{2,1,0:T(8,128)(2,1)} %load.1), calls=%async_computation.1 | async-start | bytes 655360 | tf_op jit(solution)/shard_map/all_to_all | solution.py:413
  56.5 2.2 %collective-permute-start.4 = (bf16[256,128]{1,0:T(8,128)(2,1)S(1)}, bf16[256,128]{1,0:T(8,128)(2,1)S(1)}, u32[]{:S(2)}, u32[]{:S(2)}) collective-permute-start(bf16[256,128]{1,0:T(8,128)(2,1)S(1)} %slice_bitcast_fusion), channel_id=1, source_target_pairs={{0,128},{8,136},{16,144},{24,152},{32,160},{40,168},{48,176},{56,1... | collective-permute-start | bytes 196616 | tf_op jit(solution)/shard_map/ppermute | solution.py:505
  58.7 1.3 %pair_taps.1 = (bf16[64,128]{1,0:T(8,128)(2,1)S(1)}, f32[256,1024]{1,0:T(8,128)S(1)}, f32[256,1024]{1,0:T(8,128)S(1)}) custom-call(s32[3,16]{1,0:T(4,128)S(1)} %get-tuple-element.19.table_ref, bf16[32,40,128]{2,1,0:T(8,128)(2,1)S(1)} %all-to-all-done.got_ref, bf16[128,1024]{1,0:T(8,128)(2,1)S(1)} %copy-done.4, bf16[128,1024]{1,0:T(8,128)(2,1)S(1)} %copy-done, ...), custom_call_target="tpu_custom_call" | custom-call | flops 1000000000 | bytes 786432 | tf_op jit(solution)/shard_map/pair_taps/pallas_call | solution.py:495
  59.9 3.4 %collective-permute-done.4 = bf16[256,128]{1,0:T(8,128)(2,1)S(1)} collective-permute-done((bf16[256,128]{1,0:T(8,128)(2,1)S(1)}, bf16[256,128]{1,0:T(8,128)(2,1)S(1)}, u32[]{:S(2)}, u32[]{:S(2)}) %collective-permute-start.4) | collective-permute-done | bytes 65568 | tf_op jit(solution)/shard_map/ppermute | solution.py:505
  63.4 4.9 %collective-permute-start.5 = (bf16[576,128]{1,0:T(8,128)(2,1)S(1)}, bf16[576,128]{1,0:T(8,128)(2,1)S(1)}, u32[]{:S(2)}, u32[]{:S(2)}) collective-permute-start(bf16[576,128]{1,0:T(8,128)(2,1)S(1)} %pad_maximum_fusion.own_ref), channel_id=1, source_target_pairs={{0,256},{256,0},{1,257},{257,1},{2,258},{258,2},{3,259},{259,3},{4... | collective-permute-start | bytes 442376 | tf_op jit(solution)/shard_map/ppermute | solution.py:506
  68.2 1.0 %collective-permute-done.5.core_ref = bf16[576,128]{1,0:T(8,128)(2,1)S(1)} collective-permute-done((bf16[576,128]{1,0:T(8,128)(2,1)S(1)}, bf16[576,128]{1,0:T(8,128)(2,1)S(1)}, u32[]{:S(2)}, u32[]{:S(2)}) %collective-permute-start.5) | collective-permute-done | bytes 147488 | tf_op jit(solution)/shard_map/ppermute | solution.py:506
  69.2 1.3 %local.1 = (f32[128,1024]{1,0:T(8,128)S(1)}, f32[128,1024]{1,0:T(8,128)S(1)}) custom-call(bf16[576,128]{1,0:T(8,128)(2,1)S(1)} %pad_maximum_fusion.own_ref, bf16[576,128]{1,0:T(8,128)(2,1)S(1)} %collective-permute-done.5.core_ref, f32[256,1024]{1,0:T(8,128)S(1)} %get-tuple-element.26.xs_ref, f32[256,1024]{1,0:T(8,128)S(1)} %get-tuple-element.27.gs_ref, ...), custom_call_target="tpu_custom_call" | custom-call | flops 3000000000 | bytes 2621440 | tf_op jit(solution)/shard_map/local/pallas_call | solution.py:507
  70.5 0.9 %all-to-all-done.1.got_ref = bf16[32,40,128]{2,1,0:T(8,128)(2,1)S(1)} async-done(((bf16[32,40,128]{2,1,0:T(8,128)(2,1)}), bf16[32,40,128]{2,1,0:T(8,128)(2,1)S(1)}, u32[]{:S(2)}, u32[]{:S(2)}) %all-to-all-start.1) | async-done | bytes 327712 | tf_op jit(solution)/shard_map/all_to_all | solution.py:413
  71.4 1.7 %finish.1 = (bf16[128,1024]{1,0:T(8,128)(2,1)}, bf16[128,1024]{1,0:T(8,128)(2,1)}, bf16[128,1024]{1,0:T(8,128)(2,1)}, bf16[32,256]{1,0:T(8,128)(2,1)}) custom-call(s32[3,16]{1,0:T(4,128)S(1)} %get-tuple-element.19.table_ref, bf16[32,40,128]{2,1,0:T(8,128)(2,1)S(1)} %all-to-all-done.1.got_ref, f32[128,1024]{1,0:T(8,128)S(1)} %get-tuple-element.28.mixed_ref, ...), custom_call_target="tpu_custom_call" | custom-call | flops 1310720 | bytes 2621440 | tf_op jit(solution)/shard_map/finish/pallas_call | solution.py:518
  (5 shorter events, 0.0 us)
Async XLA Ops:
  0.6 22.5 %copy-start.2 = (bf16[128,1024]{1,0:T(8,128)(2,1)S(1)}, bf16[128,1024]{1,0:T(8,128)(2,1)}, u32[]{:S(2)}) copy-start(bf16[128,1024]{1,0:T(8,128)(2,1)} %c_ref.5) | copy-start | bytes 786436
  0.6 22.5 %copy-start.4 = (bf16[128,1024]{1,0:T(8,128)(2,1)S(1)}, bf16[128,1024]{1,0:T(8,128)(2,1)}, u32[]{:S(2)}) copy-start(bf16[128,1024]{1,0:T(8,128)(2,1)} %q_ref.3) | copy-start | bytes 786436
  0.7 22.5 %copy-start.10 = (bf16[256,256]{1,0:T(8,128)(2,1)S(1)}, bf16[256,256]{1,0:T(8,128)(2,1)}, u32[]{:S(2)}) copy-start(bf16[256,256]{1,0:T(8,128)(2,1)} %constant.14.clone.inv) | copy-start | bytes 393220
  2.9 20.2 %copy-start = (bf16[128,1024]{1,0:T(8,128)(2,1)S(1)}, bf16[128,1024]{1,0:T(8,128)(2,1)}, u32[]{:S(2)}) copy-start(bf16[128,1024]{1,0:T(8,128)(2,1)} %k_ref.5) | copy-start | bytes 786436
  2.9 20.2 %copy-start.1 = (bf16[128,1024]{1,0:T(8,128)(2,1)S(1)}, bf16[128,1024]{1,0:T(8,128)(2,1)}, u32[]{:S(2)}) copy-start(bf16[128,1024]{1,0:T(8,128)(2,1)} %v_ref.5) | copy-start | bytes 786436
  3.0 20.2 %copy-start.9 = (bf16[256,256]{1,0:T(8,128)(2,1)S(1)}, bf16[256,256]{1,0:T(8,128)(2,1)}, u32[]{:S(2)}) copy-start(bf16[256,256]{1,0:T(8,128)(2,1)} %constant.12.clone.fwd.own_fwd) | copy-start | bytes 393220
  3.0 36.4 %all-to-all-start = ((bf16[32,40,128]{2,1,0:T(8,128)(2,1)}), bf16[32,40,128]{2,1,0:T(8,128)(2,1)S(1)}, u32[]{:S(2)}, u32[]{:S(2)}) async-start(bf16[32,40,128]{2,1,0:T(8,128)(2,1)} %send.1), calls=%async_computation | async-start | bytes 655360 | tf_op jit(solution)/shard_map/all_to_all | solution.py:413
  23.2 4.4 %copy-start.3 = (bf16[512,256]{1,0:T(8,128)(2,1)S(1)}, bf16[512,256]{1,0:T(8,128)(2,1)}, u32[]{:S(2)}) copy-start(bf16[512,256]{1,0:T(8,128)(2,1)} %constant.16.clone.tap) | copy-start | bytes 786436
  23.2 4.4 %copy-start.5 = (bf16[256,32]{0,1:T(8,128)(2,1)S(1)}, bf16[256,32]{0,1:T(8,128)(2,1)}, u32[]{:S(2)}) copy-start(bf16[256,32]{0,1:T(8,128)(2,1)} %param.17) | copy-start | bytes 49156
  23.2 4.4 %copy-start.6 = (s32[1,32]{1,0:T(1,128)S(1)}, s32[1,32]{1,0:T(1,128)}, u32[]{:S(2)}) copy-start(s32[1,32]{1,0:T(1,128)} %slot_hbm.1) | copy-start | bytes 388
  23.2 4.4 %copy-start.7 = (s32[1,24]{1,0:T(1,128)S(1)}, s32[1,24]{1,0:T(1,128)}, u32[]{:S(2)}) copy-start(s32[1,24]{1,0:T(1,128)} %len_hbm.1) | copy-start | bytes 292
  24.4 4.6 %collective-permute-start = (bf16[4,256,128]{2,1,0:T(8,128)(2,1)S(1)}, bf16[4,256,128]{2,1,0:T(8,128)(2,1)S(1)}, u32[]{:S(2)}, u32[]{:S(2)}) collective-permute-start(bf16[4,256,128]{2,1,0:T(8,128)(2,1)S(1)} %partial_taps.1.after_ref.own_ref), channel_id=1, source_target_pairs={{0,256},{256,0},{1,257},{257,1},{2,258},{258,2},{3,259},{259,3},{4... | collective-permute-start | bytes 786440 | tf_op jit(solution)/shard_map/ppermute | solution.py:445
  29.0 10.4 %copy-start.11 = (bf16[256,256]{1,0:T(8,128)(2,1)S(1)}, bf16[256,256]{1,0:T(8,128)(2,1)}, u32[]{:S(2)}) copy-start(bf16[256,256]{1,0:T(8,128)(2,1)} %constant.13.clone.fwd) | copy-start | bytes 393220
  29.0 10.4 %copy-start.12 = (bf16[256,256]{1,0:T(8,128)(2,1)S(1)}, bf16[256,256]{1,0:T(8,128)(2,1)}, u32[]{:S(2)}) copy-start(bf16[256,256]{1,0:T(8,128)(2,1)} %constant.15.clone.inv) | copy-start | bytes 393220
  29.1 11.4 %collective-permute-start.1 = (bf16[256,128]{1,0:T(8,128)(2,1)S(1)}, bf16[256,128]{1,0:T(8,128)(2,1)S(1)}, u32[]{:S(2)}, u32[]{:S(2)}) collective-permute-start(bf16[256,128]{1,0:T(8,128)(2,1)S(1)} %get-tuple-element.22), channel_id=1, source_target_pairs={{0,136},{8,128},{16,152},{24,144},{32,168},{40,160},{48,184},{56,1... | collective-permute-start | bytes 196616 | tf_op jit(solution)/shard_map/ppermute | solution.py:471
  32.2 9.3 %collective-permute-start.2 = (bf16[256,128]{1,0:T(8,128)(2,1)S(1)}, bf16[256,128]{1,0:T(8,128)(2,1)S(1)}, u32[]{:S(2)}, u32[]{:S(2)}) collective-permute-start(bf16[256,128]{1,0:T(8,128)(2,1)S(1)} %get-tuple-element.23), channel_id=1, source_target_pairs={{0,8},{8,0},{16,24},{24,16},{32,40},{40,32},{48,56},{56,48},{64,72... | collective-permute-start | bytes 196616 | tf_op jit(solution)/shard_map/ppermute | solution.py:470
  34.4 7.1 %collective-permute-start.3 = (bf16[256,128]{1,0:T(8,128)(2,1)S(1)}, bf16[256,128]{1,0:T(8,128)(2,1)S(1)}, u32[]{:S(2)}, u32[]{:S(2)}) collective-permute-start(bf16[256,128]{1,0:T(8,128)(2,1)S(1)} %get-tuple-element.24), channel_id=1, source_target_pairs={{0,128},{8,136},{16,144},{24,152},{32,160},{40,168},{48,176},{56,1... | collective-permute-start | bytes 196616 | tf_op jit(solution)/shard_map/ppermute | solution.py:469
  42.2 16.4 %copy-start.8 = (bf16[256,512]{1,0:T(8,128)(2,1)S(1)}, bf16[256,512]{1,0:T(8,128)(2,1)}, u32[]{:S(2)}) copy-start(bf16[256,512]{1,0:T(8,128)(2,1)} %constant.17.clone.lag) | copy-start | bytes 786436
  42.2 29.2 %all-to-all-start.1 = ((bf16[32,40,128]{2,1,0:T(8,128)(2,1)}), bf16[32,40,128]{2,1,0:T(8,128)(2,1)S(1)}, u32[]{:S(2)}, u32[]{:S(2)}) async-start(bf16[32,40,128]{2,1,0:T(8,128)(2,1)} %load.1), calls=%async_computation.1 | async-start | bytes 655360 | tf_op jit(solution)/shard_map/all_to_all | solution.py:413
  56.5 6.9 %collective-permute-start.4 = (bf16[256,128]{1,0:T(8,128)(2,1)S(1)}, bf16[256,128]{1,0:T(8,128)(2,1)S(1)}, u32[]{:S(2)}, u32[]{:S(2)}) collective-permute-start(bf16[256,128]{1,0:T(8,128)(2,1)S(1)} %slice_bitcast_fusion), channel_id=1, source_target_pairs={{0,128},{8,136},{16,144},{24,152},{32,160},{40,168},{48,176},{56,1... | collective-permute-start | bytes 196616 | tf_op jit(solution)/shard_map/ppermute | solution.py:505
  63.4 5.9 %collective-permute-start.5 = (bf16[576,128]{1,0:T(8,128)(2,1)S(1)}, bf16[576,128]{1,0:T(8,128)(2,1)S(1)}, u32[]{:S(2)}, u32[]{:S(2)}) collective-permute-start(bf16[576,128]{1,0:T(8,128)(2,1)S(1)} %pad_maximum_fusion.own_ref), channel_id=1, source_target_pairs={{0,256},{256,0},{1,257},{257,1},{2,258},{258,2},{3,259},{259,3},{4... | collective-permute-start | bytes 442376 | tf_op jit(solution)/shard_map/ppermute | solution.py:506

commit v7 on v6

--- a/solution.py
+++ b/solution.py
@@ -233,13 +233,16 @@
     zero = lax.broadcasted_iota(jnp.int32, hr.shape, 1) == 0
     spec = pair_spectra(table_ref, got_ref, fwd)
     out_ref[...] = jnp.zeros((slots, 32, SPAN), BF16)
+    both = []
     for k in range(2):
         sr, si = spec[k, :, :, :SPAN], spec[k, :, :, SPAN:]
         pr, pi = multiply(sr, si, hr[None], hi[None], zero[None], 1.0 if k == 0 else -1.0)
-        both = jnp.concatenate([pr, pi], 2).reshape(pairs * 32, PTS)
-        result = invert_right(both, inv[...]).astype(BF16)
+        both.append(jnp.concatenate([pr, pi], 2).reshape(pairs * 32, PTS))
+    result = invert_right(jnp.concatenate(both, 0), inv[...]).astype(BF16)
+    for k in range(2):
         for p in range(pairs):
-            out_ref[table_ref[1 - k, p] ^ TURN_BACK] = result[32 * p:32 * p + 32]
+            row = 32 * (k * pairs + p)
+            out_ref[table_ref[1 - k, p] ^ TURN_BACK] = result[row:row + 32]
 
 
 def load_kernel(

time: 73.6 us -> 73.6 us (level)
  no operation moved by 1% of the time
where the time goes in v7:
time: 73.6 us; the launch traced here: 73.1 us
  starting transfers between devices  54.4 us (74%)
  Pallas kernels  11 us (15%)
  waiting for transfers between devices  6.7 us (9%)
  between operations  0.97 us (1%)
    all_to_all x2, starting transfers between devices, exchange(): lax.all_to_all(array, 'ctx', split_axis=0, concat_axis=0, axis_index_grou...  34.4 us
    ppermute x1, starting transfers between devices, per_device(): core = lax.ppermute(own, 'dp', core_swap)  4.86 us
    ppermute x1, starting transfers between devices, per_device(): side = lax.ppermute(side, 'ctx', side_swap)  4.65 us
    ppermute x1, waiting for transfers between devices, per_device(): lax.ppermute(own, 'ctx', side_swap)  3.44 us
    ppermute x1, starting transfers between devices, per_device(): taken = lax.ppermute(give, 'dp', core_swap)  3.14 us
    ppermute x1, starting transfers between devices, per_device(): cross = lax.ppermute(cross, 'ctx', cross_swap)  3.04 us
    pallas_call x1, Pallas kernels, per_device(): pl.pallas_call(send_kernel, out_shape=chunk, in_specs=[HBM] * 7, out_spec...  2.26 us
    ppermute x1, starting transfers between devices, per_device(): near = lax.ppermute(near, 'ctx', next_swap)  2.19 us
  transfers between devices with their start and end apart: 8, of which 5 were waited for; matrix products, arithmetic and copies ran while one was open for 0% of the time, Pallas kernels for 9%

profile of v7, /device:TPU:1, one launch (start us, length us, event | category | flops | bytes accessed | tf_op | source)
XLA Modules:
  0.0 73.1 jit_solution(2496677496414487277)
XLA Ops:
  0.6 0.0 copy-start.2
  0.6 0.0 copy-start.4
  0.7 0.0 copy-start.10
  0.7 2.3 %send.1 = bf16[32,40,128]{2,1,0:T(8,128)(2,1)} custom-call(s32[1,32]{1,0:T(1,128)} %slot_hbm.1, s32[1,24]{1,0:T(1,128)} %len_hbm.1, bf16[32,256]{1,0:T(8,128)(2,1)} %bitcast.4, bf16[128,1024]{1,0:T(8,128)(2,1)} %q_ref.3, bf16[128,1024]{1,0:T(8,128)(2,1)} %k_ref.5, bf16[128,1024]{1,0:T(8,128)(2,1)} %v_ref.5, bf16[128,1024]{1,0:T(8,128)(2,1)} %c_ref.5), custom_call_target="tpu_custom_call" | custom-call | flops 262144 | bytes 1048576 | tf_op jit(solution)/shard_map/send/pallas_call | solution.py:421
  2.9 0.0 copy-start
  2.9 0.0 copy-start.1
  3.0 0.0 copy-start.9
  3.0 20.1 %all-to-all-start = ((bf16[32,40,128]{2,1,0:T(8,128)(2,1)}), bf16[32,40,128]{2,1,0:T(8,128)(2,1)S(1)}, u32[]{:S(2)}, u32[]{:S(2)}) async-start(bf16[32,40,128]{2,1,0:T(8,128)(2,1)} %send.1), calls=%async_computation | async-start | bytes 655360 | tf_op jit(solution)/shard_map/all_to_all | solution.py:416
  23.1 0.0 copy-done.2
  23.1 0.0 copy-done.4
  23.1 0.0 copy-done.10
  23.1 0.0 copy-done
  23.1 0.0 copy-done.1
  23.2 0.0 copy-start.3
  23.2 0.0 copy-start.5
  23.2 0.0 copy-start.6
  23.2 0.0 copy-start.7
  23.2 1.2 %partial_taps.1.after_ref.own_ref = bf16[4,256,128]{2,1,0:T(8,128)(2,1)S(1)} custom-call(bf16[128,1024]{1,0:T(8,128)(2,1)S(1)} %copy-done.4, bf16[128,1024]{1,0:T(8,128)(2,1)S(1)} %copy-done, bf16[128,1024]{1,0:T(8,128)(2,1)S(1)} %copy-done.1, bf16[128,1024]{1,0:T(8,128)(2,1)S(1)} %copy-done.2, bf16[256,256]{1,0:T(8,128)(2,1)S(1)} %copy-done.9, ...), custom_call_target="tpu_custom_call" | custom-call | flops 2000000000 | bytes 1310720 | tf_op jit(solution)/shard_map/partial_taps/pallas_call | solution.py:439
  24.4 3.1 %collective-permute-start = (bf16[4,256,128]{2,1,0:T(8,128)(2,1)S(1)}, bf16[4,256,128]{2,1,0:T(8,128)(2,1)S(1)}, u32[]{:S(2)}, u32[]{:S(2)}) collective-permute-start(bf16[4,256,128]{2,1,0:T(8,128)(2,1)S(1)} %partial_taps.1.after_ref.own_ref), channel_id=1, source_target_pairs={{0,256},{256,0},{1,257},{257,1},{2,258},{258,2},{3,259},{259,3},{4... | collective-permute-start | bytes 786440 | tf_op jit(solution)/shard_map/ppermute | solution.py:448
  27.5 0.0 copy-done.3
  27.5 0.0 copy-done.5
  27.6 0.0 copy-done.6
  27.6 0.0 copy-done.7
  27.6 1.4 %tables.1 = (s32[3,16]{1,0:T(4,128)S(1)}, f32[32,256]{1,0:T(8,128)S(1)}) custom-call(s32[1,32]{1,0:T(1,128)S(1)} %copy-done.6, s32[1,24]{1,0:T(1,128)S(1)} %copy-done.7, bf16[32,256]{1,0:T(8,128)(2,1)S(1)} %bitcast.5, bf16[512,256]{1,0:T(8,128)(2,1)S(1)} %copy-done.3, bf16[4,256,128]{2,1,0:T(8,128)(2,1)S(1)} %partial_taps.1.after_ref.own_ref), custom_call_target="tpu_custom_call" | custom-call | flops 131072 | bytes 131072 | tf_op jit(solution)/shard_map/tables/pallas_call | solution.py:459
  29.0 0.0 copy-start.11
  29.0 0.0 copy-start.12
  29.0 0.0 collective-permute-done.other_ref
  29.0 0.1 share.1
  29.1 3.0 %collective-permute-start.1 = (bf16[256,128]{1,0:T(8,128)(2,1)S(1)}, bf16[256,128]{1,0:T(8,128)(2,1)S(1)}, u32[]{:S(2)}, u32[]{:S(2)}) collective-permute-start(bf16[256,128]{1,0:T(8,128)(2,1)S(1)} %get-tuple-element.22), channel_id=1, source_target_pairs={{0,136},{8,128},{16,152},{24,144},{32,168},{40,160},{48,184},{56,1... | collective-permute-start | bytes 196616 | tf_op jit(solution)/shard_map/ppermute | solution.py:474
  32.2 2.2 %collective-permute-start.2 = (bf16[256,128]{1,0:T(8,128)(2,1)S(1)}, bf16[256,128]{1,0:T(8,128)(2,1)S(1)}, u32[]{:S(2)}, u32[]{:S(2)}) collective-permute-start(bf16[256,128]{1,0:T(8,128)(2,1)S(1)} %get-tuple-element.23), channel_id=1, source_target_pairs={{0,8},{8,0},{16,24},{24,16},{32,40},{40,32},{48,56},{56,48},{64,72... | collective-permute-start | bytes 196616 | tf_op jit(solution)/shard_map/ppermute | solution.py:473
  34.4 4.6 %collective-permute-start.3 = (bf16[256,128]{1,0:T(8,128)(2,1)S(1)}, bf16[256,128]{1,0:T(8,128)(2,1)S(1)}, u32[]{:S(2)}, u32[]{:S(2)}) collective-permute-start(bf16[256,128]{1,0:T(8,128)(2,1)S(1)} %get-tuple-element.24), channel_id=1, source_target_pairs={{0,128},{8,136},{16,144},{24,152},{32,160},{40,168},{48,176},{56,1... | collective-permute-start | bytes 196616 | tf_op jit(solution)/shard_map/ppermute | solution.py:472
  39.0 0.4 all-to-all-done.got_ref
  39.4 0.0 copy-done.12
  39.4 1.0 %pair.1.pair_ref = bf16[32,32,128]{2,1,0:T(8,128)(2,1)S(1)} custom-call(s32[3,16]{1,0:T(4,128)S(1)} %get-tuple-element.19.table_ref, bf16[32,40,128]{2,1,0:T(8,128)(2,1)S(1)} %all-to-all-done.got_ref, f32[32,256]{1,0:T(8,128)S(1)} %get-tuple-element.20.spec_ref, bf16[256,256]{1,0:T(8,128)(2,1)S(1)} %copy-done.11, bf16[256,256]{1,0:T(8,128)(2,1)S(1)} %copy-done.12), custom_call_target="tpu_custom_call" | custom-call | flops 1000000000 | bytes 1048576 | tf_op jit(solution)/shard_map/pair/pallas_call | solution.py:476
  40.4 0.0 collective-permute-done.1.side_ref
  40.4 1.0 %collective-permute-done.2.next_ref = bf16[256,128]{1,0:T(8,128)(2,1)S(1)} collective-permute-done((bf16[256,128]{1,0:T(8,128)(2,1)S(1)}, bf16[256,128]{1,0:T(8,128)(2,1)S(1)}, u32[]{:S(2)}, u32[]{:S(2)}) %collective-permute-start.2) | collective-permute-done | bytes 65568 | tf_op jit(solution)/shard_map/ppermute | solution.py:473
  41.4 0.0 collective-permute-done.3.cross_ref
  41.4 0.8 %load.1 = bf16[32,40,128]{2,1,0:T(8,128)(2,1)} custom-call(bf16[32,32,128]{2,1,0:T(8,128)(2,1)S(1)} %pair.1.pair_ref, f32[256,128]{1,0:T(8,128)S(1)} %get-tuple-element.21.keep_ref, bf16[256,128]{1,0:T(8,128)(2,1)S(1)} %collective-permute-done.1.side_ref, bf16[256,128]{1,0:T(8,128)(2,1)S(1)} %collective-permute-done.2.next_ref, ...), custom_call_target="tpu_custom_call" | custom-call | flops 131072 | bytes 524288 | tf_op jit(solution)/shard_map/load/pallas_call | solution.py:485
  42.2 0.0 copy-start.8
  42.2 14.2 %all-to-all-start.1 = ((bf16[32,40,128]{2,1,0:T(8,128)(2,1)}), bf16[32,40,128]{2,1,0:T(8,128)(2,1)S(1)}, u32[]{:S(2)}, u32[]{:S(2)}) async-start(bf16[32,40,128]{2,1,0:T(8,128)(2,1)} %load.1), calls=%async_computation.1 | async-start | bytes 655360 | tf_op jit(solution)/shard_map/all_to_all | solution.py:416
  56.5 2.2 %collective-permute-start.4 = (bf16[256,128]{1,0:T(8,128)(2,1)S(1)}, bf16[256,128]{1,0:T(8,128)(2,1)S(1)}, u32[]{:S(2)}, u32[]{:S(2)}) collective-permute-start(bf16[256,128]{1,0:T(8,128)(2,1)S(1)} %slice_bitcast_fusion), channel_id=1, source_target_pairs={{0,128},{8,136},{16,144},{24,152},{32,160},{40,168},{48,176},{56,1... | collective-permute-start | bytes 196616 | tf_op jit(solution)/shard_map/ppermute | solution.py:508
  58.7 1.3 %pair_taps.1 = (bf16[64,128]{1,0:T(8,128)(2,1)S(1)}, f32[256,1024]{1,0:T(8,128)S(1)}, f32[256,1024]{1,0:T(8,128)S(1)}) custom-call(s32[3,16]{1,0:T(4,128)S(1)} %get-tuple-element.19.table_ref, bf16[32,40,128]{2,1,0:T(8,128)(2,1)S(1)} %all-to-all-done.got_ref, bf16[128,1024]{1,0:T(8,128)(2,1)S(1)} %copy-done.4, bf16[128,1024]{1,0:T(8,128)(2,1)S(1)} %copy-done, ...), custom_call_target="tpu_custom_call" | custom-call | flops 1000000000 | bytes 786432 | tf_op jit(solution)/shard_map/pair_taps/pallas_call | solution.py:498
  59.9 3.4 %collective-permute-done.4 = bf16[256,128]{1,0:T(8,128)(2,1)S(1)} collective-permute-done((bf16[256,128]{1,0:T(8,128)(2,1)S(1)}, bf16[256,128]{1,0:T(8,128)(2,1)S(1)}, u32[]{:S(2)}, u32[]{:S(2)}) %collective-permute-start.4) | collective-permute-done | bytes 65568 | tf_op jit(solution)/shard_map/ppermute | solution.py:508
  63.4 4.9 %collective-permute-start.5 = (bf16[576,128]{1,0:T(8,128)(2,1)S(1)}, bf16[576,128]{1,0:T(8,128)(2,1)S(1)}, u32[]{:S(2)}, u32[]{:S(2)}) collective-permute-start(bf16[576,128]{1,0:T(8,128)(2,1)S(1)} %pad_maximum_fusion.own_ref), channel_id=1, source_target_pairs={{0,256},{256,0},{1,257},{257,1},{2,258},{258,2},{3,259},{259,3},{4... | collective-permute-start | bytes 442376 | tf_op jit(solution)/shard_map/ppermute | solution.py:509
  68.2 1.0 %collective-permute-done.5.core_ref = bf16[576,128]{1,0:T(8,128)(2,1)S(1)} collective-permute-done((bf16[576,128]{1,0:T(8,128)(2,1)S(1)}, bf16[576,128]{1,0:T(8,128)(2,1)S(1)}, u32[]{:S(2)}, u32[]{:S(2)}) %collective-permute-start.5) | collective-permute-done | bytes 147488 | tf_op jit(solution)/shard_map/ppermute | solution.py:509
  69.2 1.3 %local.1 = (f32[128,1024]{1,0:T(8,128)S(1)}, f32[128,1024]{1,0:T(8,128)S(1)}) custom-call(bf16[576,128]{1,0:T(8,128)(2,1)S(1)} %pad_maximum_fusion.own_ref, bf16[576,128]{1,0:T(8,128)(2,1)S(1)} %collective-permute-done.5.core_ref, f32[256,1024]{1,0:T(8,128)S(1)} %get-tuple-element.26.xs_ref, f32[256,1024]{1,0:T(8,128)S(1)} %get-tuple-element.27.gs_ref, ...), custom_call_target="tpu_custom_call" | custom-call | flops 3000000000 | bytes 2621440 | tf_op jit(solution)/shard_map/local/pallas_call | solution.py:510
  70.5 0.9 %all-to-all-done.1.got_ref = bf16[32,40,128]{2,1,0:T(8,128)(2,1)S(1)} async-done(((bf16[32,40,128]{2,1,0:T(8,128)(2,1)}), bf16[32,40,128]{2,1,0:T(8,128)(2,1)S(1)}, u32[]{:S(2)}, u32[]{:S(2)}) %all-to-all-start.1) | async-done | bytes 327712 | tf_op jit(solution)/shard_map/all_to_all | solution.py:416
  71.4 1.7 %finish.1 = (bf16[128,1024]{1,0:T(8,128)(2,1)}, bf16[128,1024]{1,0:T(8,128)(2,1)}, bf16[128,1024]{1,0:T(8,128)(2,1)}, bf16[32,256]{1,0:T(8,128)(2,1)}) custom-call(s32[3,16]{1,0:T(4,128)S(1)} %get-tuple-element.19.table_ref, bf16[32,40,128]{2,1,0:T(8,128)(2,1)S(1)} %all-to-all-done.1.got_ref, f32[128,1024]{1,0:T(8,128)S(1)} %get-tuple-element.28.mixed_ref, ...), custom_call_target="tpu_custom_call" | custom-call | flops 1310720 | bytes 2621440 | tf_op jit(solution)/shard_map/finish/pallas_call | solution.py:521
  (5 shorter events, 0.0 us)
Async XLA Ops:
  0.6 22.5 %copy-start.2 = (bf16[128,1024]{1,0:T(8,128)(2,1)S(1)}, bf16[128,1024]{1,0:T(8,128)(2,1)}, u32[]{:S(2)}) copy-start(bf16[128,1024]{1,0:T(8,128)(2,1)} %c_ref.5) | copy-start | bytes 786436
  0.6 22.5 %copy-start.4 = (bf16[128,1024]{1,0:T(8,128)(2,1)S(1)}, bf16[128,1024]{1,0:T(8,128)(2,1)}, u32[]{:S(2)}) copy-start(bf16[128,1024]{1,0:T(8,128)(2,1)} %q_ref.3) | copy-start | bytes 786436
  0.7 22.5 %copy-start.10 = (bf16[256,256]{1,0:T(8,128)(2,1)S(1)}, bf16[256,256]{1,0:T(8,128)(2,1)}, u32[]{:S(2)}) copy-start(bf16[256,256]{1,0:T(8,128)(2,1)} %constant.14.clone.inv) | copy-start | bytes 393220
  2.9 20.2 %copy-start = (bf16[128,1024]{1,0:T(8,128)(2,1)S(1)}, bf16[128,1024]{1,0:T(8,128)(2,1)}, u32[]{:S(2)}) copy-start(bf16[128,1024]{1,0:T(8,128)(2,1)} %k_ref.5) | copy-start | bytes 786436
  2.9 20.2 %copy-start.1 = (bf16[128,1024]{1,0:T(8,128)(2,1)S(1)}, bf16[128,1024]{1,0:T(8,128)(2,1)}, u32[]{:S(2)}) copy-start(bf16[128,1024]{1,0:T(8,128)(2,1)} %v_ref.5) | copy-start | bytes 786436
  3.0 20.2 %copy-start.9 = (bf16[256,256]{1,0:T(8,128)(2,1)S(1)}, bf16[256,256]{1,0:T(8,128)(2,1)}, u32[]{:S(2)}) copy-start(bf16[256,256]{1,0:T(8,128)(2,1)} %constant.12.clone.fwd.own_fwd) | copy-start | bytes 393220
  3.0 36.4 %all-to-all-start = ((bf16[32,40,128]{2,1,0:T(8,128)(2,1)}), bf16[32,40,128]{2,1,0:T(8,128)(2,1)S(1)}, u32[]{:S(2)}, u32[]{:S(2)}) async-start(bf16[32,40,128]{2,1,0:T(8,128)(2,1)} %send.1), calls=%async_computation | async-start | bytes 655360 | tf_op jit(solution)/shard_map/all_to_all | solution.py:416
  23.2 4.4 %copy-start.3 = (bf16[512,256]{1,0:T(8,128)(2,1)S(1)}, bf16[512,256]{1,0:T(8,128)(2,1)}, u32[]{:S(2)}) copy-start(bf16[512,256]{1,0:T(8,128)(2,1)} %constant.16.clone.tap) | copy-start | bytes 786436
  23.2 4.4 %copy-start.5 = (bf16[256,32]{0,1:T(8,128)(2,1)S(1)}, bf16[256,32]{0,1:T(8,128)(2,1)}, u32[]{:S(2)}) copy-start(bf16[256,32]{0,1:T(8,128)(2,1)} %param.17) | copy-start | bytes 49156
  23.2 4.4 %copy-start.6 = (s32[1,32]{1,0:T(1,128)S(1)}, s32[1,32]{1,0:T(1,128)}, u32[]{:S(2)}) copy-start(s32[1,32]{1,0:T(1,128)} %slot_hbm.1) | copy-start | bytes 388
  23.2 4.4 %copy-start.7 = (s32[1,24]{1,0:T(1,128)S(1)}, s32[1,24]{1,0:T(1,128)}, u32[]{:S(2)}) copy-start(s32[1,24]{1,0:T(1,128)} %len_hbm.1) | copy-start | bytes 292
  24.4 4.6 %collective-permute-start = (bf16[4,256,128]{2,1,0:T(8,128)(2,1)S(1)}, bf16[4,256,128]{2,1,0:T(8,128)(2,1)S(1)}, u32[]{:S(2)}, u32[]{:S(2)}) collective-permute-start(bf16[4,256,128]{2,1,0:T(8,128)(2,1)S(1)} %partial_taps.1.after_ref.own_ref), channel_id=1, source_target_pairs={{0,256},{256,0},{1,257},{257,1},{2,258},{258,2},{3,259},{259,3},{4... | collective-permute-start | bytes 786440 | tf_op jit(solution)/shard_map/ppermute | solution.py:448
  29.0 10.4 %copy-start.11 = (bf16[256,256]{1,0:T(8,128)(2,1)S(1)}, bf16[256,256]{1,0:T(8,128)(2,1)}, u32[]{:S(2)}) copy-start(bf16[256,256]{1,0:T(8,128)(2,1)} %constant.13.clone.fwd) | copy-start | bytes 393220
  29.0 10.4 %copy-start.12 = (bf16[256,256]{1,0:T(8,128)(2,1)S(1)}, bf16[256,256]{1,0:T(8,128)(2,1)}, u32[]{:S(2)}) copy-start(bf16[256,256]{1,0:T(8,128)(2,1)} %constant.15.clone.inv) | copy-start | bytes 393220
  29.1 11.3 %collective-permute-start.1 = (bf16[256,128]{1,0:T(8,128)(2,1)S(1)}, bf16[256,128]{1,0:T(8,128)(2,1)S(1)}, u32[]{:S(2)}, u32[]{:S(2)}) collective-permute-start(bf16[256,128]{1,0:T(8,128)(2,1)S(1)} %get-tuple-element.22), channel_id=1, source_target_pairs={{0,136},{8,128},{16,152},{24,144},{32,168},{40,160},{48,184},{56,1... | collective-permute-start | bytes 196616 | tf_op jit(solution)/shard_map/ppermute | solution.py:474
  32.2 9.3 %collective-permute-start.2 = (bf16[256,128]{1,0:T(8,128)(2,1)S(1)}, bf16[256,128]{1,0:T(8,128)(2,1)S(1)}, u32[]{:S(2)}, u32[]{:S(2)}) collective-permute-start(bf16[256,128]{1,0:T(8,128)(2,1)S(1)} %get-tuple-element.23), channel_id=1, source_target_pairs={{0,8},{8,0},{16,24},{24,16},{32,40},{40,32},{48,56},{56,48},{64,72... | collective-permute-start | bytes 196616 | tf_op jit(solution)/shard_map/ppermute | solution.py:473
  34.4 7.1 %collective-permute-start.3 = (bf16[256,128]{1,0:T(8,128)(2,1)S(1)}, bf16[256,128]{1,0:T(8,128)(2,1)S(1)}, u32[]{:S(2)}, u32[]{:S(2)}) collective-permute-start(bf16[256,128]{1,0:T(8,128)(2,1)S(1)} %get-tuple-element.24), channel_id=1, source_target_pairs={{0,128},{8,136},{16,144},{24,152},{32,160},{40,168},{48,176},{56,1... | collective-permute-start | bytes 196616 | tf_op jit(solution)/shard_map/ppermute | solution.py:472
  42.2 16.4 %copy-start.8 = (bf16[256,512]{1,0:T(8,128)(2,1)S(1)}, bf16[256,512]{1,0:T(8,128)(2,1)}, u32[]{:S(2)}) copy-start(bf16[256,512]{1,0:T(8,128)(2,1)} %constant.17.clone.lag) | copy-start | bytes 786436
  42.2 29.2 %all-to-all-start.1 = ((bf16[32,40,128]{2,1,0:T(8,128)(2,1)}), bf16[32,40,128]{2,1,0:T(8,128)(2,1)S(1)}, u32[]{:S(2)}, u32[]{:S(2)}) async-start(bf16[32,40,128]{2,1,0:T(8,128)(2,1)} %load.1), calls=%async_computation.1 | async-start | bytes 655360 | tf_op jit(solution)/shard_map/all_to_all | solution.py:416
  56.5 6.9 %collective-permute-start.4 = (bf16[256,128]{1,0:T(8,128)(2,1)S(1)}, bf16[256,128]{1,0:T(8,128)(2,1)S(1)}, u32[]{:S(2)}, u32[]{:S(2)}) collective-permute-start(bf16[256,128]{1,0:T(8,128)(2,1)S(1)} %slice_bitcast_fusion), channel_id=1, source_target_pairs={{0,128},{8,136},{16,144},{24,152},{32,160},{40,168},{48,176},{56,1... | collective-permute-start | bytes 196616 | tf_op jit(solution)/shard_map/ppermute | solution.py:508
  63.4 5.9 %collective-permute-start.5 = (bf16[576,128]{1,0:T(8,128)(2,1)S(1)}, bf16[576,128]{1,0:T(8,128)(2,1)S(1)}, u32[]{:S(2)}, u32[]{:S(2)}) collective-permute-start(bf16[576,128]{1,0:T(8,128)(2,1)S(1)} %pad_maximum_fusion.own_ref), channel_id=1, source_target_pairs={{0,256},{256,0},{1,257},{257,1},{2,258},{258,2},{3,259},{259,3},{4... | collective-permute-start | bytes 442376 | tf_op jit(solution)/shard_map/ppermute | solution.py:509
